TPU v7x, 128 devices: a whole 4x4x4 slice. The times are simulated.
128 devices in a mesh: dp: 8 (over y_hi, x), grid: 16 (over z, y_lo, core).
Axes of the slice: x: 4, y: 4 (y_hi: 2, y_lo: 2; y = y_hi * 2 + y_lo), z: 4, core: 2. Of those that a mesh axis runs over, the one named last changes fastest.
Arguments:
- inputs: bfloat16 [8192, 5120], P('dp'), may hold values from -6 to 6
- queries: bfloat16 [8192, 12288], P('dp', 'grid'), may hold values from -300 to 300
- key_rows: bfloat16 [8192, 1024], P('dp'), may hold values from -5 to 5
- values: bfloat16 [8192, 1024], P('dp'), may hold values from -6 to 6
- attn_out: bfloat16 [8192, 12288], P('dp', 'grid'), may hold values from -6 to 6
- grad_out: bfloat16 [8192, 12288], P('dp', 'grid'), may hold values from -6 to 6
- momentum: float32 [5120, 12288], P('dp', 'grid'), may hold values from -6 to 6
- iterate: bfloat16 [5120, 12288], P('dp', 'grid'), may hold values from -1 to 1
Outputs:
- momentum_next: float32 [5120, 12288], P('dp', 'grid')
- update: bfloat16 [5120, 12288], P('dp', 'grid')
All inputs are finite; a program needn't handle non-finite values.
Results may differ from a plain program's by a relative error of at most 0.027.
Values may be sent and summed in bfloat16 or wider, within the bound.
No kernel may reach another device: no remote copies, remote signals or barrier semaphores. Data moves between devices by JAX's collectives and lax.ppermute only.
A program may use at most 192 MiB of HBM per device.

v0:
```python
import math

import jax
import jax.numpy as jnp
from jax import lax
from jax.sharding import PartitionSpec as P

HEADS = 96
KV_HEADS = 8
HEAD_DIM = 128
SEQ_LEN = 1024
QD = 12288


linear_coef = 3.4445
cubic_coef = -4.775
quintic_coef = 2.0315


def per_device(inputs, queries, key_rows, values, attn_out, grad_out, momentum, iterate):
    heads_dev = queries.shape[1] // HEAD_DIM
    group_size = HEADS // KV_HEADS
    score_scale = 1.0 / math.sqrt(HEAD_DIM)
    kv_index = lax.axis_index("grid") * heads_dev // group_size
    key_dev = lax.dynamic_slice_in_dim(key_rows, kv_index * HEAD_DIM, HEAD_DIM, 1)
    value_dev = lax.dynamic_slice_in_dim(values, kv_index * HEAD_DIM, HEAD_DIM, 1)
    block_rows = min(512, SEQ_LEN)
    key_pos = jnp.arange(SEQ_LEN, dtype=jnp.int32)
    pieces = []
    for block_index in range(SEQ_LEN // block_rows):
        row_start = block_index * block_rows
        query_block = queries[row_start : row_start + block_rows].reshape(
            block_rows, heads_dev, HEAD_DIM
        )
        dout_block = grad_out[row_start : row_start + block_rows].reshape(
            block_rows, heads_dev, HEAD_DIM
        )
        out_block = attn_out[row_start : row_start + block_rows].reshape(
            block_rows, heads_dev, HEAD_DIM
        )
        query_pos = block_index * block_rows + jnp.arange(block_rows, dtype=jnp.int32)
        causal = key_pos[None, :] <= query_pos[:, None]
        scores = (
            jnp.einsum("qhd,kd->hqk", query_block, key_dev, preferred_element_type=jnp.float32)
            * score_scale
        )
        scores = jnp.where(causal[None], scores, -jnp.inf)
        row_max = jnp.max(scores, axis=-1, keepdims=True)
        probs = jnp.exp(scores - row_max)
        probs = probs / jnp.sum(probs, axis=-1, keepdims=True)
        grad_prob = jnp.einsum(
            "qhd,kd->hqk", dout_block, value_dev, preferred_element_type=jnp.float32
        )
        row_delta = jnp.sum(dout_block.astype(jnp.float32) * out_block.astype(jnp.float32), axis=-1)
        grad_score = (probs * (grad_prob - row_delta.T[:, :, None]) * score_scale).astype(
            jnp.bfloat16
        )
        piece_grad = jnp.einsum(
            "hqk,kd->qhd", grad_score, key_dev, preferred_element_type=jnp.float32
        )
        pieces.append(piece_grad.astype(jnp.bfloat16).reshape(block_rows, heads_dev * HEAD_DIM))
    grad_query = jnp.concatenate(pieces, axis=0)
    gradient = lax.psum_scatter(
        lax.dot_general(
            inputs, grad_query, (((0,), (0,)), ((), ())), preferred_element_type=jnp.float32
        ).astype(jnp.bfloat16),
        "dp",
        scatter_dimension=0,
        tiled=True,
    ).astype(jnp.float32)
    momentum_next = 0.95 * momentum + gradient
    iterate_all = lax.all_gather(iterate, "dp", axis=0, tiled=True)
    partial_gram = lax.dot_general(
        iterate_all, iterate, (((1,), (1,)), ((), ())), preferred_element_type=jnp.float32
    )
    gram_cols = lax.psum(partial_gram.astype(jnp.bfloat16), "grid")
    first = lax.dot_general(
        gram_cols, iterate_all, (((0,), (0,)), ((), ())), preferred_element_type=jnp.float32
    ).astype(jnp.bfloat16)
    second = lax.dot_general(
        gram_cols,
        lax.all_gather(first, "dp", axis=0, tiled=True),
        (((0,), (0,)), ((), ())),
        preferred_element_type=jnp.float32,
    )
    combined = (
        linear_coef * iterate.astype(jnp.float32)
        + cubic_coef * first.astype(jnp.float32)
        + quintic_coef * second
    )
    update = (math.sqrt(QD) * combined).astype(jnp.bfloat16)
    return (momentum_next, update)


def solution(mesh):
    placed = (
        P("dp", None),
        P("dp", "grid"),
        P("dp", None),
        P("dp", None),
        P("dp", "grid"),
        P("dp", "grid"),
        P("dp", "grid"),
        P("dp", "grid"),
    )
    return jax.shard_map(
        per_device,
        mesh=mesh,
        in_specs=placed,
        out_specs=(P("dp", "grid"), P("dp", "grid")),
        check_vma=False,
    )
```

profile of v0, /device:TPU:1, one launch (start us, length us, event | category | flops | bytes accessed | tf_op | source)
XLA Modules:
  0.0 522.9 jit_solution(13333253652645036162)
XLA Ops:
  8.0 109.3 %all-gather.3.cloned.1.call-done = bf16[5120,768]{1,0:T(8,128)(2,1)} async-done(((bf16[640,768]{1,0:T(8,128)(2,1)}), bf16[5120,768]{1,0:T(8,128)(2,1)}) %all-gather.3.cloned.1.call-update) | async-done | bytes 7864336 | tf_op jit(solution)/shard_map/all_gather | solution.py:72
  117.2 10.6 %convolution_convert_fusion.1 = bf16[5120,640]{1,0:T(8,128)(2,1)} fusion(bf16[5120,768]{1,0:T(8,128)(2,1)} %all-gather.3.cloned.1.call-done, bf16[640,768]{1,0:T(8,128)(2,1)} %param.15), kind=kOutput, calls=%fused_computation.19 | convolution fusion | flops 5036441600 | bytes 15400960 | tf_op jit(solution)/shard_map/dot_general | solution.py:73
  127.9 2.6 fusion.67
  131.9 2.6 fusion.65
  134.6 2.4 copy.63
  136.9 2.6 fusion.66
  139.6 2.3 copy.61
  141.9 2.3 copy.59
  144.2 2.3 copy.60
  146.5 2.3 copy.58
  153.2 7.4 %fusion.34 = f32[1024,512,6]{1,0,2:T(8,128)} fusion(bf16[512,6,128]{0,2,1:T(8,128)(2,1)S(1)} %bitcast.103, bf16[1024,1024]{1,0:T(8,128)(2,1)} %param.11, s32[]{:T(128)S(6)} %select_n.17), kind=kOutput, calls=%fused_computation.43 | convolution fusion | flops 805306368 | bytes 13631492 | tf_op jit(solution)/shard_map/qhd,kd->hqk/dot_general | solution.py:51
  160.6 6.3 %fusion.39 = f32[1024,512,6]{1,0,2:T(8,128)} fusion(bf16[512,6,128]{0,2,1:T(8,128)(2,1)S(1)} %bitcast.106, bf16[1024,1024]{1,0:T(8,128)(2,1)S(1)} %copy-done, s32[]{:T(128)S(6)} %select_n.17), kind=kOutput, calls=%fused_computation.48 | convolution fusion | flops 805306368 | bytes 13631492 | tf_op jit(solution)/shard_map/qhd,kd->hqk/dot_general | solution.py:44
  166.8 17.3 %fusion.28 = bf16[128,6,512]{2,0,1:T(8,128)(2,1)} fusion(f32[1024,512,6]{1,0,2:T(8,128)} %fusion.34, f32[6,512]{1,0:T(8,128)S(1)} %bitcast.111, bf16[1024,1024]{1,0:T(8,128)(2,1)S(1)} %copy-done, s32[]{:T(128)S(6)} %select_n.17, f32[1024,512,6]{1,0,2:T(8,128)} %fusion.39, pred[512,1024]{0,1:T(8,128)(4,1)} %iota_compare_fusion), kind=kOutput, calls=%fused_computation.41 | convolution fusion | flops 837165056 | bytes 39862276 | tf_op jit(solution)/shard_map/hqk,kd->qhd/dot_general | solution.py:58
  184.1 7.4 %fusion.36 = f32[1024,512,6]{1,0,2:T(8,128)} fusion(bf16[512,6,128]{0,2,1:T(8,128)(2,1)S(1)} %bitcast.105, bf16[1024,1024]{1,0:T(8,128)(2,1)} %param.11, s32[]{:T(128)S(6)} %select_n.17), kind=kOutput, calls=%fused_computation.45 | convolution fusion | flops 805306368 | bytes 13631492 | tf_op jit(solution)/shard_map/qhd,kd->hqk/dot_general | solution.py:51
  191.5 6.2 %fusion.41 = f32[1024,512,6]{1,0,2:T(8,128)} fusion(bf16[512,6,128]{0,2,1:T(8,128)(2,1)S(1)} %bitcast.107, bf16[1024,1024]{1,0:T(8,128)(2,1)S(1)} %copy-done, s32[]{:T(128)S(6)} %select_n.17), kind=kOutput, calls=%fused_computation.50 | convolution fusion | flops 805306368 | bytes 13631492 | tf_op jit(solution)/shard_map/qhd,kd->hqk/dot_general | solution.py:44
  197.7 16.7 %fusion.31 = bf16[128,6,512]{2,0,1:T(8,128)(2,1)} fusion(f32[1024,512,6]{1,0,2:T(8,128)} %fusion.36, f32[6,512]{1,0:T(8,128)S(1)} %bitcast.110, bf16[1024,1024]{1,0:T(8,128)(2,1)S(1)} %copy-done, s32[]{:T(128)S(6)} %select_n.17, f32[1024,512,6]{1,0,2:T(8,128)} %fusion.41, pred[512,1024]{0,1:T(8,128)(4,1)S(1)} %iota_compare_fusion.1), kind=kOutput, calls=%fused_computation.42 | convolution fusion | flops 837165056 | bytes 39862276 | tf_op jit(solution)/shard_map/hqk,kd->qhd/dot_general | solution.py:58
  214.5 13.5 %fusion.12 = bf16[5120,768]{0,1:T(8,128)(2,1)} fusion(bf16[1024,5120]{1,0:T(8,128)(2,1)} %param.8, bf16[512,768]{0,1:T(8,128)(2,1)S(1)} %bitcast.112, bf16[512,768]{0,1:T(8,128)(2,1)} %bitcast.113), kind=kOutput, calls=%fused_computation.20 | convolution fusion | flops 8060141568 | bytes 19922944 | tf_op jit(solution)/shard_map/dot_general | solution.py:64
  227.9 10.7 %copy.56 = bf16[5120,768]{1,0:T(8,128)(2,1)} copy(bf16[5120,768]{0,1:T(8,128)(2,1)} %fusion.12) | data formatting | bytes 15728640
  238.7 44.0 %all-reduce.2.cloned.1.call-done = bf16[5120,640]{1,0:T(8,128)(2,1)} async-done(((bf16[5120,640]{1,0:T(8,128)(2,1)}), bf16[5120,640]{1,0:T(8,128)(2,1)}) %all-reduce.2.cloned.1.call-update) | async-done | bytes 6553616 | tf_op jit(solution)/shard_map/psum | solution.py:76
  282.7 11.4 %convolution_convert_fusion.2 = bf16[640,768]{1,0:T(8,128)(2,1)} fusion(bf16[5120,640]{1,0:T(8,128)(2,1)} %all-reduce.2.cloned.1.call-done, bf16[5120,768]{1,0:T(8,128)(2,1)} %all-gather.3.cloned.1.call-done), kind=kOutput, calls=%fused_computation.40 | convolution fusion | flops 5033656320 | bytes 15400960 | tf_op jit(solution)/shard_map/dot_general | solution.py:77
  296.3 103.0 %reduce-scatter.4.cloned.1.call-done = bf16[640,768]{1,0:T(8,128)(2,1)} async-done(((bf16[5120,768]{1,0:T(8,128)(2,1)}), bf16[640,768]{1,0:T(8,128)(2,1)}) %reduce-scatter.4.cloned.1.call-update) | async-done | bytes 983056
  402.4 3.0 copy.45
  405.4 98.8 %all-gather.5.cloned.1.call-done = bf16[5120,768]{1,0:T(8,128)(2,1)} async-done(((bf16[640,768]{1,0:T(8,128)(2,1)}), bf16[5120,768]{1,0:T(8,128)(2,1)}) %all-gather.5.cloned.1.call-update) | async-done | bytes 7864336 | tf_op jit(solution)/shard_map/all_gather | solution.py:82
  504.2 12.1 %multiply_convert_fusion = bf16[640,768]{1,0:T(8,128)(2,1)} fusion(bf16[640,768]{1,0:T(8,128)(2,1)} %convolution_convert_fusion.2, bf16[640,768]{1,0:T(8,128)(2,1)} %param.15, bf16[5120,640]{1,0:T(8,128)(2,1)} %all-reduce.2.cloned.1.call-done, bf16[5120,768]{1,0:T(8,128)(2,1)} %all-gather.5.cloned.1.call-done), kind=kOutput, calls=%fused_computation.31 | convolution fusion | flops 5037588480 | bytes 17367040 | tf_op jit(solution)/shard_map/dot_general | solution.py:80
  (29 shorter events, 11.9 us)
Async XLA Ops:
  7.2 153.4 %copy-start = (bf16[1024,1024]{1,0:T(8,128)(2,1)S(1)}, bf16[1024,1024]{1,0:T(8,128)(2,1)}, u32[]{:S(2)}) copy-start(bf16[1024,1024]{1,0:T(8,128)(2,1)} %param.10) | copy-start | bytes 6291460
  7.2 110.0 %all-gather.3.cloned.1.call-start = ((), (), s32[]{:S(2)}) async-start(), calls=%async_computation.1 | async-start | bytes 8847360 | tf_op jit(solution)/shard_map/all_gather | solution.py:72
  7.9 274.8 %all-reduce.2.cloned.1.call-start = ((), (), s32[]{:S(2)}) async-start(), calls=%async_computation.2 | async-start | bytes 13107200 | tf_op jit(solution)/shard_map/psum | solution.py:76
  127.8 271.5 %reduce-scatter.4.cloned.1.call-start = ((), (), s32[]{:S(2)}) async-start(), calls=%async_computation.4 | async-start | bytes 8847360
  153.2 7.4 %copy-start.3 = (bf16[512,768]{0,1:T(8,128)(2,1)S(1)}, bf16[512,768]{0,1:T(8,128)(2,1)}, u32[]{:S(2)}) copy-start(bf16[512,768]{0,1:T(8,128)(2,1)} %copy.61) | copy-start | bytes 2359300
  166.8 17.3 %copy-start.2 = (bf16[512,768]{0,1:T(8,128)(2,1)S(1)}, bf16[512,768]{0,1:T(8,128)(2,1)}, u32[]{:S(2)}) copy-start(bf16[512,768]{0,1:T(8,128)(2,1)} %copy.59) | copy-start | bytes 2359300
  184.1 7.4 %copy-start.4 = (bf16[512,768]{0,1:T(8,128)(2,1)S(1)}, bf16[512,768]{0,1:T(8,128)(2,1)}, u32[]{:S(2)}) copy-start(bf16[512,768]{0,1:T(8,128)(2,1)} %copy.58) | copy-start | bytes 2359300
  197.7 16.7 %copy-start.5 = (bf16[128,6,512]{2,0,1:T(8,128)(2,1)S(1)}, bf16[128,6,512]{2,0,1:T(8,128)(2,1)}, u32[]{:S(2)}) copy-start(bf16[128,6,512]{2,0,1:T(8,128)(2,1)} %fusion.28) | copy-start | bytes 2359300
  238.6 265.6 %all-gather.5.cloned.1.call-start = ((), (), s32[]{:S(2)}) async-start(), calls=%async_computation.3 | async-start | bytes 8847360 | tf_op jit(solution)/shard_map/all_gather | solution.py:82
  402.4 113.9 %copy-start.1 = (bf16[1024,1024]{1,0:T(8,128)(2,1)S(1)}, bf16[1024,1024]{1,0:T(8,128)(2,1)}, u32[]{:S(2)}) copy-start(bf16[1024,1024]{1,0:T(8,128)(2,1)} %param.10) | copy-start | bytes 6291460
Sparse Core Ops, SparseCore 0:
  10.3 106.8 all-gather.2
  127.9 154.7 all-reduce.1
  287.2 112.0 reduce-scatter.3
  402.0 102.1 all-gather.4
where the time goes:
time: 524 us; the launch traced here: 523 us
  waiting for transfers between devices  356 us (68%)
  matrix products  109 us (21%)
  local copies, waits for them, and re-layouts  38.3 us (7%)
  between operations  13.9 us (3%)
  other arithmetic  5.89 us (1%)
    all_gather x1, waiting for transfers between devices, per_device(): iterate_all = lax.all_gather(iterate, 'dp', axis=0, tiled=True)  109 us
    unnamed x5, waiting for transfers between devices  104 us
    all_gather x1, waiting for transfers between devices, per_device(): lax.all_gather(first, 'dp', axis=0, tiled=True)  98.8 us
    psum x1, waiting for transfers between devices, per_device(): gram_cols = lax.psum(partial_gram.astype(jnp.bfloat16), 'grid')  44 us
    dot_general x2, matrix products, per_device(): jnp.einsum('hqk,kd->qhd', grad_score, key_dev, preferred_element_type=jnp...  34 us
    unnamed x22, local copies, waits for them, and re-layouts  30.4 us
    dot_general x2, matrix products, per_device(): jnp.einsum('qhd,kd->hqk', dout_block, value_dev, preferred_element_type=j...  14.8 us
    dot_general x1, matrix products, per_device(): lax.dot_general(inputs, grad_query, (((0,), (0,)), ((), ())), preferred_e...  13.5 us
  transfers between devices with their start and end apart: 4, of which 4 were waited for; matrix products, arithmetic and copies ran while one was open for 25% of the time, Pallas kernels for 0%

commit v1 on v0

v1 whole, which is shorter than its diff:
```python
import math

import jax
import jax.numpy as jnp
import numpy as np
from jax import lax
from jax.experimental import pallas as pl
from jax.experimental.pallas import tpu as pltpu
from jax.sharding import PartitionSpec as P

HEADS = 96
KV_HEADS = 8
HEAD_DIM = 128
SEQ_LEN = 1024
QD = 12288
D = 5120
ROWS = 640
COLS = 768
HALF = 320
QUART = 160
SHAPE = (2, 4, 4, 2, 2)

linear_coef = 3.4445
cubic_coef = -4.775
quintic_coef = 2.0315

VMEM = 60 * 1024 * 1024


def make_perm(move):
    pairs = []
    for source in range(128):
        place = np.unravel_index(source, SHAPE)
        target = [int(a) % b for a, b in zip(move(*place), SHAPE)]
        pairs.append((source, int(np.ravel_multi_index(target, SHAPE))))
    return pairs


X_UP = make_perm(lambda yh, x, z, yl, c: (yh, x + 1, z, yl, c))
X_DOWN = make_perm(lambda yh, x, z, yl, c: (yh, x - 1, z, yl, c))
Z_UP = make_perm(lambda yh, x, z, yl, c: (yh, x, z + 1, yl, c))
Z_DOWN = make_perm(lambda yh, x, z, yl, c: (yh, x, z - 1, yl, c))
Z_FAR = make_perm(lambda yh, x, z, yl, c: (yh, x, z + 2, yl, c))
X_FAR = make_perm(lambda yh, x, z, yl, c: (yh, x + 2, z, yl, c))
Y_HI = make_perm(lambda yh, x, z, yl, c: (yh + 1, x, z, yl, c))
Y_LO = make_perm(lambda yh, x, z, yl, c: (yh, x, z, yl + 1, c))
CORE = make_perm(lambda yh, x, z, yl, c: (yh, x, z, yl, c + 1))


def move(array, perm):
    return lax.ppermute(array, ("dp", "grid"), perm)


def place():
    dp = lax.axis_index("dp")
    grid = lax.axis_index("grid")
    return dp // 4, dp % 4, grid // 4, (grid // 2) % 2, grid % 2


def cost(flops, bytes_accessed, transcendentals=0):
    return pl.CostEstimate(
        flops=flops, bytes_accessed=bytes_accessed, transcendentals=transcendentals
    )


def dot(a, b, ca, cb):
    return lax.dot_general(a, b, (((ca,), (cb,)), ((), ())), preferred_element_type=jnp.float32)


def attention_kernel(q_ref, k_ref, v_ref, o_ref, do_ref, out_ref):
    block = 256
    scale = 1.0 / math.sqrt(HEAD_DIM)
    rows = lax.broadcasted_iota(jnp.int32, (block, block), 0)
    cols = lax.broadcasted_iota(jnp.int32, (block, block), 1)
    keep = cols <= rows
    for r in range(SEQ_LEN // block):
        start, length = r * block, (r + 1) * block
        q = q_ref[start:length, :]
        do = do_ref[start:length, :]
        o = o_ref[start:length, :]
        delta = jnp.sum(do.astype(jnp.float32) * o.astype(jnp.float32), axis=-1, keepdims=True)
        diag = jnp.where(keep, dot(q, k_ref[start:length, :], 1, 1), -jnp.inf)
        row_max = jnp.max(diag, axis=-1, keepdims=True)
        if r:
            body = dot(q, k_ref[:start, :], 1, 1)
            row_max = jnp.maximum(row_max, jnp.max(body, axis=-1, keepdims=True))
        e = jnp.exp((diag - row_max) * scale)
        total = jnp.sum(e, axis=-1, keepdims=True)
        g = (e * (dot(do, v_ref[start:length, :], 1, 1) - delta)).astype(jnp.bfloat16)
        grad = dot(g, k_ref[start:length, :], 1, 0)
        if r:
            e = jnp.exp((body - row_max) * scale)
            total = total + jnp.sum(e, axis=-1, keepdims=True)
            g = (e * (dot(do, v_ref[:start, :], 1, 1) - delta)).astype(jnp.bfloat16)
            grad = grad + dot(g, k_ref[:start, :], 1, 0)
        grad = grad * (scale / total)
        out_ref[:, start:length] = grad.T.astype(jnp.bfloat16)


def attention(queries, keys, values, attn_out, grad_out, kv_index):
    heads = queries.shape[1] // HEAD_DIM
    mine = pl.BlockSpec((SEQ_LEN, HEAD_DIM), lambda h, kv: (0, h))
    shared = pl.BlockSpec((SEQ_LEN, HEAD_DIM), lambda h, kv: (0, kv[0]))

    def body(kv, *refs):
        attention_kernel(*refs)

    return pl.pallas_call(
        body,
        grid_spec=pltpu.PrefetchScalarGridSpec(
            num_scalar_prefetch=1,
            grid=(heads,),
            in_specs=[mine, shared, shared, mine, mine],
            out_specs=pl.BlockSpec((HEAD_DIM, SEQ_LEN), lambda h, kv: (h, 0)),
        ),
        out_shape=jax.ShapeDtypeStruct((heads * HEAD_DIM, SEQ_LEN), jnp.bfloat16),
        compiler_params=pltpu.CompilerParams(vmem_limit_bytes=VMEM),
        cost_estimate=cost(24 * 10**9, 8 * 10**6, 4 * 10**6),
        name="attention",
    )(kv_index, queries, keys, values, attn_out, grad_out)


def gradient_kernel(gq_ref, in_ref, out_ref):
    out_ref[0] = dot(gq_ref[...], in_ref[...], 1, 0).astype(jnp.bfloat16)


def gradient_partial(grad_query_t, inputs):
    blocks = D // ROWS
    return pl.pallas_call(
        gradient_kernel,
        grid=(blocks,),
        in_specs=[
            pl.BlockSpec((COLS, SEQ_LEN), lambda k: (0, 0)),
            pl.BlockSpec((SEQ_LEN, ROWS), lambda k: (0, k)),
        ],
        out_specs=pl.BlockSpec((1, COLS, ROWS), lambda k: (k, 0, 0)),
        out_shape=jax.ShapeDtypeStruct((blocks, COLS, ROWS), jnp.bfloat16),
        compiler_params=pltpu.CompilerParams(vmem_limit_bytes=VMEM),
        cost_estimate=cost(2 * D * COLS * SEQ_LEN, 20 * 10**6),
        name="gradient",
    )(grad_query_t, inputs)


def gram_kernel(own_ref, b0, b1, b2a, b2b, b3, keep_ref, send_ref):
    _, x, z, _, core = place()
    for ahead, block in enumerate((b0, b1, None, b3)):
        slot = (x + ahead - z + 4) % 4
        for out_ref, half in ((keep_ref, core), (send_ref, 1 - core)):
            if block is None:

                @pl.when(half == 0)
                def _():
                    out_ref[slot] = dot(b2a[...], own_ref[...], 1, 1).astype(jnp.bfloat16)

                @pl.when(half == 1)
                def _():
                    out_ref[slot] = dot(b2b[...], own_ref[...], 1, 1).astype(jnp.bfloat16)

            else:
                rows = block[pl.ds(pl.multiple_of(half * HALF, HALF), HALF), :]
                out_ref[slot] = dot(rows, own_ref[...], 1, 1).astype(jnp.bfloat16)


def gram_partial(own, blocks):
    here, above, far, below = blocks
    out = jax.ShapeDtypeStruct((4, HALF, ROWS), jnp.bfloat16)
    return pl.pallas_call(
        gram_kernel,
        in_specs=[pl.BlockSpec(memory_space=pltpu.VMEM)] * 6,
        out_specs=[pl.BlockSpec(memory_space=pltpu.VMEM)] * 2,
        out_shape=[out, out],
        compiler_params=pltpu.CompilerParams(vmem_limit_bytes=VMEM),
        cost_estimate=cost(8 * ROWS * ROWS * COLS, 9 * 10**6),
        name="gram",
    )(own, here, above, *far, below)


def reduce_gram(keep, send):
    _, _, _, yl, _ = place()
    total = (keep.astype(jnp.float32) + move(send, CORE).astype(jnp.float32)).astype(jnp.bfloat16)
    up = move(total[1], Z_UP)
    down = move(total[3], Z_DOWN)
    far = move(total[2], Z_FAR)
    f32 = jnp.float32
    summed = total[0].astype(f32) + up.astype(f32) + down.astype(f32) + far.astype(f32)
    pair = summed.reshape(2, QUART, ROWS)
    mine = lax.dynamic_index_in_dim(pair, yl, 0, False)
    theirs = lax.dynamic_index_in_dim(pair, 1 - yl, 0, False).astype(jnp.bfloat16)
    return (mine + move(theirs, Y_LO).astype(f32)).astype(jnp.bfloat16)


PIECES = [(0, 0), (0, 1), (3, 0), (1, 0), (2, 0), (3, 1), (1, 1), (2, 1)]


def gather_first(own):
    return move(own, Z_UP), move(own, Z_DOWN), move(own, Y_LO), move(own, Z_FAR)


def gather_second(own, arrived):
    below, above, lo, far = arrived
    lo_below = move(lo, Z_UP)
    lo_above = move(lo, Z_DOWN)
    lo_far = move(far, Y_LO)
    first = jnp.stack([own, lo, below, above, far])
    second = jnp.stack([lo_below, lo_above, lo_far])
    return first, second, move(first, CORE), move(second, CORE)


def copies_of(gathered, target, sems):
    first, second, other_first, other_second = gathered
    _, _, z, yl, core = place()
    out = []
    for flipped, (early, late) in enumerate(((first, second), (other_first, other_second))):
        for n, (ahead, flip) in enumerate(PIECES):
            source = early.at[n] if n < 5 else late.at[n - 5]
            z_piece = (z + ahead) % 4
            yl_piece = (yl + flip) % 2
            core_piece = (core + flipped) % 2
            for yh in range(2):
                row = yh * 4 * ROWS + z_piece * ROWS + core_piece * HALF + yl_piece * QUART
                out.append(
                    pltpu.make_async_copy(
                        source.at[yh],
                        target.at[pl.ds(pl.multiple_of(row, QUART), QUART), :],
                        sems.at[len(out)],
                    )
                )
    return out


def square_kernel(own_ref, g0, g1, g2, g3, *refs):
    pieces = refs[:8]
    out_ref, full, acc, sems = refs[8:]
    yh, x, _, _, _ = place()
    copies = copies_of((g0, g1, g2, g3), full, sems)
    for copy in copies:
        copy.start()
    for copy in copies:
        copy.wait()
    acc[...] = jnp.zeros_like(acc)
    for n, piece in enumerate(pieces):
        block = ((yh + n // 4) % 2) * 4 + (x + n % 4) % 4
        lhs = piece[...].reshape(HALF, ROWS)
        rhs = full[pl.ds(pl.multiple_of(block * ROWS, ROWS), ROWS), :]
        acc[...] += dot(lhs, rhs, 1, 0)
    own = own_ref[...].reshape(HALF, ROWS).astype(jnp.float32)
    out = cubic_coef * own + quintic_coef * acc[...]
    out_ref[...] = out.astype(jnp.bfloat16).reshape(2, QUART, ROWS)


def square(own, gathered, rows):
    anywhere = pl.BlockSpec(memory_space=pl.ANY)
    inside = pl.BlockSpec(memory_space=pltpu.VMEM)
    return pl.pallas_call(
        square_kernel,
        in_specs=[inside] + [anywhere] * 4 + [inside] * 8,
        out_specs=inside,
        out_shape=jax.ShapeDtypeStruct((2, QUART, ROWS), jnp.bfloat16),
        scratch_shapes=[
            pltpu.VMEM((D, ROWS), jnp.bfloat16),
            pltpu.VMEM((HALF, ROWS), jnp.float32),
            pltpu.SemaphoreType.DMA((32,)),
        ],
        compiler_params=pltpu.CompilerParams(vmem_limit_bytes=VMEM),
        cost_estimate=cost(2 * HALF * D * ROWS, 11 * 10**6),
        name="square",
    )(own, *gathered, *rows)


def update_kernel(own_ref, n0, n1, n2, n3, *refs):
    blocks = refs[:10]
    out_ref, full, rhs, acc, sems, block_sems = refs[10:]
    yh, x, _, _, _ = place()
    copies = copies_of((n0, n1, n2, n3), full, sems)
    at = 0
    for flip in range(2):
        for ahead in range(4):
            row = ((yh + flip) % 2) * 4 * ROWS + ((x + ahead) % 4) * ROWS
            pieces = 2 if ahead == 2 else 1
            size = ROWS // pieces
            for piece in range(pieces):
                copies.append(
                    pltpu.make_async_copy(
                        blocks[at],
                        rhs.at[pl.ds(pl.multiple_of(row + piece * size, QUART), size), :],
                        block_sems.at[at],
                    )
                )
                at += 1
    for copy in copies:
        copy.start()
    for copy in copies:
        copy.wait()
    acc[...] = jnp.zeros_like(acc)

    def step(k, carry):
        at_k = pl.ds(pl.multiple_of(k * ROWS, ROWS), ROWS)
        acc[...] += dot(full[at_k, :], rhs[at_k, :], 0, 0)
        return carry

    lax.fori_loop(0, 8, step, 0)
    out = linear_coef * own_ref[...].astype(jnp.float32) + acc[...]
    out_ref[...] = (math.sqrt(QD) * out).astype(jnp.bfloat16)


def update_of(own, gathered, blocks):
    anywhere = pl.BlockSpec(memory_space=pl.ANY)
    inside = pl.BlockSpec(memory_space=pltpu.VMEM)
    return pl.pallas_call(
        update_kernel,
        in_specs=[inside] + [anywhere] * 14,
        out_specs=inside,
        out_shape=jax.ShapeDtypeStruct((ROWS, COLS), jnp.bfloat16),
        scratch_shapes=[
            pltpu.VMEM((D, ROWS), jnp.bfloat16),
            pltpu.VMEM((D, COLS), jnp.bfloat16),
            pltpu.VMEM((ROWS, COLS), jnp.float32),
            pltpu.SemaphoreType.DMA((32,)),
            pltpu.SemaphoreType.DMA((10,)),
        ],
        compiler_params=pltpu.CompilerParams(vmem_limit_bytes=VMEM),
        cost_estimate=cost(2 * D * ROWS * COLS, 15 * 10**6),
        name="update",
    )(own, *gathered, *blocks)


def per_device(inputs, queries, key_rows, values, attn_out, grad_out, momentum, iterate):
    yh = place()[0]
    together = lax.optimization_barrier

    own = iterate
    below = move(own, X_UP)
    above = move(own, X_DOWN)
    across = move(own, Y_HI)
    kv_index = (lax.axis_index("grid") // 2).astype(jnp.int32).reshape(1)
    grad_query_t = attention(queries, key_rows, values, attn_out, grad_out, kv_index)
    below, above, across, grad_query_t = together((below, above, across, grad_query_t))
    far = (move(below[:HALF], X_UP), move(above[HALF:], X_DOWN))
    far, below, above, across = together((far, below, above, across))
    across_below = move(across, X_UP)
    across_above = move(across, X_DOWN)
    across_far = (move(far[0], Y_HI), move(far[1], Y_HI))
    near = reduce_gram(*gram_partial(own, (own, above, far, below)))

    partial = gradient_partial(grad_query_t, inputs)
    gradient_t = lax.psum_scatter(partial, "dp", scatter_dimension=0, tiled=False)
    momentum_next = 0.95 * momentum + gradient_t.astype(jnp.float32).T

    across_below, across_above, across_far, partial = together(
        (across_below, across_above, across_far, partial)
    )
    other = reduce_gram(
        *gram_partial(own, (across, across_above, across_far, across_below))
    )
    rows = jnp.where(yh == 0, jnp.stack([near, other]), jnp.stack([other, near]))

    over_grid = gather_first(rows)
    over_dp = (move(rows, X_UP), move(rows, X_DOWN), move(rows, Y_HI), move(rows, X_FAR))
    over_grid, over_dp = together((over_grid, over_dp))
    over_grid = gather_second(rows, over_grid)
    r_below, r_above, r_across, r_far = over_dp
    over_dp = (
        rows,
        r_above,
        r_far,
        r_below,
        r_across,
        move(r_across, X_DOWN),
        move(r_far, Y_HI),
        move(r_across, X_UP),
    )
    combined = square(rows, over_grid, over_dp)
    over_grid = together(gather_first(combined))
    update = update_of(
        own,
        gather_second(combined, over_grid),
        (own, above, *far, below, across, across_above, *across_far, across_below),
    )
    return (momentum_next, update)


def solution(mesh):
    placed = (
        P("dp", None),
        P("dp", "grid"),
        P("dp", None),
        P("dp", None),
        P("dp", "grid"),
        P("dp", "grid"),
        P("dp", "grid"),
        P("dp", "grid"),
    )
    return jax.shard_map(
        per_device,
        mesh=mesh,
        in_specs=placed,
        out_specs=(P("dp", "grid"), P("dp", "grid")),
        check_vma=False,
    )
```

time: 524 us -> 328 us (0.63)
  waiting for transfers between devices: 356 us -> 127 us
  matrix products: 109 us -> 0 us
  starting transfers between devices: 0.16 us -> 92.1 us
  Pallas kernels: 0 us -> 70.2 us
  local copies, waits for them, and re-layouts: 38.3 us -> 15.4 us
    all_gather x2 -> x0, waiting for transfers between devices: 208 us -> none  [the longest x1 109 us: per_device(): iterate_all = lax.all_gather(iterate, 'dp', axis=0, tiled=True)]
    ppermute x0 -> x44, waiting for transfers between devices: none -> 127 us  [move(): return lax.ppermute(array, ('dp', 'grid'), perm)]
    dot_general x10 -> x0, matrix products: 109 us -> none  [the longest x2 34 us: per_device(): jnp.einsum('hqk,kd->qhd', grad_score, key_dev, preferred_element_type=jnp...]
    unnamed x5 -> x1, waiting for transfers between devices: 104 us -> 0.02 us
    ppermute x0 -> x44, starting transfers between devices: none -> 92.1 us  [move(): return lax.ppermute(array, ('dp', 'grid'), perm)]
    pallas_call x0 -> x6, Pallas kernels: none -> 70.2 us  [the longest x1 16 us: update_of(): pl.pallas_call(update_kernel, in_specs=[inside] + [anywhere] * 14, out_sp...]
    psum x1 -> x0, waiting for transfers between devices: 44 us -> none  [per_device(): gram_cols = lax.psum(partial_gram.astype(jnp.bfloat16), 'grid')]
    unnamed x22 -> x45, local copies, waits for them, and re-layouts: 30.4 us -> 12.3 us
  transfers between devices with their start and end apart: 4 -> 45, of which waited for: 4 -> 27; matrix products, arithmetic and copies ran while one was open for 25% -> 5% of each run, Pallas kernels for 0% -> 17%
where the time goes in v1:
time: 328 us; the launch traced here: 327 us
  waiting for transfers between devices  127 us (39%)
  starting transfers between devices  92.1 us (28%)
  Pallas kernels  70.2 us (21%)
  local copies, waits for them, and re-layouts  15.4 us (5%)
  between operations  14.4 us (4%)
  other arithmetic  8.43 us (3%)
    ppermute x44, waiting for transfers between devices, move(): return lax.ppermute(array, ('dp', 'grid'), perm)  127 us
    ppermute x44, starting transfers between devices, move(): return lax.ppermute(array, ('dp', 'grid'), perm)  92.1 us
    pallas_call x1, Pallas kernels, update_of(): pl.pallas_call(update_kernel, in_specs=[inside] + [anywhere] * 14, out_sp...  16 us
    pallas_call x2, Pallas kernels, gram_partial(): pl.pallas_call(gram_kernel, in_specs=[pl.BlockSpec(memory_space=pltpu.VME...  15.8 us
    pallas_call x1, Pallas kernels, gradient_partial(): pl.pallas_call(gradient_kernel, grid=(blocks,), in_specs=[pl.BlockSpec((C...  15 us
    pallas_call x1, Pallas kernels, attention(): pl.pallas_call(body, grid_spec=pltpu.PrefetchScalarGridSpec(num_scalar_pr...  14.3 us
    unnamed x45, local copies, waits for them, and re-layouts  12.3 us
    pallas_call x1, Pallas kernels, square(): pl.pallas_call(square_kernel, in_specs=[inside] + [anywhere] * 4 + [insid...  9.06 us
  transfers between devices with their start and end apart: 45, of which 27 were waited for; matrix products, arithmetic and copies ran while one was open for 5% of the time, Pallas kernels for 17%

profile of v1, /device:TPU:1, one launch (start us, length us, event | category | flops | bytes accessed | tf_op | source)
XLA Modules:
  0.0 327.4 jit_solution(1617185430299171325)
XLA Ops:
  13.7 14.3 %attention.1.gq_ref = bf16[768,1024]{1,0:T(8,128)(2,1)} custom-call(s32[1]{0:T(128)} %bitcast.kv, bf16[1024,768]{1,0:T(8,128)(2,1)} %refs_0_.2, bf16[1024,1024]{1,0:T(8,128)(2,1)} %refs_1_.1, bf16[1024,1024]{1,0:T(8,128)(2,1)} %refs_2_.1, bf16[1024,768]{1,0:T(8,128)(2,1)} %refs_3_.1, bf16[1024,768]{1,0:T(8,128)(2,1)} %refs_4_.1), custom_call_target="tpu_custom_call" | custom-call | flops 24000000000 | bytes 8000000 | tf_op jit(solution)/shard_map/attention/pallas_call | solution.py:108
  28.0 4.0 %collective-permute-done.b3.refs_4_ = bf16[640,768]{1,0:T(8,128)(2,1)S(1)} collective-permute-done((bf16[640,768]{1,0:T(8,128)(2,1)}, bf16[640,768]{1,0:T(8,128)(2,1)S(1)}, u32[]{:S(2)}, u32[]{:S(2)}) %collective-permute-start) | collective-permute-done | bytes 983072 | tf_op jit(solution)/shard_map/ppermute | solution.py:51
  34.7 15.0 %gradient.1 = bf16[8,768,640]{2,1,0:T(8,128)(2,1)} custom-call(bf16[768,1024]{1,0:T(8,128)(2,1)} %attention.1.gq_ref, bf16[1024,5120]{1,0:T(8,128)(2,1)} %in_ref.1), custom_call_target="tpu_custom_call" | custom-call | flops 8053063680 | bytes 20000000 | tf_op jit(solution)/shard_map/gradient/pallas_call | solution.py:129
  52.6 9.2 %collective-permute-done.3.b2a.refs_2_ = bf16[320,768]{1,0:T(8,128)(2,1)} collective-permute-done((bf16[320,768]{1,0:T(8,128)(2,1)S(1)}, bf16[320,768]{1,0:T(8,128)(2,1)}, u32[]{:S(2)}, u32[]{:S(2)}) %collective-permute-start.3) | collective-permute-done | bytes 491552 | tf_op jit(solution)/shard_map/ppermute | solution.py:51
  67.4 7.9 %gram.2 = (bf16[4,320,640]{2,1,0:T(8,128)(2,1)}, bf16[4,320,640]{2,1,0:T(8,128)(2,1)}) custom-call(bf16[640,768]{1,0:T(8,128)(2,1)} %refs_0_.3, bf16[640,768]{1,0:T(8,128)(2,1)} %refs_0_.3, bf16[640,768]{1,0:T(8,128)(2,1)} %copy-done.16, bf16[320,768]{1,0:T(8,128)(2,1)} %collective-permute-done.3.b2a.refs_2_, bf16[320,768]{1,0:T(8,128)(2,1)} %copy-done.17, ...), custom_call_target="tpu_custom_call" | custom-call | flops 2516582400 | bytes 9000000 | tf_op jit(solution)/shard_map/gram/pallas_call | solution.py:167
  75.3 8.4 %collective-permute-start.5 = (bf16[4,320,640]{2,1,0:T(8,128)(2,1)}, bf16[4,320,640]{2,1,0:T(8,128)(2,1)S(1)}, u32[]{:S(2)}, u32[]{:S(2)}) collective-permute-start(bf16[4,320,640]{2,1,0:T(8,128)(2,1)} %get-tuple-element.40), channel_id=1, source_target_pairs={{0,1},{1,0},{2,3},{3,2},{4,5},{5,4},{6,7},{7,6},{8,9},{9,8},{10,11... | collective-permute-start | bytes 4915208 | tf_op jit(solution)/shard_map/ppermute | solution.py:51
  83.8 13.8 %collective-permute-done.13.b2b.refs_8_ = bf16[320,768]{1,0:T(8,128)(2,1)} collective-permute-done((bf16[320,768]{1,0:T(8,128)(2,1)S(1)}, bf16[320,768]{1,0:T(8,128)(2,1)}, u32[]{:S(2)}, u32[]{:S(2)}) %collective-permute-start.13) | collective-permute-done | bytes 491552 | tf_op jit(solution)/shard_map/ppermute | solution.py:51
  101.4 7.9 %gram.3 = (bf16[4,320,640]{2,1,0:T(8,128)(2,1)}, bf16[4,320,640]{2,1,0:T(8,128)(2,1)}) custom-call(bf16[640,768]{1,0:T(8,128)(2,1)} %refs_0_.3, bf16[640,768]{1,0:T(8,128)(2,1)} %collective-permute-done.2.b0.refs_5_, bf16[640,768]{1,0:T(8,128)(2,1)} %collective-permute-done.11.b1.refs_6_, bf16[320,768]{1,0:T(8,128)(2,1)} %collective-permute-done.12.b2a.refs_7_, ...), custom_call_target="tpu_custom_call" | custom-call | flops 2516582400 | bytes 9000000 | tf_op jit(solution)/shard_map/gram/pallas_call | solution.py:167
  109.3 8.2 %collective-permute-start.14 = (bf16[4,320,640]{2,1,0:T(8,128)(2,1)}, bf16[4,320,640]{2,1,0:T(8,128)(2,1)S(1)}, u32[]{:S(2)}, u32[]{:S(2)}) collective-permute-start(bf16[4,320,640]{2,1,0:T(8,128)(2,1)} %get-tuple-element.47), channel_id=1, source_target_pairs={{0,1},{1,0},{2,3},{3,2},{4,5},{5,4},{6,7},{7,6},{8,9},{9,8},{10,11... | collective-permute-start | bytes 4915208 | tf_op jit(solution)/shard_map/ppermute | solution.py:51
  121.6 5.9 %collective-permute-start.8 = (bf16[320,640]{1,0:T(8,128)(2,1)S(1)}, bf16[320,640]{1,0:T(8,128)(2,1)}, u32[]{:S(2)}, u32[]{:S(2)}) collective-permute-start(bf16[320,640]{1,0:T(8,128)(2,1)S(1)} %get-tuple-element.63), channel_id=1, source_target_pairs={{0,8},{1,9},{2,10},{3,11},{4,12},{5,13},{6,14},{7,15},{8,0},{9,1},... | collective-permute-start | bytes 1228808 | tf_op jit(solution)/shard_map/ppermute | solution.py:51
  139.2 8.6 %collective-permute-done.7 = bf16[320,640]{1,0:T(8,128)(2,1)} collective-permute-done((bf16[320,640]{1,0:T(8,128)(2,1)}, bf16[320,640]{1,0:T(8,128)(2,1)}, u32[]{:S(2)}, u32[]{:S(2)}) %collective-permute-start.7) | collective-permute-done | bytes 409632 | tf_op jit(solution)/shard_map/ppermute | solution.py:51
  155.1 10.3 %collective-permute-done.16 = bf16[320,640]{1,0:T(8,128)(2,1)} collective-permute-done((bf16[320,640]{1,0:T(8,128)(2,1)}, bf16[320,640]{1,0:T(8,128)(2,1)}, u32[]{:S(2)}, u32[]{:S(2)}) %collective-permute-start.16) | collective-permute-done | bytes 409632 | tf_op jit(solution)/shard_map/ppermute | solution.py:51
  169.4 5.4 %collective-permute-done.18 = bf16[160,640]{1,0:T(8,128)(2,1)S(1)} collective-permute-done((bf16[160,640]{1,0:T(8,128)(2,1)S(1)}, bf16[160,640]{1,0:T(8,128)(2,1)S(1)}, u32[]{:S(2)}, u32[]{:S(2)}) %collective-permute-start.18) | collective-permute-done | bytes 204832 | tf_op jit(solution)/shard_map/ppermute | solution.py:51
  181.1 6.0 %collective-permute-done.19 = bf16[2,160,640]{2,1,0:T(8,128)(2,1)S(1)} collective-permute-done((bf16[2,160,640]{2,1,0:T(8,128)(2,1)S(1)}, bf16[2,160,640]{2,1,0:T(8,128)(2,1)S(1)}, u32[]{:S(2)}, u32[]{:S(2)}) %collective-permute-start.19) | collective-permute-done | bytes 409632 | tf_op jit(solution)/shard_map/ppermute | solution.py:51
  188.5 4.4 %collective-permute-start.25 = (bf16[2,160,640]{2,1,0:T(8,128)(2,1)S(1)}, bf16[2,160,640]{2,1,0:T(8,128)(2,1)S(1)}, u32[]{:S(2)}, u32[]{:S(2)}) collective-permute-start(bf16[2,160,640]{2,1,0:T(8,128)(2,1)S(1)} %maximum_select_fusion.own_ref.refs_0_), channel_id=1, source_target_pairs={{0,64},{1,65},{2,66},{3,67},{4,68},{5,69},{6,70},{7,71},{8,72},{9,... | collective-permute-start | bytes 1228808 | tf_op jit(solution)/shard_map/ppermute | solution.py:51
  193.0 4.0 %collective-permute-done.22 = bf16[2,160,640]{2,1,0:T(8,128)(2,1)S(1)} collective-permute-done((bf16[2,160,640]{2,1,0:T(8,128)(2,1)S(1)}, bf16[2,160,640]{2,1,0:T(8,128)(2,1)S(1)}, u32[]{:S(2)}, u32[]{:S(2)}) %collective-permute-start.22) | collective-permute-done | bytes 409632 | tf_op jit(solution)/shard_map/ppermute | solution.py:51
  201.8 8.3 %collective-permute-start.30 = (bf16[5,2,160,640]{3,2,1,0:T(8,128)(2,1)S(1)}, bf16[5,2,160,640]{3,2,1,0:T(8,128)(2,1)}, u32[]{:S(2)}, u32[]{:S(2)}) collective-permute-start(bf16[5,2,160,640]{3,2,1,0:T(8,128)(2,1)S(1)} %bitcast_dynamic-update-slice_fusion.5.g0), channel_id=1, source_target_pairs={{0,1},{1,0},{2,3},{3,2},{4,5},{5,4},{6,7},{7,6},{8,9},{9,8},{10,11... | collective-permute-start | bytes 6144008 | tf_op jit(solution)/shard_map/ppermute | solution.py:51
  213.5 7.6 %collective-permute-done.29 = bf16[2,160,640]{2,1,0:T(8,128)(2,1)S(1)} collective-permute-done((bf16[2,160,640]{2,1,0:T(8,128)(2,1)S(1)}, bf16[2,160,640]{2,1,0:T(8,128)(2,1)S(1)}, u32[]{:S(2)}, u32[]{:S(2)}) %collective-permute-start.29) | collective-permute-done | bytes 409632 | tf_op jit(solution)/shard_map/ppermute | solution.py:51
  230.9 8.4 %collective-permute-done.32.refs_5_ = bf16[2,160,640]{2,1,0:T(8,128)(2,1)S(1)} collective-permute-done((bf16[2,160,640]{2,1,0:T(8,128)(2,1)S(1)}, bf16[2,160,640]{2,1,0:T(8,128)(2,1)S(1)}, u32[]{:S(2)}, u32[]{:S(2)}) %collective-permute-start.32) | collective-permute-done | bytes 409632 | tf_op jit(solution)/shard_map/ppermute | solution.py:51
  244.6 9.1 %square.1 = bf16[2,160,640]{2,1,0:T(8,128)(2,1)} custom-call(bf16[2,160,640]{2,1,0:T(8,128)(2,1)} %copy-done.1, bf16[5,2,160,640]{3,2,1,0:T(8,128)(2,1)} %copy-done.2, bf16[3,2,160,640]{3,2,1,0:T(8,128)(2,1)} %copy-done, bf16[5,2,160,640]{3,2,1,0:T(8,128)(2,1)} %collective-permute-done.30.g2, bf16[3,2,160,640]{3,2,1,0:T(8,128)(2,1)} %copy-done.7, ...), custom_call_target="tpu_custom_call" | custom-call | flops 2097152000 | bytes 11000000 | tf_op jit(solution)/shard_map/square/pallas_call | solution.py:254
  259.5 6.7 %collective-permute-done.35 = bf16[2,160,640]{2,1,0:T(8,128)(2,1)S(1)} collective-permute-done((bf16[2,160,640]{2,1,0:T(8,128)(2,1)}, bf16[2,160,640]{2,1,0:T(8,128)(2,1)S(1)}, u32[]{:S(2)}, u32[]{:S(2)}) %collective-permute-start.35) | collective-permute-done | bytes 409632 | tf_op jit(solution)/shard_map/ppermute | solution.py:51
  266.3 5.8 %collective-permute-done.38 = bf16[2,160,640]{2,1,0:T(8,128)(2,1)S(1)} collective-permute-done((bf16[2,160,640]{2,1,0:T(8,128)(2,1)}, bf16[2,160,640]{2,1,0:T(8,128)(2,1)S(1)}, u32[]{:S(2)}, u32[]{:S(2)}) %collective-permute-start.38) | collective-permute-done | bytes 409632 | tf_op jit(solution)/shard_map/ppermute | solution.py:51
  282.9 7.1 %collective-permute-done.41 = bf16[2,160,640]{2,1,0:T(8,128)(2,1)S(1)} collective-permute-done((bf16[2,160,640]{2,1,0:T(8,128)(2,1)S(1)}, bf16[2,160,640]{2,1,0:T(8,128)(2,1)S(1)}, u32[]{:S(2)}, u32[]{:S(2)}) %collective-permute-start.41) | collective-permute-done | bytes 409632 | tf_op jit(solution)/shard_map/ppermute | solution.py:51
  299.0 16.0 %update.1 = bf16[640,768]{1,0:T(8,128)(2,1)} custom-call(bf16[640,768]{1,0:T(8,128)(2,1)} %refs_0_.3, bf16[5,2,160,640]{3,2,1,0:T(8,128)(2,1)} %bitcast_dynamic-update-slice_fusion.n0, bf16[3,2,160,640]{3,2,1,0:T(8,128)(2,1)} %copy-done.6, bf16[5,2,160,640]{3,2,1,0:T(8,128)(2,1)} %collective-permute-done.42.n2, ...), custom_call_target="tpu_custom_call" | custom-call | flops 5033164800 | bytes 15000000 | tf_op jit(solution)/shard_map/update/pallas_call | solution.py:309
  (137 shorter events, 110.8 us)
Async XLA Ops:
  7.2 307.8 %reduce-scatter.2.cloned.1.call-start = ((), (), s32[]{:S(2)}) async-start(), calls=%async_computation.1 | async-start | bytes 8847360 | tf_op jit(solution)/shard_map/reduce_scatter | solution.py:346
  7.2 24.7 %collective-permute-start = (bf16[640,768]{1,0:T(8,128)(2,1)}, bf16[640,768]{1,0:T(8,128)(2,1)S(1)}, u32[]{:S(2)}, u32[]{:S(2)}) collective-permute-start(bf16[640,768]{1,0:T(8,128)(2,1)} %refs_0_.3), channel_id=1, source_target_pairs={{0,16},{1,17},{2,18},{3,19},{4,20},{5,21},{6,22},{7,23},{8,24},{9,... | collective-permute-start | bytes 2949128 | tf_op jit(solution)/shard_map/ppermute | solution.py:51
  9.3 22.6 %collective-permute-start.1 = (bf16[640,768]{1,0:T(8,128)(2,1)}, bf16[640,768]{1,0:T(8,128)(2,1)S(1)}, u32[]{:S(2)}, u32[]{:S(2)}) collective-permute-start(bf16[640,768]{1,0:T(8,128)(2,1)} %refs_0_.3), channel_id=1, source_target_pairs={{0,48},{1,49},{2,50},{3,51},{4,52},{5,53},{6,54},{7,55},{8,56},{9,... | collective-permute-start | bytes 2949128 | tf_op jit(solution)/shard_map/ppermute | solution.py:51
  10.7 24.0 %collective-permute-start.2 = (bf16[640,768]{1,0:T(8,128)(2,1)}, bf16[640,768]{1,0:T(8,128)(2,1)}, u32[]{:S(2)}, u32[]{:S(2)}) collective-permute-start(bf16[640,768]{1,0:T(8,128)(2,1)} %refs_0_.3), channel_id=1, source_target_pairs={{0,64},{1,65},{2,66},{3,67},{4,68},{5,69},{6,70},{7,71},{8,72},{9,... | collective-permute-start | bytes 2949128 | tf_op jit(solution)/shard_map/ppermute | solution.py:51
  61.8 37.9 %collective-permute-start.10 = (bf16[640,768]{1,0:T(8,128)(2,1)}, bf16[640,768]{1,0:T(8,128)(2,1)}, u32[]{:S(2)}, u32[]{:S(2)}) collective-permute-start(bf16[640,768]{1,0:T(8,128)(2,1)} %collective-permute-done.2.b0.refs_5_), channel_id=1, source_target_pairs={{0,16},{1,17},{2,18},{3,19},{4,20},{5,21},{6,22},{7,23},{8,24},{9,... | collective-permute-start | bytes 2949128 | tf_op jit(solution)/shard_map/ppermute | solution.py:51
  61.8 39.6 %collective-permute-start.11 = (bf16[640,768]{1,0:T(8,128)(2,1)}, bf16[640,768]{1,0:T(8,128)(2,1)}, u32[]{:S(2)}, u32[]{:S(2)}) collective-permute-start(bf16[640,768]{1,0:T(8,128)(2,1)} %collective-permute-done.2.b0.refs_5_), channel_id=1, source_target_pairs={{0,48},{1,49},{2,50},{3,51},{4,52},{5,53},{6,54},{7,55},{8,56},{9,... | collective-permute-start | bytes 2949128 | tf_op jit(solution)/shard_map/ppermute | solution.py:51
  64.4 19.4 %collective-permute-start.12 = (bf16[320,768]{1,0:T(8,128)(2,1)}, bf16[320,768]{1,0:T(8,128)(2,1)}, u32[]{:S(2)}, u32[]{:S(2)}) collective-permute-start(bf16[320,768]{1,0:T(8,128)(2,1)} %collective-permute-done.3.b2a.refs_2_), channel_id=1, source_target_pairs={{0,64},{1,65},{2,66},{3,67},{4,68},{5,69},{6,70},{7,71},{8,72},{9,... | collective-permute-start | bytes 1474568 | tf_op jit(solution)/shard_map/ppermute | solution.py:51
  67.2 30.4 %collective-permute-start.13 = (bf16[320,768]{1,0:T(8,128)(2,1)S(1)}, bf16[320,768]{1,0:T(8,128)(2,1)}, u32[]{:S(2)}, u32[]{:S(2)}) collective-permute-start(bf16[320,768]{1,0:T(8,128)(2,1)S(1)} %collective-permute-done.4.b2b.refs_3_), channel_id=1, source_target_pairs={{0,64},{1,65},{2,66},{3,67},{4,68},{5,69},{6,70},{7,71},{8,72},{9,... | collective-permute-start | bytes 1474568 | tf_op jit(solution)/shard_map/ppermute | solution.py:51
  75.3 42.2 %collective-permute-start.5 = (bf16[4,320,640]{2,1,0:T(8,128)(2,1)}, bf16[4,320,640]{2,1,0:T(8,128)(2,1)S(1)}, u32[]{:S(2)}, u32[]{:S(2)}) collective-permute-start(bf16[4,320,640]{2,1,0:T(8,128)(2,1)} %get-tuple-element.40), channel_id=1, source_target_pairs={{0,1},{1,0},{2,3},{3,2},{4,5},{5,4},{6,7},{7,6},{8,9},{9,8},{10,11... | collective-permute-start | bytes 4915208 | tf_op jit(solution)/shard_map/ppermute | solution.py:51
  109.3 19.9 %collective-permute-start.14 = (bf16[4,320,640]{2,1,0:T(8,128)(2,1)}, bf16[4,320,640]{2,1,0:T(8,128)(2,1)S(1)}, u32[]{:S(2)}, u32[]{:S(2)}) collective-permute-start(bf16[4,320,640]{2,1,0:T(8,128)(2,1)} %get-tuple-element.47), channel_id=1, source_target_pairs={{0,1},{1,0},{2,3},{3,2},{4,5},{5,4},{6,7},{7,6},{8,9},{9,8},{10,11... | collective-permute-start | bytes 4915208 | tf_op jit(solution)/shard_map/ppermute | solution.py:51
  121.6 15.8 %collective-permute-start.8 = (bf16[320,640]{1,0:T(8,128)(2,1)S(1)}, bf16[320,640]{1,0:T(8,128)(2,1)}, u32[]{:S(2)}, u32[]{:S(2)}) collective-permute-start(bf16[320,640]{1,0:T(8,128)(2,1)S(1)} %get-tuple-element.63), channel_id=1, source_target_pairs={{0,8},{1,9},{2,10},{3,11},{4,12},{5,13},{6,14},{7,15},{8,0},{9,1},... | collective-permute-start | bytes 1228808 | tf_op jit(solution)/shard_map/ppermute | solution.py:51
  127.5 20.3 %collective-permute-start.7 = (bf16[320,640]{1,0:T(8,128)(2,1)}, bf16[320,640]{1,0:T(8,128)(2,1)}, u32[]{:S(2)}, u32[]{:S(2)}) collective-permute-start(bf16[320,640]{1,0:T(8,128)(2,1)} %get-tuple-element.64), channel_id=1, source_target_pairs={{0,12},{1,13},{2,14},{3,15},{4,0},{5,1},{6,2},{7,3},{8,4},{9,5},{1... | collective-permute-start | bytes 1228808 | tf_op jit(solution)/shard_map/ppermute | solution.py:51
  128.7 19.1 %collective-permute-start.6 = (bf16[320,640]{1,0:T(8,128)(2,1)}, bf16[320,640]{1,0:T(8,128)(2,1)}, u32[]{:S(2)}, u32[]{:S(2)}) collective-permute-start(bf16[320,640]{1,0:T(8,128)(2,1)} %get-tuple-element.62), channel_id=1, source_target_pairs={{0,4},{1,5},{2,6},{3,7},{4,8},{5,9},{6,10},{7,11},{8,12},{9,13},{1... | collective-permute-start | bytes 1228808 | tf_op jit(solution)/shard_map/ppermute | solution.py:51
  130.8 24.3 %collective-permute-start.17 = (bf16[320,640]{1,0:T(8,128)(2,1)}, bf16[320,640]{1,0:T(8,128)(2,1)}, u32[]{:S(2)}, u32[]{:S(2)}) collective-permute-start(bf16[320,640]{1,0:T(8,128)(2,1)} %get-tuple-element.66), channel_id=1, source_target_pairs={{0,8},{1,9},{2,10},{3,11},{4,12},{5,13},{6,14},{7,15},{8,0},{9,1},... | collective-permute-start | bytes 1228808 | tf_op jit(solution)/shard_map/ppermute | solution.py:51
  132.6 32.8 %collective-permute-start.16 = (bf16[320,640]{1,0:T(8,128)(2,1)}, bf16[320,640]{1,0:T(8,128)(2,1)}, u32[]{:S(2)}, u32[]{:S(2)}) collective-permute-start(bf16[320,640]{1,0:T(8,128)(2,1)} %get-tuple-element.67), channel_id=1, source_target_pairs={{0,12},{1,13},{2,14},{3,15},{4,0},{5,1},{6,2},{7,3},{8,4},{9,5},{1... | collective-permute-start | bytes 1228808 | tf_op jit(solution)/shard_map/ppermute | solution.py:51
  137.5 27.9 %collective-permute-start.15 = (bf16[320,640]{1,0:T(8,128)(2,1)}, bf16[320,640]{1,0:T(8,128)(2,1)}, u32[]{:S(2)}, u32[]{:S(2)}) collective-permute-start(bf16[320,640]{1,0:T(8,128)(2,1)} %get-tuple-element.65), channel_id=1, source_target_pairs={{0,4},{1,5},{2,6},{3,7},{4,8},{5,9},{6,10},{7,11},{8,12},{9,13},{1... | collective-permute-start | bytes 1228808 | tf_op jit(solution)/shard_map/ppermute | solution.py:51
  149.3 20.1 %collective-permute-start.9 = (bf16[160,640]{1,0:T(8,128)(2,1)S(1)}, bf16[160,640]{1,0:T(8,128)(2,1)S(1)}, u32[]{:S(2)}, u32[]{:S(2)}) collective-permute-start(bf16[160,640]{1,0:T(8,128)(2,1)S(1)} %fusion.8), channel_id=1, source_target_pairs={{0,2},{1,3},{2,0},{3,1},{4,6},{5,7},{6,4},{7,5},{8,10},{9,11},{10,... | collective-permute-start | bytes 614408 | tf_op jit(solution)/shard_map/ppermute | solution.py:51
  178.2 14.7 %collective-permute-start.21 = (bf16[2,160,640]{2,1,0:T(8,128)(2,1)S(1)}, bf16[2,160,640]{2,1,0:T(8,128)(2,1)S(1)}, u32[]{:S(2)}, u32[]{:S(2)}) collective-permute-start(bf16[2,160,640]{2,1,0:T(8,128)(2,1)S(1)} %maximum_select_fusion.own_ref.refs_0_), channel_id=1, source_target_pairs={{0,2},{1,3},{2,0},{3,1},{4,6},{5,7},{6,4},{7,5},{8,10},{9,11},{10,... | collective-permute-start | bytes 1228808 | tf_op jit(solution)/shard_map/ppermute | solution.py:51
  178.2 18.9 %collective-permute-start.22 = (bf16[2,160,640]{2,1,0:T(8,128)(2,1)S(1)}, bf16[2,160,640]{2,1,0:T(8,128)(2,1)S(1)}, u32[]{:S(2)}, u32[]{:S(2)}) collective-permute-start(bf16[2,160,640]{2,1,0:T(8,128)(2,1)S(1)} %maximum_select_fusion.own_ref.refs_0_), channel_id=1, source_target_pairs={{0,8},{1,9},{2,10},{3,11},{4,12},{5,13},{6,14},{7,15},{8,0},{9,1},... | collective-permute-start | bytes 1228808 | tf_op jit(solution)/shard_map/ppermute | solution.py:51
  179.8 17.2 %collective-permute-start.23 = (bf16[2,160,640]{2,1,0:T(8,128)(2,1)S(1)}, bf16[2,160,640]{2,1,0:T(8,128)(2,1)S(1)}, u32[]{:S(2)}, u32[]{:S(2)}) collective-permute-start(bf16[2,160,640]{2,1,0:T(8,128)(2,1)S(1)} %maximum_select_fusion.own_ref.refs_0_), channel_id=1, source_target_pairs={{0,16},{1,17},{2,18},{3,19},{4,20},{5,21},{6,22},{7,23},{8,24},{9,... | collective-permute-start | bytes 1228808 | tf_op jit(solution)/shard_map/ppermute | solution.py:51
  201.8 42.8 %collective-permute-start.30 = (bf16[5,2,160,640]{3,2,1,0:T(8,128)(2,1)S(1)}, bf16[5,2,160,640]{3,2,1,0:T(8,128)(2,1)}, u32[]{:S(2)}, u32[]{:S(2)}) collective-permute-start(bf16[5,2,160,640]{3,2,1,0:T(8,128)(2,1)S(1)} %bitcast_dynamic-update-slice_fusion.5.g0), channel_id=1, source_target_pairs={{0,1},{1,0},{2,3},{3,2},{4,5},{5,4},{6,7},{7,6},{8,9},{9,8},{10,11... | collective-permute-start | bytes 6144008 | tf_op jit(solution)/shard_map/ppermute | solution.py:51
  225.3 17.4 %collective-permute-start.31 = (bf16[3,2,160,640]{3,2,1,0:T(8,128)(2,1)S(1)}, bf16[3,2,160,640]{3,2,1,0:T(8,128)(2,1)S(1)}, u32[]{:S(2)}, u32[]{:S(2)}) collective-permute-start(bf16[3,2,160,640]{3,2,1,0:T(8,128)(2,1)S(1)} %pad_maximum_fusion.g1), channel_id=1, source_target_pairs={{0,1},{1,0},{2,3},{3,2},{4,5},{5,4},{6,7},{7,6},{8,9},{9,8},{10,11... | collective-permute-start | bytes 3686408 | tf_op jit(solution)/shard_map/ppermute | solution.py:51
  257.7 14.4 %collective-permute-start.38 = (bf16[2,160,640]{2,1,0:T(8,128)(2,1)}, bf16[2,160,640]{2,1,0:T(8,128)(2,1)S(1)}, u32[]{:S(2)}, u32[]{:S(2)}) collective-permute-start(bf16[2,160,640]{2,1,0:T(8,128)(2,1)} %square.1), channel_id=1, source_target_pairs={{0,8},{1,9},{2,10},{3,11},{4,12},{5,13},{6,14},{7,15},{8,0},{9,1},... | collective-permute-start | bytes 1228808 | tf_op jit(solution)/shard_map/ppermute | solution.py:51
  275.3 23.7 %collective-permute-start.42 = (bf16[5,2,160,640]{3,2,1,0:T(8,128)(2,1)}, bf16[5,2,160,640]{3,2,1,0:T(8,128)(2,1)}, u32[]{:S(2)}, u32[]{:S(2)}) collective-permute-start(bf16[5,2,160,640]{3,2,1,0:T(8,128)(2,1)} %bitcast_dynamic-update-slice_fusion.n0), channel_id=1, source_target_pairs={{0,1},{1,0},{2,3},{3,2},{4,5},{5,4},{6,7},{7,6},{8,9},{9,8},{10,11... | collective-permute-start | bytes 6144008 | tf_op jit(solution)/shard_map/ppermute | solution.py:51
  (39 other events, 542.0 us)
Sparse Core Ops, SparseCore 0:
  49.8 134.4 reduce-scatter.1

commit v2 on v0

v2 whole, which is shorter than its diff:
```python
import math

import jax
import jax.numpy as jnp
import numpy as np
from jax import lax
from jax.experimental import pallas as pl
from jax.experimental.pallas import tpu as pltpu
from jax.sharding import PartitionSpec as P

HEADS = 96
KV_HEADS = 8
HEAD_DIM = 128
SEQ_LEN = 1024
QD = 12288
D = 5120
ROWS = 640
COLS = 768
HALF = 320
QUART = 160
SHAPE = (2, 4, 4, 2, 2)

linear_coef = 3.4445
cubic_coef = -4.775
quintic_coef = 2.0315

VMEM = 60 * 1024 * 1024


def make_perm(move):
    pairs = []
    for source in range(128):
        place = np.unravel_index(source, SHAPE)
        target = [int(a) % b for a, b in zip(move(*place), SHAPE)]
        pairs.append((source, int(np.ravel_multi_index(target, SHAPE))))
    return pairs


X_UP = make_perm(lambda yh, x, z, yl, c: (yh, x + 1, z, yl, c))
X_DOWN = make_perm(lambda yh, x, z, yl, c: (yh, x - 1, z, yl, c))
Z_UP = make_perm(lambda yh, x, z, yl, c: (yh, x, z + 1, yl, c))
Z_DOWN = make_perm(lambda yh, x, z, yl, c: (yh, x, z - 1, yl, c))
Z_FAR = make_perm(lambda yh, x, z, yl, c: (yh, x, z + 2, yl, c))
X_FAR = make_perm(lambda yh, x, z, yl, c: (yh, x + 2, z, yl, c))
Y_HI = make_perm(lambda yh, x, z, yl, c: (yh + 1, x, z, yl, c))
Y_LO = make_perm(lambda yh, x, z, yl, c: (yh, x, z, yl + 1, c))
CORE = make_perm(lambda yh, x, z, yl, c: (yh, x, z, yl, c + 1))


def move(array, perm):
    return lax.ppermute(array, ("y_hi", "x", "grid"), perm)


def place():
    grid = lax.axis_index("grid")
    return (
        lax.axis_index("y_hi"),
        lax.axis_index("x"),
        grid // 4,
        (grid // 2) % 2,
        grid % 2,
    )


def cost(flops, bytes_accessed, transcendentals=0):
    return pl.CostEstimate(
        flops=flops, bytes_accessed=bytes_accessed, transcendentals=transcendentals
    )


def dot(a, b, ca, cb):
    return lax.dot_general(a, b, (((ca,), (cb,)), ((), ())), preferred_element_type=jnp.float32)


def attention_kernel(q_ref, k_ref, v_ref, o_ref, do_ref, out_ref):
    block = 256
    scale = 1.0 / math.sqrt(HEAD_DIM)
    rows = lax.broadcasted_iota(jnp.int32, (block, block), 0)
    cols = lax.broadcasted_iota(jnp.int32, (block, block), 1)
    keep = cols <= rows
    for r in range(SEQ_LEN // block):
        start, length = r * block, (r + 1) * block
        q = q_ref[start:length, :]
        do = do_ref[start:length, :]
        o = o_ref[start:length, :]
        delta = jnp.sum(do.astype(jnp.float32) * o.astype(jnp.float32), axis=-1, keepdims=True)
        diag = jnp.where(keep, dot(q, k_ref[start:length, :], 1, 1), -jnp.inf)
        row_max = jnp.max(diag, axis=-1, keepdims=True)
        if r:
            body = dot(q, k_ref[:start, :], 1, 1)
            row_max = jnp.maximum(row_max, jnp.max(body, axis=-1, keepdims=True))
        e = jnp.exp((diag - row_max) * scale)
        total = jnp.sum(e, axis=-1, keepdims=True)
        g = (e * (dot(do, v_ref[start:length, :], 1, 1) - delta)).astype(jnp.bfloat16)
        grad = dot(g, k_ref[start:length, :], 1, 0)
        if r:
            e = jnp.exp((body - row_max) * scale)
            total = total + jnp.sum(e, axis=-1, keepdims=True)
            g = (e * (dot(do, v_ref[:start, :], 1, 1) - delta)).astype(jnp.bfloat16)
            grad = grad + dot(g, k_ref[:start, :], 1, 0)
        grad = grad * (scale / total)
        out_ref[:, start:length] = grad.T.astype(jnp.bfloat16)


def attention(queries, keys, values, attn_out, grad_out, kv_index):
    heads = queries.shape[1] // HEAD_DIM
    mine = pl.BlockSpec((SEQ_LEN, HEAD_DIM), lambda h, kv: (0, h))
    shared = pl.BlockSpec((SEQ_LEN, HEAD_DIM), lambda h, kv: (0, kv[0]))

    def body(kv, *refs):
        attention_kernel(*refs)

    return pl.pallas_call(
        body,
        grid_spec=pltpu.PrefetchScalarGridSpec(
            num_scalar_prefetch=1,
            grid=(heads,),
            in_specs=[mine, shared, shared, mine, mine],
            out_specs=pl.BlockSpec((HEAD_DIM, SEQ_LEN), lambda h, kv: (h, 0)),
        ),
        out_shape=jax.ShapeDtypeStruct((heads * HEAD_DIM, SEQ_LEN), jnp.bfloat16),
        compiler_params=pltpu.CompilerParams(vmem_limit_bytes=VMEM),
        cost_estimate=cost(24 * 10**9, 8 * 10**6, 4 * 10**6),
        name="attention",
    )(kv_index, queries, keys, values, attn_out, grad_out)


def gradient_kernel(block_ref, gq_ref, in_ref, out_ref):
    out_ref[0] = dot(gq_ref[...], in_ref[...], 1, 0).astype(jnp.bfloat16)


def gradient_partial(grad_query_t, inputs, yh):
    return pl.pallas_call(
        gradient_kernel,
        grid_spec=pltpu.PrefetchScalarGridSpec(
            num_scalar_prefetch=1,
            grid=(4,),
            in_specs=[
                pl.BlockSpec((COLS, SEQ_LEN), lambda k, yh: (0, 0)),
                pl.BlockSpec((SEQ_LEN, ROWS), lambda k, yh: (0, yh[0] * 4 + k)),
            ],
            out_specs=pl.BlockSpec((1, COLS, ROWS), lambda k, yh: (k, 0, 0)),
        ),
        out_shape=jax.ShapeDtypeStruct((4, COLS, ROWS), jnp.bfloat16),
        compiler_params=pltpu.CompilerParams(vmem_limit_bytes=VMEM),
        cost_estimate=cost(16 * ROWS * COLS * SEQ_LEN, 12 * 10**6),
        name="gradient",
    )(yh.astype(jnp.int32).reshape(1), grad_query_t, inputs)


def momentum_kernel(m_ref, g_ref, h_ref, out_ref):
    total = h_ref[...].astype(jnp.float32)
    for n in range(4):
        total = total + g_ref[n].astype(jnp.float32)
    out_ref[...] = 0.95 * m_ref[...] + total.T


def momentum_of(momentum, terms, term):
    mine = pl.BlockSpec((128, COLS), lambda k: (k, 0))
    return pl.pallas_call(
        momentum_kernel,
        grid=(ROWS // 128,),
        in_specs=[
            mine,
            pl.BlockSpec((4, COLS, 128), lambda k: (0, 0, k)),
            pl.BlockSpec((COLS, 128), lambda k: (0, k)),
        ],
        out_specs=mine,
        out_shape=jax.ShapeDtypeStruct((ROWS, COLS), jnp.float32),
        compiler_params=pltpu.CompilerParams(vmem_limit_bytes=VMEM),
        cost_estimate=cost(9 * ROWS * COLS, 9 * 10**6),
        name="momentum",
    )(momentum, terms, term)


def gram_kernel(*refs):
    own, own_other = refs[8:10]
    outs, (lhs, rhs, sems) = refs[10:14], refs[14:]
    _, x, z, _, core = place()
    copies = []
    for n, block in enumerate(refs[:8]):
        slot = (x + n % 4 - z + 4) % 4
        side = slice(n // 4 * COLS, (n // 4 + 1) * COLS)
        copies.append(pltpu.make_async_copy(block, rhs.at[rows_of(slot, ROWS), side], sems.at[n]))
    for n, block in enumerate((own, own_other)):
        copies.append(
            pltpu.make_async_copy(
                block.at[rows_of(core, HALF), :],
                lhs.at[:, n * COLS : (n + 1) * COLS],
                sems.at[8 + n],
            )
        )
    for copy in copies:
        copy.start()
    for copy in copies:
        copy.wait()
    for pair in range(2):
        value = dot(lhs[...], rhs[pair * 2 * ROWS : (pair + 1) * 2 * ROWS, :], 1, 1)
        for n in range(2):
            out_ref = outs[pair * 2 + n]
            out_ref[...] = value[:, n * ROWS : (n + 1) * ROWS].astype(out_ref.dtype)


def gram_partial(own, own_other, blocks, other_blocks):
    shape = (HALF, ROWS)
    return pl.pallas_call(
        gram_kernel,
        in_specs=[pl.BlockSpec(memory_space=pl.ANY)] * 10,
        out_specs=[pl.BlockSpec(memory_space=pltpu.VMEM)] * 4,
        out_shape=[jax.ShapeDtypeStruct(shape, jnp.float32)]
        + [jax.ShapeDtypeStruct(shape, jnp.bfloat16)] * 3,
        scratch_shapes=[
            pltpu.VMEM((HALF, 2 * COLS), jnp.bfloat16),
            pltpu.VMEM((4 * ROWS, 2 * COLS), jnp.bfloat16),
            pltpu.SemaphoreType.DMA((10,)),
        ],
        compiler_params=pltpu.CompilerParams(vmem_limit_bytes=VMEM),
        cost_estimate=cost(1, 1),
        name="gram",
    )(*blocks, *other_blocks, own, own_other)


def piece_place(n):
    yh, x, z, yl, _ = place()
    return ((yl + n // 4 + yh) % 2) * 4 + (z + n % 4 - x + 4) % 4


def dp_block(n):
    yh, x, _, _, _ = place()
    return ((yh + n // 4) % 2) * 4 + (x + n % 4) % 4


def rows_of(index, size):
    return pl.ds(pl.multiple_of(index * size, size), size)


def square_kernel(*refs):
    grid_refs, dp_refs = refs[:8], refs[8:16]
    out_ref, lhs, rhs, acc, lhs_sems, rhs_sems = refs[20:]
    core = place()[4]
    dp_refs += tuple(refs[16].at[n] for n in range(5)) + refs[17:20]
    copies = []
    for n, piece in enumerate(grid_refs):
        copies.append(
            pltpu.make_async_copy(piece, lhs.at[:, rows_of(piece_place(n), ROWS)], lhs_sems.at[n])
        )
    for n, piece in enumerate(dp_refs):
        side = core if n < 8 else 1 - core
        copies.append(
            pltpu.make_async_copy(
                piece, rhs.at[rows_of(n % 8 * 2 + side, HALF), :], rhs_sems.at[n]
            )
        )
    for copy in copies:
        copy.start()
    for copy in copies[:8]:
        copy.wait()
    for k in range(4):
        for n in (2 * k, 2 * k + 1, 2 * k + 8, 2 * k + 9):
            copies[8 + n].wait()
        at = slice(k * 2 * ROWS, (k + 1) * 2 * ROWS)
        term = dot(lhs[:, at], rhs[at, :], 1, 0)
        if k:
            acc[...] += term
        else:
            acc[...] = term
    out = cubic_coef * lhs[:, rows_of(piece_place(0), ROWS)].astype(jnp.float32)
    out_ref[...] = (out + quintic_coef * acc[...]).astype(jnp.bfloat16)


def square(over_grid, over_dp):
    return pl.pallas_call(
        square_kernel,
        in_specs=[pl.BlockSpec(memory_space=pl.ANY)] * 20,
        out_specs=pl.BlockSpec(memory_space=pltpu.VMEM),
        out_shape=jax.ShapeDtypeStruct((HALF, ROWS), jnp.bfloat16),
        scratch_shapes=[
            pltpu.VMEM((HALF, D), jnp.bfloat16),
            pltpu.VMEM((D, ROWS), jnp.bfloat16),
            pltpu.VMEM((HALF, ROWS), jnp.float32),
            pltpu.SemaphoreType.DMA((8,)),
            pltpu.SemaphoreType.DMA((16,)),
        ],
        compiler_params=pltpu.CompilerParams(vmem_limit_bytes=VMEM),
        cost_estimate=cost(4 * HALF * D * ROWS, 11 * 10**6),
        name="square",
    )(*over_grid, *over_dp)


def update_kernel(*refs):
    n_refs, x_refs = refs[:8], refs[8:24]
    mine_ref, other_ref, lhs, rhs, acc, lhs_sems, rhs_sems = refs[24:]
    core = place()[4]
    copies = []
    for n, piece in enumerate(n_refs):
        copies.append(
            pltpu.make_async_copy(piece, lhs.at[:, rows_of(piece_place(n), ROWS)], lhs_sems.at[n])
        )
    for n in range(8):
        for side in range(2):
            copies.append(
                pltpu.make_async_copy(
                    x_refs[side * 8 + n],
                    rhs.at[n * ROWS : (n + 1) * ROWS, side * COLS : (side + 1) * COLS],
                    rhs_sems.at[2 * n + side],
                )
            )
    for copy in copies:
        copy.start()
    for copy in copies[:8]:
        copy.wait()
    for k in range(4):
        for copy in copies[8 + 4 * k : 12 + 4 * k]:
            copy.wait()
        at = slice(k * 2 * ROWS, (k + 1) * 2 * ROWS)
        term = dot(lhs[:, at], rhs[at, :], 1, 0)
        if k:
            acc[...] += term
        else:
            acc[...] = term
    own = rhs[rows_of(core, HALF), :].astype(jnp.float32)
    out = (math.sqrt(QD) * (linear_coef * own + acc[...])).astype(jnp.bfloat16)
    mine_ref[...] = out[:, :COLS]
    other_ref[...] = out[:, COLS:]


def update_of(pieces, blocks, other_blocks):
    inside = pl.BlockSpec(memory_space=pltpu.VMEM)
    out = jax.ShapeDtypeStruct((HALF, COLS), jnp.bfloat16)
    return pl.pallas_call(
        update_kernel,
        in_specs=[pl.BlockSpec(memory_space=pl.ANY)] * 24,
        out_specs=[inside, inside],
        out_shape=[out, out],
        scratch_shapes=[
            pltpu.VMEM((HALF, D), jnp.bfloat16),
            pltpu.VMEM((D, 2 * COLS), jnp.bfloat16),
            pltpu.VMEM((HALF, 2 * COLS), jnp.float32),
            pltpu.SemaphoreType.DMA((8,)),
            pltpu.SemaphoreType.DMA((16,)),
        ],
        compiler_params=pltpu.CompilerParams(vmem_limit_bytes=VMEM),
        cost_estimate=cost(1, 1),
        name="update",
    )(*pieces, *blocks, *other_blocks)


def per_device(inputs, queries, key_rows, values, attn_out, grad_out, momentum, iterate):
    yh, _, _, yl, core = place()
    together = lax.optimization_barrier
    f32, bf16 = jnp.float32, jnp.bfloat16

    own = iterate
    below = move(own, X_UP)
    above = move(own, X_DOWN)
    across = move(own, Y_HI)
    kv_index = (lax.axis_index("grid") // 2).astype(jnp.int32).reshape(1)
    grad_query_t = attention(queries, key_rows, values, attn_out, grad_out, kv_index)
    below, above, across, grad_query_t = together((below, above, across, grad_query_t))

    far_top, far_bottom = move(below[:HALF], X_UP), move(above[HALF:], X_DOWN)
    own_other, above_other, below_other = move(own, CORE), move(above, CORE), move(below, CORE)
    far_partial = gradient_partial(grad_query_t, inputs, 1 - yh)
    far_top, far_bottom, above, across, grad_query_t, far_partial = together(
        (far_top, far_bottom, above, across, grad_query_t, far_partial)
    )
    own_other, above_other, below_other, far_top = together(
        (own_other, above_other, below_other, far_top)
    )
    far = jnp.concatenate([far_top, far_bottom])

    across_below = move(across, X_UP)
    across_above = move(across, X_DOWN)
    across_far = move(far, Y_HI)
    far_other, across_other = move(far, CORE), move(across, CORE)
    near, near1, near2, near3 = gram_partial(
        own,
        own_other,
        (own, above, far, below),
        (own_other, above_other, far_other, below_other),
    )
    near1, near3 = move(near1, Z_UP), move(near3, Z_DOWN)
    partial = gradient_partial(grad_query_t, inputs, yh)
    across_below, across_above, across_far, across_other, near, near1, near2, near3, partial = (
        together(
            (across_below, across_above, across_far, across_other)
            + (near, near1, near2, near3, partial)
        )
    )
    far_partial, across_below = together((far_partial, across_below))
    far_terms = lax.all_to_all(far_partial, "x", 0, 0, tiled=True)

    far_swapped = move(across_far, CORE)
    above_swapped = move(across_above, CORE)
    below_swapped = move(across_below, CORE)
    near2 = move(near2, Z_FAR)
    far_swapped, above_swapped, below_swapped = together(
        (far_swapped, above_swapped, below_swapped)
    )
    other, other1, other2, other3 = gram_partial(
        own,
        own_other,
        (across, across_above, across_far, across_below),
        (across_other, above_swapped, far_swapped, below_swapped),
    )
    other, other1, other2, other3, near2 = together((other, other1, other2, other3, near2))
    other1, other2, other3 = move(other1, Z_UP), move(other2, Z_FAR), move(other3, Z_DOWN)
    near = near + near1.astype(f32) + near3.astype(f32) + near2.astype(f32)
    other1, other2, other3, near = together((other1, other2, other3, near))
    other = other + other1.astype(f32) + other3.astype(f32) + other2.astype(f32)
    same = yh == yl
    kept = jnp.where(same, near, other)
    rows = (kept + move(jnp.where(same, other, near).astype(bf16), Y_LO).astype(f32)).astype(bf16)

    rows, far_terms = together((rows, far_terms))

    z_below, z_above = move(rows, Z_UP), move(rows, Z_DOWN)
    x_below, x_above = move(rows, X_UP), move(rows, X_DOWN)
    lo, x_across = move(rows, Y_LO), move(rows, Y_HI)
    z_far, x_far = move(rows, Z_FAR), move(rows, X_FAR)
    z_below, z_above, x_below, x_above, lo, x_across, z_far, x_far = together(
        (z_below, z_above, x_below, x_above, lo, x_across, z_far, x_far)
    )
    lo_below, lo_above, lo_far = move(lo, Z_UP), move(lo, Z_DOWN), move(z_far, Y_LO)
    a_below, a_above, a_far = move(x_across, X_UP), move(x_across, X_DOWN), move(x_far, Y_HI)
    first_other = move(jnp.stack([rows, x_above, x_far, x_below, x_across]), CORE)
    lo_below, lo_above, lo_far, a_below, a_above, a_far = together(
        (lo_below, lo_above, lo_far, a_below, a_above, a_far)
    )
    partial, lo_below = together((partial, lo_below))
    terms = lax.all_to_all(partial, "x", 0, 0, tiled=True)
    combined = square(
        (rows, z_above, z_far, z_below, lo, lo_above, lo_far, lo_below),
        (rows, x_above, x_far, x_below, x_across, a_above, a_far, a_below)
        + (first_other, move(a_above, CORE), move(a_far, CORE), move(a_below, CORE)),
    )

    z_below, z_above = move(combined, Z_UP), move(combined, Z_DOWN)
    lo, z_far = move(combined, Y_LO), move(combined, Z_FAR)
    far_term = move(sum(far_terms[n].astype(f32) for n in range(4)).astype(bf16), Y_HI)
    z_below, z_above, lo, z_far, far_term = together((z_below, z_above, lo, z_far, far_term))
    lo_below, lo_above, lo_far = move(lo, Z_UP), move(lo, Z_DOWN), move(z_far, Y_LO)
    lo_below, lo_above, lo_far = together((lo_below, lo_above, lo_far))
    mine, theirs = update_of(
        (combined, z_above, z_far, z_below, lo, lo_above, lo_far, lo_below),
        (own, above, far, below, across, across_above, across_far, across_below),
        (own_other, above_other, far_other, below_other, across_other)
        + (above_swapped, far_swapped, below_swapped),
    )
    momentum, theirs = together((momentum, theirs))
    momentum_next = momentum_of(momentum, terms, far_term)
    theirs = move(theirs, CORE)
    update = jnp.where(
        core == 0, jnp.concatenate([mine, theirs]), jnp.concatenate([theirs, mine])
    )
    return (momentum_next, update)


def solution(mesh):
    parts = jax.sharding.Mesh(mesh.devices.reshape(2, 4, 16), ("y_hi", "x", "grid"))
    dp = ("y_hi", "x")
    rows, both = P(dp, None), P(dp, "grid")
    return jax.shard_map(
        per_device,
        mesh=parts,
        in_specs=(rows, both, rows, rows, both, both, both, both),
        out_specs=(both, both),
        check_vma=False,
    )
```

time: 524 us -> 270 us (0.52)
  waiting for transfers between devices: 356 us -> 103 us
  matrix products: 109 us -> 0 us
  starting transfers between devices: 0.16 us -> 75.7 us
  Pallas kernels: 0 us -> 73.3 us
  local copies, waits for them, and re-layouts: 38.3 us -> 9.71 us
  between operations: 13.9 us -> 1 us
    all_gather x2 -> x0, waiting for transfers between devices: 208 us -> none  [the longest x1 109 us: per_device(): iterate_all = lax.all_gather(iterate, 'dp', axis=0, tiled=True)]
    dot_general x10 -> x0, matrix products: 109 us -> none  [the longest x2 34 us: per_device(): jnp.einsum('hqk,kd->qhd', grad_score, key_dev, preferred_element_type=jnp...]
    unnamed x5 -> x0, waiting for transfers between devices: 104 us -> none
    ppermute x0 -> x50, waiting for transfers between devices: none -> 103 us  [move(): return lax.ppermute(array, ('y_hi', 'x', 'grid'), perm)]
    pallas_call x0 -> x8, Pallas kernels: none -> 73.3 us  [the longest x2 17.4 us: gradient_partial(): pl.pallas_call(gradient_kernel, grid_spec=pltpu.PrefetchScalarGridSpec(nu...]
    ppermute x0 -> x50, starting transfers between devices: none -> 66.1 us  [move(): return lax.ppermute(array, ('y_hi', 'x', 'grid'), perm)]
    psum x1 -> x0, waiting for transfers between devices: 44 us -> none  [per_device(): gram_cols = lax.psum(partial_gram.astype(jnp.bfloat16), 'grid')]
    unnamed x22 -> x73, local copies, waits for them, and re-layouts: 30.4 us -> 7.24 us
  transfers between devices with their start and end apart: 4 -> 52, of which waited for: 4 -> 28; matrix products, arithmetic and copies ran while one was open for 25% -> 3% of each run, Pallas kernels for 0% -> 25%
where the time goes in v2:
time: 270 us; the launch traced here: 269 us
  waiting for transfers between devices  103 us (38%)
  starting transfers between devices  75.7 us (28%)
  Pallas kernels  73.3 us (27%)
  local copies, waits for them, and re-layouts  9.71 us (4%)
  other arithmetic  6.96 us (3%)
    ppermute x50, waiting for transfers between devices, move(): return lax.ppermute(array, ('y_hi', 'x', 'grid'), perm)  103 us
    ppermute x50, starting transfers between devices, move(): return lax.ppermute(array, ('y_hi', 'x', 'grid'), perm)  66.1 us
    pallas_call x2, Pallas kernels, gradient_partial(): pl.pallas_call(gradient_kernel, grid_spec=pltpu.PrefetchScalarGridSpec(nu...  17.4 us
    pallas_call x1, Pallas kernels, attention(): pl.pallas_call(body, grid_spec=pltpu.PrefetchScalarGridSpec(num_scalar_pr...  14.3 us
    pallas_call x2, Pallas kernels, gram_partial(): pl.pallas_call(gram_kernel, in_specs=[pl.BlockSpec(memory_space=pl.ANY)]...  14.1 us
    pallas_call x1, Pallas kernels, update_of(): pl.pallas_call(update_kernel, in_specs=[pl.BlockSpec(memory_space=pl.ANY)...  12.5 us
    pallas_call x1, Pallas kernels, square(): pl.pallas_call(square_kernel, in_specs=[pl.BlockSpec(memory_space=pl.ANY)...  8.96 us
    unnamed x73, local copies, waits for them, and re-layouts  7.24 us
  transfers between devices with their start and end apart: 52, of which 28 were waited for; matrix products, arithmetic and copies ran while one was open for 3% of the time, Pallas kernels for 25%

profile of v2, /device:TPU:1, one launch (start us, length us, event | category | flops | bytes accessed | tf_op | source)
XLA Modules:
  0.0 269.4 jit_solution(4737275640069249230)
XLA Ops:
  7.6 14.3 %attention.1.gq_ref = bf16[768,1024]{1,0:T(8,128)(2,1)} custom-call(s32[1]{0:T(128)} %bitcast.kv, bf16[1024,768]{1,0:T(8,128)(2,1)} %refs_0_.2, bf16[1024,1024]{1,0:T(8,128)(2,1)} %refs_1_.1, bf16[1024,1024]{1,0:T(8,128)(2,1)} %refs_2_.1, bf16[1024,768]{1,0:T(8,128)(2,1)} %refs_3_.1, bf16[1024,768]{1,0:T(8,128)(2,1)} %refs_4_.1), custom_call_target="tpu_custom_call" | custom-call | flops 24000000000 | bytes 8000000 | tf_op jit(solution)/shard_map/attention/pallas_call | solution.py:113
  21.9 5.4 %collective-permute-done.2.refs_0_.refs_12_ = bf16[640,768]{1,0:T(8,128)(2,1)} collective-permute-done((bf16[640,768]{1,0:T(8,128)(2,1)}, bf16[640,768]{1,0:T(8,128)(2,1)}, u32[]{:S(2)}, u32[]{:S(2)}) %collective-permute-start.2) | collective-permute-done | bytes 983072 | tf_op jit(solution)/shard_map/ppermute | solution.py:51
  37.6 8.8 %gradient.2 = bf16[4,768,640]{2,1,0:T(8,128)(2,1)} custom-call(s32[1]{0:T(128)} %bitcast.1.block_ref, bf16[768,1024]{1,0:T(8,128)(2,1)} %attention.1.gq_ref, bf16[1024,5120]{1,0:T(8,128)(2,1)} %in_ref.3), custom_call_target="tpu_custom_call" | custom-call | flops 8053063680 | bytes 12000000 | tf_op jit(solution)/shard_map/gradient/pallas_call | solution.py:133
  53.9 7.1 %gram.2 = (f32[320,640]{1,0:T(8,128)}, bf16[320,640]{1,0:T(8,128)(2,1)}, bf16[320,640]{1,0:T(8,128)(2,1)}, bf16[320,640]{1,0:T(8,128)(2,1)}) custom-call(bf16[640,768]{1,0:T(8,128)(2,1)} %refs_8_.5, bf16[640,768]{1,0:T(8,128)(2,1)} %copy-done.1, bf16[640,768]{1,0:T(8,128)(2,1)} %copy-done.3, bf16[640,768]{1,0:T(8,128)(2,1)} %copy-done.2, ...), custom_call_target="tpu_custom_call" | custom-call | flops 1 | bytes 1 | tf_op jit(solution)/shard_map/gram/pallas_call | solution.py:206
  64.9 8.7 %gradient.3 = bf16[4,768,640]{2,1,0:T(8,128)(2,1)} custom-call(s32[1]{0:T(128)} %bitcast.2.block_ref, bf16[768,1024]{1,0:T(8,128)(2,1)} %attention.1.gq_ref, bf16[1024,5120]{1,0:T(8,128)(2,1)} %in_ref.3), custom_call_target="tpu_custom_call" | custom-call | flops 8053063680 | bytes 12000000 | tf_op jit(solution)/shard_map/gradient/pallas_call | solution.py:133
  77.1 4.8 %all-to-all-start = ((bf16[4,768,640]{2,1,0:T(8,128)(2,1)}), bf16[4,768,640]{2,1,0:T(8,128)(2,1)}, u32[]{:S(2)}, u32[]{:S(2)}) async-start(bf16[4,768,640]{2,1,0:T(8,128)(2,1)} %gradient.2), calls=%async_computation | async-start | bytes 7864320 | tf_op jit(solution)/shard_map/all_to_all | solution.py:391
  84.1 3.6 %collective-permute-start.18 = (bf16[320,640]{1,0:T(8,128)(2,1)}, bf16[320,640]{1,0:T(8,128)(2,1)}, u32[]{:S(2)}, u32[]{:S(2)}) collective-permute-start(bf16[320,640]{1,0:T(8,128)(2,1)} %get-tuple-element.107), channel_id=1, source_target_pairs={{0,8},{1,9},{2,10},{3,11},{4,12},{5,13},{6,14},{7,15},{8,0},{9,1},... | collective-permute-start | bytes 1228808 | tf_op jit(solution)/shard_map/ppermute | solution.py:51
  89.9 7.1 %gram.3 = (f32[320,640]{1,0:T(8,128)}, bf16[320,640]{1,0:T(8,128)(2,1)}, bf16[320,640]{1,0:T(8,128)(2,1)}, bf16[320,640]{1,0:T(8,128)(2,1)}) custom-call(bf16[640,768]{1,0:T(8,128)(2,1)} %collective-permute-done.2.refs_0_.refs_12_, bf16[640,768]{1,0:T(8,128)(2,1)} %collective-permute-done.6.refs_1_.refs_13_, ...), custom_call_target="tpu_custom_call" | custom-call | flops 1 | bytes 1 | tf_op jit(solution)/shard_map/gram/pallas_call | solution.py:206
  98.6 3.3 %collective-permute-start.20 = (bf16[320,640]{1,0:T(8,128)(2,1)}, bf16[320,640]{1,0:T(8,128)(2,1)S(1)}, u32[]{:S(2)}, u32[]{:S(2)}) collective-permute-start(bf16[320,640]{1,0:T(8,128)(2,1)} %get-tuple-element.109), channel_id=1, source_target_pairs={{0,8},{1,9},{2,10},{3,11},{4,12},{5,13},{6,14},{7,15},{8,0},{9,1},... | collective-permute-start | bytes 1228808 | tf_op jit(solution)/shard_map/ppermute | solution.py:51
  104.0 6.0 %collective-permute-done.19 = bf16[320,640]{1,0:T(8,128)(2,1)S(1)} collective-permute-done((bf16[320,640]{1,0:T(8,128)(2,1)}, bf16[320,640]{1,0:T(8,128)(2,1)S(1)}, u32[]{:S(2)}, u32[]{:S(2)}) %collective-permute-start.19) | collective-permute-done | bytes 409632 | tf_op jit(solution)/shard_map/ppermute | solution.py:51
  110.0 9.6 %collective-permute-done.20 = bf16[320,640]{1,0:T(8,128)(2,1)S(1)} collective-permute-done((bf16[320,640]{1,0:T(8,128)(2,1)}, bf16[320,640]{1,0:T(8,128)(2,1)S(1)}, u32[]{:S(2)}, u32[]{:S(2)}) %collective-permute-start.20) | collective-permute-done | bytes 409632 | tf_op jit(solution)/shard_map/ppermute | solution.py:51
  120.4 8.9 %collective-permute-done.22 = bf16[320,640]{1,0:T(8,128)(2,1)S(1)} collective-permute-done((bf16[320,640]{1,0:T(8,128)(2,1)S(1)}, bf16[320,640]{1,0:T(8,128)(2,1)S(1)}, u32[]{:S(2)}, u32[]{:S(2)}) %collective-permute-start.22) | collective-permute-done | bytes 409632 | tf_op jit(solution)/shard_map/ppermute | solution.py:51
  129.6 3.3 %collective-permute-start.30 = (bf16[320,640]{1,0:T(8,128)(2,1)S(1)}, bf16[320,640]{1,0:T(8,128)(2,1)S(1)}, u32[]{:S(2)}, u32[]{:S(2)}) collective-permute-start(bf16[320,640]{1,0:T(8,128)(2,1)S(1)} %add_convert_fusion.1.refs_0_.refs_8_), channel_id=1, source_target_pairs={{0,32},{1,33},{2,34},{3,35},{4,36},{5,37},{6,38},{7,39},{8,40},{9,... | collective-permute-start | bytes 1228808 | tf_op jit(solution)/shard_map/ppermute | solution.py:51
  142.4 5.5 %collective-permute-start.24 = (bf16[320,640]{1,0:T(8,128)(2,1)S(1)}, bf16[320,640]{1,0:T(8,128)(2,1)S(1)}, u32[]{:S(2)}, u32[]{:S(2)}) collective-permute-start(bf16[320,640]{1,0:T(8,128)(2,1)S(1)} %add_convert_fusion.1.refs_0_.refs_8_), channel_id=1, source_target_pairs={{0,12},{1,13},{2,14},{3,15},{4,0},{5,1},{6,2},{7,3},{8,4},{9,5},{1... | collective-permute-start | bytes 1228808 | tf_op jit(solution)/shard_map/ppermute | solution.py:51
  159.6 4.7 %collective-permute-start.37 = (bf16[5,320,640]{2,1,0:T(8,128)(2,1)}, bf16[5,320,640]{2,1,0:T(8,128)(2,1)}, u32[]{:S(2)}, u32[]{:S(2)}) collective-permute-start(bf16[5,320,640]{2,1,0:T(8,128)(2,1)} %bitcast_dynamic-update-slice_fusion), channel_id=1, source_target_pairs={{0,1},{1,0},{2,3},{3,2},{4,5},{5,4},{6,7},{7,6},{8,9},{9,8},{10,11... | collective-permute-start | bytes 6144008 | tf_op jit(solution)/shard_map/ppermute | solution.py:51
  167.7 7.6 %collective-permute-done.33.refs_6_ = bf16[320,640]{1,0:T(8,128)(2,1)S(1)} collective-permute-done((bf16[320,640]{1,0:T(8,128)(2,1)S(1)}, bf16[320,640]{1,0:T(8,128)(2,1)S(1)}, u32[]{:S(2)}, u32[]{:S(2)}) %collective-permute-start.33) | collective-permute-done | bytes 409632 | tf_op jit(solution)/shard_map/ppermute | solution.py:51
  177.3 7.4 %collective-permute-done.36.refs_14_ = bf16[320,640]{1,0:T(8,128)(2,1)} collective-permute-done((bf16[320,640]{1,0:T(8,128)(2,1)S(1)}, bf16[320,640]{1,0:T(8,128)(2,1)}, u32[]{:S(2)}, u32[]{:S(2)}) %collective-permute-start.36) | collective-permute-done | bytes 409632 | tf_op jit(solution)/shard_map/ppermute | solution.py:51
  187.0 4.8 %all-to-all-start.1 = ((bf16[4,768,640]{2,1,0:T(8,128)(2,1)}), bf16[4,768,640]{2,1,0:T(8,128)(2,1)}, u32[]{:S(2)}, u32[]{:S(2)}) async-start(bf16[4,768,640]{2,1,0:T(8,128)(2,1)} %gradient.3), calls=%async_computation.1 | async-start | bytes 7864320 | tf_op jit(solution)/shard_map/all_to_all | solution.py:431
  200.0 9.0 %square.1.refs_0_ = bf16[320,640]{1,0:T(8,128)(2,1)} custom-call(bf16[320,640]{1,0:T(8,128)(2,1)} %copy-done.9, bf16[320,640]{1,0:T(8,128)(2,1)} %copy-done.25, bf16[320,640]{1,0:T(8,128)(2,1)} %copy-done.23, bf16[320,640]{1,0:T(8,128)(2,1)} %copy-done.26, bf16[320,640]{1,0:T(8,128)(2,1)} %copy-done.24, bf16[320,640]{1,0:T(8,128)(2,1)} %copy-done.28, ...), custom_call_target="tpu_custom_call" | custom-call | flops 4194304000 | bytes 11000000 | tf_op jit(solution)/shard_map/square/pallas_call | solution.py:272
  212.1 10.7 %collective-permute-done.45.h_ref = bf16[768,640]{1,0:T(8,128)(2,1)S(1)} collective-permute-done((bf16[768,640]{1,0:T(8,128)(2,1)S(1)}, bf16[768,640]{1,0:T(8,128)(2,1)S(1)}, u32[]{:S(2)}, u32[]{:S(2)}) %collective-permute-start.45) | collective-permute-done | bytes 983072 | tf_op jit(solution)/shard_map/ppermute | solution.py:51
  222.7 7.2 %collective-permute-done.43.refs_4_ = bf16[320,640]{1,0:T(8,128)(2,1)S(1)} collective-permute-done((bf16[320,640]{1,0:T(8,128)(2,1)}, bf16[320,640]{1,0:T(8,128)(2,1)S(1)}, u32[]{:S(2)}, u32[]{:S(2)}) %collective-permute-start.43) | collective-permute-done | bytes 409632 | tf_op jit(solution)/shard_map/ppermute | solution.py:51
  232.9 8.8 %collective-permute-done.48.refs_6_ = bf16[320,640]{1,0:T(8,128)(2,1)S(1)} collective-permute-done((bf16[320,640]{1,0:T(8,128)(2,1)S(1)}, bf16[320,640]{1,0:T(8,128)(2,1)S(1)}, u32[]{:S(2)}, u32[]{:S(2)}) %collective-permute-start.48) | collective-permute-done | bytes 409632 | tf_op jit(solution)/shard_map/ppermute | solution.py:51
  244.5 12.5 %update.1 = (bf16[320,768]{1,0:T(8,128)(2,1)}, bf16[320,768]{1,0:T(8,128)(2,1)}) custom-call(bf16[320,640]{1,0:T(8,128)(2,1)} %square.1.refs_0_, bf16[320,640]{1,0:T(8,128)(2,1)} %copy-done.14, bf16[320,640]{1,0:T(8,128)(2,1)} %copy-done.12, bf16[320,640]{1,0:T(8,128)(2,1)} %copy-done.15, bf16[320,640]{1,0:T(8,128)(2,1)} %copy-done.13, ...), custom_call_target="tpu_custom_call" | custom-call | flops 1 | bytes 1 | tf_op jit(solution)/shard_map/update/pallas_call | solution.py:330
  263.5 6.0 %momentum.1 = f32[640,768]{1,0:T(8,128)} custom-call(f32[640,768]{1,0:T(8,128)} %m_ref, bf16[4,768,640]{2,1,0:T(8,128)(2,1)} %all-to-all-done.1.g_ref, bf16[768,640]{1,0:T(8,128)(2,1)} %copy-done.10), custom_call_target="tpu_custom_call" | custom-call | flops 4423680 | bytes 9000000 | tf_op jit(solution)/shard_map/momentum/pallas_call | solution.py:160
  (170 shorter events, 93.6 us)
Async XLA Ops:
  0.6 47.9 %collective-permute-start.7 = (bf16[640,768]{1,0:T(8,128)(2,1)}, bf16[640,768]{1,0:T(8,128)(2,1)S(1)}, u32[]{:S(2)}, u32[]{:S(2)}) collective-permute-start(bf16[640,768]{1,0:T(8,128)(2,1)} %refs_8_.5), channel_id=1, source_target_pairs={{0,1},{1,0},{2,3},{3,2},{4,5},{5,4},{6,7},{7,6},{8,9},{9,8},{10,11... | collective-permute-start | bytes 2949128 | tf_op jit(solution)/shard_map/ppermute | solution.py:51
  2.1 25.2 %collective-permute-start.2 = (bf16[640,768]{1,0:T(8,128)(2,1)}, bf16[640,768]{1,0:T(8,128)(2,1)}, u32[]{:S(2)}, u32[]{:S(2)}) collective-permute-start(bf16[640,768]{1,0:T(8,128)(2,1)} %refs_8_.5), channel_id=1, source_target_pairs={{0,64},{1,65},{2,66},{3,67},{4,68},{5,69},{6,70},{7,71},{8,72},{9,... | collective-permute-start | bytes 2949128 | tf_op jit(solution)/shard_map/ppermute | solution.py:51
  5.1 23.6 %collective-permute-start.1 = (bf16[640,768]{1,0:T(8,128)(2,1)}, bf16[640,768]{1,0:T(8,128)(2,1)S(1)}, u32[]{:S(2)}, u32[]{:S(2)}) collective-permute-start(bf16[640,768]{1,0:T(8,128)(2,1)} %refs_8_.5), channel_id=1, source_target_pairs={{0,48},{1,49},{2,50},{3,51},{4,52},{5,53},{6,54},{7,55},{8,56},{9,... | collective-permute-start | bytes 2949128 | tf_op jit(solution)/shard_map/ppermute | solution.py:51
  7.6 24.1 %collective-permute-start = (bf16[640,768]{1,0:T(8,128)(2,1)}, bf16[640,768]{1,0:T(8,128)(2,1)S(1)}, u32[]{:S(2)}, u32[]{:S(2)}) collective-permute-start(bf16[640,768]{1,0:T(8,128)(2,1)} %refs_8_.5), channel_id=1, source_target_pairs={{0,16},{1,17},{2,18},{3,19},{4,20},{5,21},{6,22},{7,23},{8,24},{9,... | collective-permute-start | bytes 2949128 | tf_op jit(solution)/shard_map/ppermute | solution.py:51
  31.7 16.9 %collective-permute-start.8 = (bf16[640,768]{1,0:T(8,128)(2,1)S(1)}, bf16[640,768]{1,0:T(8,128)(2,1)}, u32[]{:S(2)}, u32[]{:S(2)}) collective-permute-start(bf16[640,768]{1,0:T(8,128)(2,1)S(1)} %collective-permute-done.1.refs_1_.refs_9_), channel_id=1, source_target_pairs={{0,1},{1,0},{2,3},{3,2},{4,5},{5,4},{6,7},{7,6},{8,9},{9,8},{10,11... | collective-permute-start | bytes 2949128 | tf_op jit(solution)/shard_map/ppermute | solution.py:51
  33.2 15.4 %collective-permute-start.9 = (bf16[640,768]{1,0:T(8,128)(2,1)S(1)}, bf16[640,768]{1,0:T(8,128)(2,1)}, u32[]{:S(2)}, u32[]{:S(2)}) collective-permute-start(bf16[640,768]{1,0:T(8,128)(2,1)S(1)} %collective-permute-done.refs_3_.refs_11_), channel_id=1, source_target_pairs={{0,1},{1,0},{2,3},{3,2},{4,5},{5,4},{6,7},{7,6},{8,9},{9,8},{10,11... | collective-permute-start | bytes 2949128 | tf_op jit(solution)/shard_map/ppermute | solution.py:51
  50.2 23.7 %collective-permute-start.6 = (bf16[640,768]{1,0:T(8,128)(2,1)}, bf16[640,768]{1,0:T(8,128)(2,1)}, u32[]{:S(2)}, u32[]{:S(2)}) collective-permute-start(bf16[640,768]{1,0:T(8,128)(2,1)} %collective-permute-done.2.refs_0_.refs_12_), channel_id=1, source_target_pairs={{0,48},{1,49},{2,50},{3,51},{4,52},{5,53},{6,54},{7,55},{8,56},{9,... | collective-permute-start | bytes 2949128 | tf_op jit(solution)/shard_map/ppermute | solution.py:51
  52.9 24.1 %collective-permute-start.5 = (bf16[640,768]{1,0:T(8,128)(2,1)}, bf16[640,768]{1,0:T(8,128)(2,1)}, u32[]{:S(2)}, u32[]{:S(2)}) collective-permute-start(bf16[640,768]{1,0:T(8,128)(2,1)} %collective-permute-done.2.refs_0_.refs_12_), channel_id=1, source_target_pairs={{0,16},{1,17},{2,18},{3,19},{4,20},{5,21},{6,22},{7,23},{8,24},{9,... | collective-permute-start | bytes 2949128 | tf_op jit(solution)/shard_map/ppermute | solution.py:51
  52.9 24.2 %collective-permute-start.10 = (bf16[640,768]{1,0:T(8,128)(2,1)S(1)}, bf16[640,768]{1,0:T(8,128)(2,1)}, u32[]{:S(2)}, u32[]{:S(2)}) collective-permute-start(bf16[640,768]{1,0:T(8,128)(2,1)S(1)} %constant_dynamic-update-slice_fusion.refs_2_.refs_10_), channel_id=1, source_target_pairs={{0,64},{1,65},{2,66},{3,67},{4,68},{5,69},{6,70},{7,71},{8,72},{9,... | collective-permute-start | bytes 2949128 | tf_op jit(solution)/shard_map/ppermute | solution.py:51
  61.0 16.1 %collective-permute-start.13 = (bf16[320,640]{1,0:T(8,128)(2,1)}, bf16[320,640]{1,0:T(8,128)(2,1)}, u32[]{:S(2)}, u32[]{:S(2)}) collective-permute-start(bf16[320,640]{1,0:T(8,128)(2,1)} %get-tuple-element.90), channel_id=1, source_target_pairs={{0,4},{1,5},{2,6},{3,7},{4,8},{5,9},{6,10},{7,11},{8,12},{9,13},{1... | collective-permute-start | bytes 1228808 | tf_op jit(solution)/shard_map/ppermute | solution.py:51
  62.7 14.4 %collective-permute-start.14 = (bf16[320,640]{1,0:T(8,128)(2,1)}, bf16[320,640]{1,0:T(8,128)(2,1)}, u32[]{:S(2)}, u32[]{:S(2)}) collective-permute-start(bf16[320,640]{1,0:T(8,128)(2,1)} %get-tuple-element.92), channel_id=1, source_target_pairs={{0,12},{1,13},{2,14},{3,15},{4,0},{5,1},{6,2},{7,3},{8,4},{9,5},{1... | collective-permute-start | bytes 1228808 | tf_op jit(solution)/shard_map/ppermute | solution.py:51
  77.1 52.5 %all-to-all-start = ((bf16[4,768,640]{2,1,0:T(8,128)(2,1)}), bf16[4,768,640]{2,1,0:T(8,128)(2,1)}, u32[]{:S(2)}, u32[]{:S(2)}) async-start(bf16[4,768,640]{2,1,0:T(8,128)(2,1)} %gradient.2), calls=%async_computation | async-start | bytes 7864320 | tf_op jit(solution)/shard_map/all_to_all | solution.py:391
  98.6 21.0 %collective-permute-start.20 = (bf16[320,640]{1,0:T(8,128)(2,1)}, bf16[320,640]{1,0:T(8,128)(2,1)S(1)}, u32[]{:S(2)}, u32[]{:S(2)}) collective-permute-start(bf16[320,640]{1,0:T(8,128)(2,1)} %get-tuple-element.109), channel_id=1, source_target_pairs={{0,8},{1,9},{2,10},{3,11},{4,12},{5,13},{6,14},{7,15},{8,0},{9,1},... | collective-permute-start | bytes 1228808 | tf_op jit(solution)/shard_map/ppermute | solution.py:51
  101.9 17.7 %collective-permute-start.21 = (bf16[320,640]{1,0:T(8,128)(2,1)}, bf16[320,640]{1,0:T(8,128)(2,1)S(1)}, u32[]{:S(2)}, u32[]{:S(2)}) collective-permute-start(bf16[320,640]{1,0:T(8,128)(2,1)} %get-tuple-element.110), channel_id=1, source_target_pairs={{0,12},{1,13},{2,14},{3,15},{4,0},{5,1},{6,2},{7,3},{8,4},{9,5},{1... | collective-permute-start | bytes 1228808 | tf_op jit(solution)/shard_map/ppermute | solution.py:51
  135.2 15.5 %collective-permute-start.27 = (bf16[320,640]{1,0:T(8,128)(2,1)S(1)}, bf16[320,640]{1,0:T(8,128)(2,1)S(1)}, u32[]{:S(2)}, u32[]{:S(2)}) collective-permute-start(bf16[320,640]{1,0:T(8,128)(2,1)S(1)} %add_convert_fusion.1.refs_0_.refs_8_), channel_id=1, source_target_pairs={{0,2},{1,3},{2,0},{3,1},{4,6},{5,7},{6,4},{7,5},{8,10},{9,11},{10,... | collective-permute-start | bytes 1228808 | tf_op jit(solution)/shard_map/ppermute | solution.py:51
  135.8 15.0 %collective-permute-start.26 = (bf16[320,640]{1,0:T(8,128)(2,1)S(1)}, bf16[320,640]{1,0:T(8,128)(2,1)S(1)}, u32[]{:S(2)}, u32[]{:S(2)}) collective-permute-start(bf16[320,640]{1,0:T(8,128)(2,1)S(1)} %add_convert_fusion.1.refs_0_.refs_8_), channel_id=1, source_target_pairs={{0,48},{1,49},{2,50},{3,51},{4,52},{5,53},{6,54},{7,55},{8,56},{9,... | collective-permute-start | bytes 1228808 | tf_op jit(solution)/shard_map/ppermute | solution.py:51
  159.6 39.4 %collective-permute-start.37 = (bf16[5,320,640]{2,1,0:T(8,128)(2,1)}, bf16[5,320,640]{2,1,0:T(8,128)(2,1)}, u32[]{:S(2)}, u32[]{:S(2)}) collective-permute-start(bf16[5,320,640]{2,1,0:T(8,128)(2,1)} %bitcast_dynamic-update-slice_fusion), channel_id=1, source_target_pairs={{0,1},{1,0},{2,3},{3,2},{4,5},{5,4},{6,7},{7,6},{8,9},{9,8},{10,11... | collective-permute-start | bytes 6144008 | tf_op jit(solution)/shard_map/ppermute | solution.py:51
  166.2 18.5 %collective-permute-start.36 = (bf16[320,640]{1,0:T(8,128)(2,1)S(1)}, bf16[320,640]{1,0:T(8,128)(2,1)}, u32[]{:S(2)}, u32[]{:S(2)}) collective-permute-start(bf16[320,640]{1,0:T(8,128)(2,1)S(1)} %collective-permute-done.30.refs_10_), channel_id=1, source_target_pairs={{0,64},{1,65},{2,66},{3,67},{4,68},{5,69},{6,70},{7,71},{8,72},{9,... | collective-permute-start | bytes 1228808 | tf_op jit(solution)/shard_map/ppermute | solution.py:51
  187.0 76.5 %all-to-all-start.1 = ((bf16[4,768,640]{2,1,0:T(8,128)(2,1)}), bf16[4,768,640]{2,1,0:T(8,128)(2,1)}, u32[]{:S(2)}, u32[]{:S(2)}) async-start(bf16[4,768,640]{2,1,0:T(8,128)(2,1)} %gradient.3), calls=%async_computation.1 | async-start | bytes 7864320 | tf_op jit(solution)/shard_map/all_to_all | solution.py:431
  197.5 25.2 %collective-permute-start.45 = (bf16[768,640]{1,0:T(8,128)(2,1)S(1)}, bf16[768,640]{1,0:T(8,128)(2,1)S(1)}, u32[]{:S(2)}, u32[]{:S(2)}) collective-permute-start(bf16[768,640]{1,0:T(8,128)(2,1)S(1)} %fusion), channel_id=1, source_target_pairs={{0,64},{1,65},{2,66},{3,67},{4,68},{5,69},{6,70},{7,71},{8,72},{9,... | collective-permute-start | bytes 2949128 | tf_op jit(solution)/shard_map/ppermute | solution.py:51
  209.0 13.8 %collective-permute-start.44 = (bf16[320,640]{1,0:T(8,128)(2,1)}, bf16[320,640]{1,0:T(8,128)(2,1)S(1)}, u32[]{:S(2)}, u32[]{:S(2)}) collective-permute-start(bf16[320,640]{1,0:T(8,128)(2,1)} %square.1.refs_0_), channel_id=1, source_target_pairs={{0,8},{1,9},{2,10},{3,11},{4,12},{5,13},{6,14},{7,15},{8,0},{9,1},... | collective-permute-start | bytes 1228808 | tf_op jit(solution)/shard_map/ppermute | solution.py:51
  209.4 20.5 %collective-permute-start.43 = (bf16[320,640]{1,0:T(8,128)(2,1)}, bf16[320,640]{1,0:T(8,128)(2,1)S(1)}, u32[]{:S(2)}, u32[]{:S(2)}) collective-permute-start(bf16[320,640]{1,0:T(8,128)(2,1)} %square.1.refs_0_), channel_id=1, source_target_pairs={{0,2},{1,3},{2,0},{3,1},{4,6},{5,7},{6,4},{7,5},{8,10},{9,11},{10,... | collective-permute-start | bytes 1228808 | tf_op jit(solution)/shard_map/ppermute | solution.py:51
  209.7 20.2 %collective-permute-start.42 = (bf16[320,640]{1,0:T(8,128)(2,1)}, bf16[320,640]{1,0:T(8,128)(2,1)S(1)}, u32[]{:S(2)}, u32[]{:S(2)}) collective-permute-start(bf16[320,640]{1,0:T(8,128)(2,1)} %square.1.refs_0_), channel_id=1, source_target_pairs={{0,12},{1,13},{2,14},{3,15},{4,0},{5,1},{6,2},{7,3},{8,4},{9,5},{1... | collective-permute-start | bytes 1228808 | tf_op jit(solution)/shard_map/ppermute | solution.py:51
  212.1 19.0 %collective-permute-start.41 = (bf16[320,640]{1,0:T(8,128)(2,1)}, bf16[320,640]{1,0:T(8,128)(2,1)S(1)}, u32[]{:S(2)}, u32[]{:S(2)}) collective-permute-start(bf16[320,640]{1,0:T(8,128)(2,1)} %square.1.refs_0_), channel_id=1, source_target_pairs={{0,4},{1,5},{2,6},{3,7},{4,8},{5,9},{6,10},{7,11},{8,12},{9,13},{1... | collective-permute-start | bytes 1228808 | tf_op jit(solution)/shard_map/ppermute | solution.py:51
  (62 other events, 763.2 us)

commit v3 on v2

--- a/solution.py
+++ b/solution.py
@@ -235,20 +235,22 @@
 
 
 def square_kernel(*refs):
-    grid_refs, dp_refs = refs[:8], refs[8:16]
-    out_ref, lhs, rhs, acc, lhs_sems, rhs_sems = refs[20:]
-    core = place()[4]
-    dp_refs += tuple(refs[16].at[n] for n in range(5)) + refs[17:20]
+    grid_refs, dp_refs = refs[:8], refs[8:12]
+    out_ref, lhs, rhs, acc, lhs_sems, rhs_sems = refs[12:]
+    yh, _, z, yl, core = place()
+    places = [((yl + n // 4 + yh) % 2) * 4 + (z + n % 4) % 4 for n in range(8)]
     copies = []
     for n, piece in enumerate(grid_refs):
         copies.append(
-            pltpu.make_async_copy(piece, lhs.at[:, rows_of(piece_place(n), ROWS)], lhs_sems.at[n])
+            pltpu.make_async_copy(piece, lhs.at[:, rows_of(places[n], ROWS)], lhs_sems.at[n])
         )
-    for n, piece in enumerate(dp_refs):
+    for n in range(16):
         side = core if n < 8 else 1 - core
         copies.append(
             pltpu.make_async_copy(
-                piece, rhs.at[rows_of(n % 8 * 2 + side, HALF), :], rhs_sems.at[n]
+                dp_refs[n // 4].at[n % 4],
+                rhs.at[rows_of(n % 8 * 2 + side, HALF), :],
+                rhs_sems.at[n],
             )
         )
     for copy in copies:
@@ -264,14 +266,14 @@
             acc[...] += term
         else:
             acc[...] = term
-    out = cubic_coef * lhs[:, rows_of(piece_place(0), ROWS)].astype(jnp.float32)
+    out = cubic_coef * lhs[:, rows_of(places[0], ROWS)].astype(jnp.float32)
     out_ref[...] = (out + quintic_coef * acc[...]).astype(jnp.bfloat16)
 
 
 def square(over_grid, over_dp):
     return pl.pallas_call(
         square_kernel,
-        in_specs=[pl.BlockSpec(memory_space=pl.ANY)] * 20,
+        in_specs=[pl.BlockSpec(memory_space=pl.ANY)] * 12,
         out_specs=pl.BlockSpec(memory_space=pltpu.VMEM),
         out_shape=jax.ShapeDtypeStruct((HALF, ROWS), jnp.bfloat16),
         scratch_shapes=[
@@ -320,18 +322,19 @@
             acc[...] = term
     own = rhs[rows_of(core, HALF), :].astype(jnp.float32)
     out = (math.sqrt(QD) * (linear_coef * own + acc[...])).astype(jnp.bfloat16)
-    mine_ref[...] = out[:, :COLS]
+    mine_ref[rows_of(core, HALF), :] = out[:, :COLS]
     other_ref[...] = out[:, COLS:]
 
 
 def update_of(pieces, blocks, other_blocks):
     inside = pl.BlockSpec(memory_space=pltpu.VMEM)
-    out = jax.ShapeDtypeStruct((HALF, COLS), jnp.bfloat16)
+    mine = jax.ShapeDtypeStruct((ROWS, COLS), jnp.bfloat16)
+    other = jax.ShapeDtypeStruct((HALF, COLS), jnp.bfloat16)
     return pl.pallas_call(
         update_kernel,
         in_specs=[pl.BlockSpec(memory_space=pl.ANY)] * 24,
         out_specs=[inside, inside],
-        out_shape=[out, out],
+        out_shape=[mine, other],
         scratch_shapes=[
             pltpu.VMEM((HALF, D), jnp.bfloat16),
             pltpu.VMEM((D, 2 * COLS), jnp.bfloat16),
@@ -379,16 +382,12 @@
         (own, above, far, below),
         (own_other, above_other, far_other, below_other),
     )
+    far_partial, near = together((far_partial, near))
+    far_terms = lax.all_to_all(far_partial, "x", 0, 0, tiled=True)
     near1, near3 = move(near1, Z_UP), move(near3, Z_DOWN)
-    partial = gradient_partial(grad_query_t, inputs, yh)
-    across_below, across_above, across_far, across_other, near, near1, near2, near3, partial = (
-        together(
-            (across_below, across_above, across_far, across_other)
-            + (near, near1, near2, near3, partial)
-        )
-    )
-    far_partial, across_below = together((far_partial, across_below))
-    far_terms = lax.all_to_all(far_partial, "x", 0, 0, tiled=True)
+    across_below, across_above, across_far, across_other, near, near1, near2, near3 = together(
+        (across_below, across_above, across_far, across_other, near, near1, near2, near3)
+    )
 
     far_swapped = move(across_far, CORE)
     above_swapped = move(across_above, CORE)
@@ -412,47 +411,48 @@
     kept = jnp.where(same, near, other)
     rows = (kept + move(jnp.where(same, other, near).astype(bf16), Y_LO).astype(f32)).astype(bf16)
 
-    rows, far_terms = together((rows, far_terms))
-
+    rows, far_terms, grad_query_t = together((rows, far_terms, grad_query_t))
+
+    def along_x(piece):
+        return lax.all_to_all(jnp.broadcast_to(piece, (4, HALF, ROWS)), "x", 0, 0, tiled=True)
+
+    lo, z_far = move(rows, Y_LO), move(rows, Z_FAR)
+    across_rows = move(rows, Y_HI)
+    here = along_x(rows)
+    partial = gradient_partial(grad_query_t, inputs, yh)
+    far_term = sum(far_terms[n].astype(f32) for n in range(4)).astype(bf16)
+    rows, lo, z_far, across_rows, here, partial, far_term = together(
+        (rows, lo, z_far, across_rows, here, partial, far_term)
+    )
     z_below, z_above = move(rows, Z_UP), move(rows, Z_DOWN)
-    x_below, x_above = move(rows, X_UP), move(rows, X_DOWN)
-    lo, x_across = move(rows, Y_LO), move(rows, Y_HI)
-    z_far, x_far = move(rows, Z_FAR), move(rows, X_FAR)
-    z_below, z_above, x_below, x_above, lo, x_across, z_far, x_far = together(
-        (z_below, z_above, x_below, x_above, lo, x_across, z_far, x_far)
-    )
     lo_below, lo_above, lo_far = move(lo, Z_UP), move(lo, Z_DOWN), move(z_far, Y_LO)
-    a_below, a_above, a_far = move(x_across, X_UP), move(x_across, X_DOWN), move(x_far, Y_HI)
-    first_other = move(jnp.stack([rows, x_above, x_far, x_below, x_across]), CORE)
-    lo_below, lo_above, lo_far, a_below, a_above, a_far = together(
-        (lo_below, lo_above, lo_far, a_below, a_above, a_far)
-    )
+    there = along_x(across_rows)
     partial, lo_below = together((partial, lo_below))
     terms = lax.all_to_all(partial, "x", 0, 0, tiled=True)
+    z_below, z_above, lo_below, lo_above, lo_far, there, here, far_term = together(
+        (z_below, z_above, lo_below, lo_above, lo_far, there, here, far_term)
+    )
     combined = square(
         (rows, z_above, z_far, z_below, lo, lo_above, lo_far, lo_below),
-        (rows, x_above, x_far, x_below, x_across, a_above, a_far, a_below)
-        + (first_other, move(a_above, CORE), move(a_far, CORE), move(a_below, CORE)),
+        (here, there, move(here, CORE), move(there, CORE)),
     )
 
     z_below, z_above = move(combined, Z_UP), move(combined, Z_DOWN)
     lo, z_far = move(combined, Y_LO), move(combined, Z_FAR)
-    far_term = move(sum(far_terms[n].astype(f32) for n in range(4)).astype(bf16), Y_HI)
+    far_term = move(far_term, Y_HI)
     z_below, z_above, lo, z_far, far_term = together((z_below, z_above, lo, z_far, far_term))
     lo_below, lo_above, lo_far = move(lo, Z_UP), move(lo, Z_DOWN), move(z_far, Y_LO)
-    lo_below, lo_above, lo_far = together((lo_below, lo_above, lo_far))
+    momentum_next = momentum_of(momentum, terms, far_term)
+    lo_below, lo_above, lo_far, momentum_next = together(
+        (lo_below, lo_above, lo_far, momentum_next)
+    )
     mine, theirs = update_of(
         (combined, z_above, z_far, z_below, lo, lo_above, lo_far, lo_below),
         (own, above, far, below, across, across_above, across_far, across_below),
         (own_other, above_other, far_other, below_other, across_other)
         + (above_swapped, far_swapped, below_swapped),
     )
-    momentum, theirs = together((momentum, theirs))
-    momentum_next = momentum_of(momentum, terms, far_term)
-    theirs = move(theirs, CORE)
-    update = jnp.where(
-        core == 0, jnp.concatenate([mine, theirs]), jnp.concatenate([theirs, mine])
-    )
+    update = lax.dynamic_update_slice(mine, move(theirs, CORE), ((1 - core) * HALF, 0))
     return (momentum_next, update)
 
 

time: 270 us -> 255 us (0.944)
  waiting for transfers between devices: 103 us -> 81.6 us
  starting transfers between devices: 75.7 us -> 83.4 us
    ppermute x50 -> x42, waiting for transfers between devices: 103 us -> 77.6 us  [move(): return lax.ppermute(array, ('y_hi', 'x', 'grid'), perm)]
    all_to_all x0 -> x2, starting transfers between devices: none -> 7.15 us  [along_x(): lax.all_to_all(jnp.broadcast_to(piece, (4, HALF, ROWS)), 'x', 0, 0, tiled...]
    all_to_all x0 -> x2, waiting for transfers between devices: none -> 4.07 us  [along_x(): lax.all_to_all(jnp.broadcast_to(piece, (4, HALF, ROWS)), 'x', 0, 0, tiled...]
    broadcast_in_dim x0 -> x2, local copies, waits for them, and re-layouts: none -> 2.74 us  [along_x(): jnp.broadcast_to(piece, (4, HALF, ROWS))]
    unnamed x73 -> x55, local copies, waits for them, and re-layouts: 7.24 us -> 4.75 us
    ppermute x50 -> x42, starting transfers between devices: 66.1 us -> 66.5 us  [move(): return lax.ppermute(array, ('y_hi', 'x', 'grid'), perm)]
  transfers between devices with their start and end apart: 52 -> 46, of which waited for: 28 -> 27; matrix products, arithmetic and copies ran while one was open for 3% -> 3% of each run, Pallas kernels for 25% -> 24%
where the time goes in v3:
time: 255 us
  starting transfers between devices  83.4 us (33%)
  waiting for transfers between devices  81.6 us (32%)
  Pallas kernels  73.3 us (29%)
  local copies, waits for them, and re-layouts  9.96 us (4%)
  other arithmetic  5.5 us (2%)
    ppermute x42, waiting for transfers between devices, move(): return lax.ppermute(array, ('y_hi', 'x', 'grid'), perm)  77.6 us
    ppermute x42, starting transfers between devices, move(): return lax.ppermute(array, ('y_hi', 'x', 'grid'), perm)  66.5 us
    pallas_call x2, Pallas kernels, gradient_partial(): pl.pallas_call(gradient_kernel, grid_spec=pltpu.PrefetchScalarGridSpec(nu...  17.4 us
    pallas_call x1, Pallas kernels, attention(): pl.pallas_call(body, grid_spec=pltpu.PrefetchScalarGridSpec(num_scalar_pr...  14.3 us
    pallas_call x2, Pallas kernels, gram_partial(): pl.pallas_call(gram_kernel, in_specs=[pl.BlockSpec(memory_space=pl.ANY)]...  14.2 us
    pallas_call x1, Pallas kernels, update_of(): pl.pallas_call(update_kernel, in_specs=[pl.BlockSpec(memory_space=pl.ANY)...  12.6 us
    pallas_call x1, Pallas kernels, square(): pl.pallas_call(square_kernel, in_specs=[pl.BlockSpec(memory_space=pl.ANY)...  8.9 us
    all_to_all x2, starting transfers between devices, along_x(): lax.all_to_all(jnp.broadcast_to(piece, (4, HALF, ROWS)), 'x', 0, 0, tiled...  7.15 us
  transfers between devices with their start and end apart: 46, of which 27 were waited for; matrix products, arithmetic and copies ran while one was open for 3% of the time, Pallas kernels for 24%

profile of v3, /device:TPU:1, one launch (start us, length us, event | category | flops | bytes accessed | tf_op | source)
XLA Modules:
  0.0 254.7 jit_solution(12232129566282249579)
XLA Ops:
  7.6 14.3 %attention.1.gq_ref = bf16[768,1024]{1,0:T(8,128)(2,1)} custom-call(s32[1]{0:T(128)} %bitcast.kv, bf16[1024,768]{1,0:T(8,128)(2,1)} %refs_0_.2, bf16[1024,1024]{1,0:T(8,128)(2,1)} %refs_1_.1, bf16[1024,1024]{1,0:T(8,128)(2,1)} %refs_2_.1, bf16[1024,768]{1,0:T(8,128)(2,1)} %refs_3_.1, bf16[1024,768]{1,0:T(8,128)(2,1)} %refs_4_.1), custom_call_target="tpu_custom_call" | custom-call | flops 24000000000 | bytes 8000000 | tf_op jit(solution)/shard_map/attention/pallas_call | solution.py:113
  21.9 5.4 %collective-permute-done.2.refs_0_.refs_12_ = bf16[640,768]{1,0:T(8,128)(2,1)} collective-permute-done((bf16[640,768]{1,0:T(8,128)(2,1)}, bf16[640,768]{1,0:T(8,128)(2,1)}, u32[]{:S(2)}, u32[]{:S(2)}) %collective-permute-start.2) | collective-permute-done | bytes 983072 | tf_op jit(solution)/shard_map/ppermute | solution.py:51
  37.5 8.7 %gradient.2 = bf16[4,768,640]{2,1,0:T(8,128)(2,1)} custom-call(s32[1]{0:T(128)} %bitcast.1.block_ref, bf16[768,1024]{1,0:T(8,128)(2,1)} %attention.1.gq_ref, bf16[1024,5120]{1,0:T(8,128)(2,1)} %in_ref.3), custom_call_target="tpu_custom_call" | custom-call | flops 8053063680 | bytes 12000000 | tf_op jit(solution)/shard_map/gradient/pallas_call | solution.py:133
  53.9 7.1 %gram.2 = (f32[320,640]{1,0:T(8,128)}, bf16[320,640]{1,0:T(8,128)(2,1)}, bf16[320,640]{1,0:T(8,128)(2,1)}, bf16[320,640]{1,0:T(8,128)(2,1)}) custom-call(bf16[640,768]{1,0:T(8,128)(2,1)} %refs_8_.5, bf16[640,768]{1,0:T(8,128)(2,1)} %copy-done.1, bf16[640,768]{1,0:T(8,128)(2,1)} %copy-done.3, bf16[640,768]{1,0:T(8,128)(2,1)} %copy-done.2, ...), custom_call_target="tpu_custom_call" | custom-call | flops 1 | bytes 1 | tf_op jit(solution)/shard_map/gram/pallas_call | solution.py:206
  61.0 5.0 %all-to-all-start = ((bf16[4,768,640]{2,1,0:T(8,128)(2,1)}), bf16[4,768,640]{2,1,0:T(8,128)(2,1)}, u32[]{:S(2)}, u32[]{:S(2)}) async-start(bf16[4,768,640]{2,1,0:T(8,128)(2,1)} %gradient.2), calls=%async_computation | async-start | bytes 7864320 | tf_op jit(solution)/shard_map/all_to_all | solution.py:386
  69.9 4.0 %collective-permute-done.6.refs_1_.refs_13_ = bf16[640,768]{1,0:T(8,128)(2,1)} collective-permute-done((bf16[640,768]{1,0:T(8,128)(2,1)}, bf16[640,768]{1,0:T(8,128)(2,1)}, u32[]{:S(2)}, u32[]{:S(2)}) %collective-permute-start.6) | collective-permute-done | bytes 983072 | tf_op jit(solution)/shard_map/ppermute | solution.py:51
  86.5 7.1 %gram.3 = (f32[320,640]{1,0:T(8,128)}, bf16[320,640]{1,0:T(8,128)(2,1)}, bf16[320,640]{1,0:T(8,128)(2,1)}, bf16[320,640]{1,0:T(8,128)(2,1)}) custom-call(bf16[640,768]{1,0:T(8,128)(2,1)} %collective-permute-done.2.refs_0_.refs_12_, bf16[640,768]{1,0:T(8,128)(2,1)} %collective-permute-done.6.refs_1_.refs_13_, ...), custom_call_target="tpu_custom_call" | custom-call | flops 1 | bytes 1 | tf_op jit(solution)/shard_map/gram/pallas_call | solution.py:206
  100.3 6.0 %collective-permute-done.19 = bf16[320,640]{1,0:T(8,128)(2,1)S(1)} collective-permute-done((bf16[320,640]{1,0:T(8,128)(2,1)}, bf16[320,640]{1,0:T(8,128)(2,1)S(1)}, u32[]{:S(2)}, u32[]{:S(2)}) %collective-permute-start.19) | collective-permute-done | bytes 409632 | tf_op jit(solution)/shard_map/ppermute | solution.py:51
  106.3 9.6 %collective-permute-done.20 = bf16[320,640]{1,0:T(8,128)(2,1)S(1)} collective-permute-done((bf16[320,640]{1,0:T(8,128)(2,1)}, bf16[320,640]{1,0:T(8,128)(2,1)S(1)}, u32[]{:S(2)}, u32[]{:S(2)}) %collective-permute-start.20) | collective-permute-done | bytes 409632 | tf_op jit(solution)/shard_map/ppermute | solution.py:51
  117.0 8.6 %collective-permute-done.22 = bf16[320,640]{1,0:T(8,128)(2,1)S(1)} collective-permute-done((bf16[320,640]{1,0:T(8,128)(2,1)S(1)}, bf16[320,640]{1,0:T(8,128)(2,1)S(1)}, u32[]{:S(2)}, u32[]{:S(2)}) %collective-permute-start.22) | collective-permute-done | bytes 409632 | tf_op jit(solution)/shard_map/ppermute | solution.py:51
  127.2 3.6 %all-to-all-start.1 = ((bf16[4,320,640]{2,1,0:T(8,128)(2,1)}), bf16[4,320,640]{2,1,0:T(8,128)(2,1)S(1)}, u32[]{:S(2)}, u32[]{:S(2)}) async-start(bf16[4,320,640]{2,1,0:T(8,128)(2,1)} %broadcast_in_dim.6), calls=%async_computation.1 | async-start | bytes 3276800 | tf_op jit(solution)/shard_map/all_to_all | solution.py:417
  135.5 8.7 %gradient.3 = bf16[4,768,640]{2,1,0:T(8,128)(2,1)} custom-call(s32[1]{0:T(128)} %bitcast.2.block_ref, bf16[768,1024]{1,0:T(8,128)(2,1)} %attention.1.gq_ref, bf16[1024,5120]{1,0:T(8,128)(2,1)} %in_ref.3), custom_call_target="tpu_custom_call" | custom-call | flops 8053063680 | bytes 12000000 | tf_op jit(solution)/shard_map/gradient/pallas_call | solution.py:133
  144.2 3.5 %fusion = bf16[768,640]{1,0:T(8,128)(2,1)} fusion(bf16[4,768,640]{2,1,0:T(8,128)(2,1)} %all-to-all-done), kind=kLoop, calls=%fused_computation.1 | loop fusion | flops 3932160 | bytes 4915200 | tf_op jit(solution)/shard_map/add | solution.py:423
  151.0 3.6 %all-to-all-start.2 = ((bf16[4,320,640]{2,1,0:T(8,128)(2,1)}), bf16[4,320,640]{2,1,0:T(8,128)(2,1)S(1)}, u32[]{:S(2)}, u32[]{:S(2)}) async-start(bf16[4,320,640]{2,1,0:T(8,128)(2,1)} %broadcast_in_dim.7), calls=%async_computation.2 | async-start | bytes 3276800 | tf_op jit(solution)/shard_map/all_to_all | solution.py:417
  154.6 3.6 %collective-permute-start.28 = (bf16[320,640]{1,0:T(8,128)(2,1)}, bf16[320,640]{1,0:T(8,128)(2,1)}, u32[]{:S(2)}, u32[]{:S(2)}) collective-permute-start(bf16[320,640]{1,0:T(8,128)(2,1)} %copy-done.24), channel_id=1, source_target_pairs={{0,4},{1,5},{2,6},{3,7},{4,8},{5,9},{6,10},{7,11},{8,12},{9,13},{1... | collective-permute-start | bytes 1228808 | tf_op jit(solution)/shard_map/ppermute | solution.py:51
  167.6 3.7 %all-to-all-done.2.refs_9_ = bf16[4,320,640]{2,1,0:T(8,128)(2,1)S(1)} async-done(((bf16[4,320,640]{2,1,0:T(8,128)(2,1)}), bf16[4,320,640]{2,1,0:T(8,128)(2,1)S(1)}, u32[]{:S(2)}, u32[]{:S(2)}) %all-to-all-start.2) | async-done | bytes 1638432 | tf_op jit(solution)/shard_map/all_to_all | solution.py:417
  171.3 4.8 %all-to-all-start.3 = ((bf16[4,768,640]{2,1,0:T(8,128)(2,1)}), bf16[4,768,640]{2,1,0:T(8,128)(2,1)}, u32[]{:S(2)}, u32[]{:S(2)}) async-start(bf16[4,768,640]{2,1,0:T(8,128)(2,1)} %gradient.3), calls=%async_computation.3 | async-start | bytes 7864320 | tf_op jit(solution)/shard_map/all_to_all | solution.py:431
  176.4 5.5 %collective-permute-start.31 = (bf16[4,320,640]{2,1,0:T(8,128)(2,1)S(1)}, bf16[4,320,640]{2,1,0:T(8,128)(2,1)S(1)}, u32[]{:S(2)}, u32[]{:S(2)}) collective-permute-start(bf16[4,320,640]{2,1,0:T(8,128)(2,1)S(1)} %all-to-all-done.1.refs_8_), channel_id=1, source_target_pairs={{0,1},{1,0},{2,3},{3,2},{4,5},{5,4},{6,7},{7,6},{8,9},{9,8},{10,11... | collective-permute-start | bytes 4915208 | tf_op jit(solution)/shard_map/ppermute | solution.py:51
  187.6 8.9 %square.1.refs_0_ = bf16[320,640]{1,0:T(8,128)(2,1)} custom-call(bf16[320,640]{1,0:T(8,128)(2,1)} %copy-done.11, bf16[320,640]{1,0:T(8,128)(2,1)} %collective-permute-done.27.refs_1_, bf16[320,640]{1,0:T(8,128)(2,1)} %copy-done.23, bf16[320,640]{1,0:T(8,128)(2,1)} %collective-permute-done.26.refs_3_, bf16[320,640]{1,0:T(8,128)(2,1)} %copy-done.24, ...), custom_call_target="tpu_custom_call" | custom-call | flops 4194304000 | bytes 11000000 | tf_op jit(solution)/shard_map/square/pallas_call | solution.py:274
  199.2 4.5 %collective-permute-start.34 = (bf16[320,640]{1,0:T(8,128)(2,1)}, bf16[320,640]{1,0:T(8,128)(2,1)S(1)}, u32[]{:S(2)}, u32[]{:S(2)}) collective-permute-start(bf16[320,640]{1,0:T(8,128)(2,1)} %square.1.refs_0_), channel_id=1, source_target_pairs={{0,12},{1,13},{2,14},{3,15},{4,0},{5,1},{6,2},{7,3},{8,4},{9,5},{1... | collective-permute-start | bytes 1228808 | tf_op jit(solution)/shard_map/ppermute | solution.py:51
  209.1 6.2 %collective-permute-done.35.refs_4_ = bf16[320,640]{1,0:T(8,128)(2,1)S(1)} collective-permute-done((bf16[320,640]{1,0:T(8,128)(2,1)}, bf16[320,640]{1,0:T(8,128)(2,1)S(1)}, u32[]{:S(2)}, u32[]{:S(2)}) %collective-permute-start.35) | collective-permute-done | bytes 409632 | tf_op jit(solution)/shard_map/ppermute | solution.py:51
  215.3 6.2 %collective-permute-done.34.refs_1_ = bf16[320,640]{1,0:T(8,128)(2,1)S(1)} collective-permute-done((bf16[320,640]{1,0:T(8,128)(2,1)}, bf16[320,640]{1,0:T(8,128)(2,1)S(1)}, u32[]{:S(2)}, u32[]{:S(2)}) %collective-permute-start.34) | collective-permute-done | bytes 409632 | tf_op jit(solution)/shard_map/ppermute | solution.py:51
  225.7 6.0 %momentum.1 = f32[640,768]{1,0:T(8,128)} custom-call(f32[640,768]{1,0:T(8,128)} %m_ref.1, bf16[4,768,640]{2,1,0:T(8,128)(2,1)} %all-to-all-done.3.g_ref, bf16[768,640]{1,0:T(8,128)(2,1)} %collective-permute-done.37.h_ref), custom_call_target="tpu_custom_call" | custom-call | flops 4423680 | bytes 9000000 | tf_op jit(solution)/shard_map/momentum/pallas_call | solution.py:160
  237.7 12.6 %update.1 = (bf16[640,768]{1,0:T(8,128)(2,1)}, bf16[320,768]{1,0:T(8,128)(2,1)}) custom-call(bf16[320,640]{1,0:T(8,128)(2,1)} %square.1.refs_0_, bf16[320,640]{1,0:T(8,128)(2,1)} %copy-done.15, bf16[320,640]{1,0:T(8,128)(2,1)} %copy-done.13, bf16[320,640]{1,0:T(8,128)(2,1)} %copy-done.16, bf16[320,640]{1,0:T(8,128)(2,1)} %copy-done.14, ...), custom_call_target="tpu_custom_call" | custom-call | flops 1 | bytes 1 | tf_op jit(solution)/shard_map/update/pallas_call | solution.py:333
  (141 shorter events, 96.7 us)
Async XLA Ops:
  0.6 47.9 %collective-permute-start.7 = (bf16[640,768]{1,0:T(8,128)(2,1)}, bf16[640,768]{1,0:T(8,128)(2,1)S(1)}, u32[]{:S(2)}, u32[]{:S(2)}) collective-permute-start(bf16[640,768]{1,0:T(8,128)(2,1)} %refs_8_.5), channel_id=1, source_target_pairs={{0,1},{1,0},{2,3},{3,2},{4,5},{5,4},{6,7},{7,6},{8,9},{9,8},{10,11... | collective-permute-start | bytes 2949128 | tf_op jit(solution)/shard_map/ppermute | solution.py:51
  2.1 25.2 %collective-permute-start.2 = (bf16[640,768]{1,0:T(8,128)(2,1)}, bf16[640,768]{1,0:T(8,128)(2,1)}, u32[]{:S(2)}, u32[]{:S(2)}) collective-permute-start(bf16[640,768]{1,0:T(8,128)(2,1)} %refs_8_.5), channel_id=1, source_target_pairs={{0,64},{1,65},{2,66},{3,67},{4,68},{5,69},{6,70},{7,71},{8,72},{9,... | collective-permute-start | bytes 2949128 | tf_op jit(solution)/shard_map/ppermute | solution.py:51
  5.1 23.6 %collective-permute-start.1 = (bf16[640,768]{1,0:T(8,128)(2,1)}, bf16[640,768]{1,0:T(8,128)(2,1)S(1)}, u32[]{:S(2)}, u32[]{:S(2)}) collective-permute-start(bf16[640,768]{1,0:T(8,128)(2,1)} %refs_8_.5), channel_id=1, source_target_pairs={{0,48},{1,49},{2,50},{3,51},{4,52},{5,53},{6,54},{7,55},{8,56},{9,... | collective-permute-start | bytes 2949128 | tf_op jit(solution)/shard_map/ppermute | solution.py:51
  7.6 24.1 %collective-permute-start = (bf16[640,768]{1,0:T(8,128)(2,1)}, bf16[640,768]{1,0:T(8,128)(2,1)S(1)}, u32[]{:S(2)}, u32[]{:S(2)}) collective-permute-start(bf16[640,768]{1,0:T(8,128)(2,1)} %refs_8_.5), channel_id=1, source_target_pairs={{0,16},{1,17},{2,18},{3,19},{4,20},{5,21},{6,22},{7,23},{8,24},{9,... | collective-permute-start | bytes 2949128 | tf_op jit(solution)/shard_map/ppermute | solution.py:51
  31.7 16.8 %collective-permute-start.8 = (bf16[640,768]{1,0:T(8,128)(2,1)S(1)}, bf16[640,768]{1,0:T(8,128)(2,1)}, u32[]{:S(2)}, u32[]{:S(2)}) collective-permute-start(bf16[640,768]{1,0:T(8,128)(2,1)S(1)} %collective-permute-done.1.refs_1_.refs_9_), channel_id=1, source_target_pairs={{0,1},{1,0},{2,3},{3,2},{4,5},{5,4},{6,7},{7,6},{8,9},{9,8},{10,11... | collective-permute-start | bytes 2949128 | tf_op jit(solution)/shard_map/ppermute | solution.py:51
  33.2 15.3 %collective-permute-start.9 = (bf16[640,768]{1,0:T(8,128)(2,1)S(1)}, bf16[640,768]{1,0:T(8,128)(2,1)}, u32[]{:S(2)}, u32[]{:S(2)}) collective-permute-start(bf16[640,768]{1,0:T(8,128)(2,1)S(1)} %collective-permute-done.refs_3_.refs_11_), channel_id=1, source_target_pairs={{0,1},{1,0},{2,3},{3,2},{4,5},{5,4},{6,7},{7,6},{8,9},{9,8},{10,11... | collective-permute-start | bytes 2949128 | tf_op jit(solution)/shard_map/ppermute | solution.py:51
  50.1 17.6 %collective-permute-start.11 = (bf16[640,768]{1,0:T(8,128)(2,1)}, bf16[640,768]{1,0:T(8,128)(2,1)}, u32[]{:S(2)}, u32[]{:S(2)}) collective-permute-start(bf16[640,768]{1,0:T(8,128)(2,1)} %collective-permute-done.2.refs_0_.refs_12_), channel_id=1, source_target_pairs={{0,1},{1,0},{2,3},{3,2},{4,5},{5,4},{6,7},{7,6},{8,9},{9,8},{10,11... | collective-permute-start | bytes 2949128 | tf_op jit(solution)/shard_map/ppermute | solution.py:51
  50.2 23.7 %collective-permute-start.6 = (bf16[640,768]{1,0:T(8,128)(2,1)}, bf16[640,768]{1,0:T(8,128)(2,1)}, u32[]{:S(2)}, u32[]{:S(2)}) collective-permute-start(bf16[640,768]{1,0:T(8,128)(2,1)} %collective-permute-done.2.refs_0_.refs_12_), channel_id=1, source_target_pairs={{0,48},{1,49},{2,50},{3,51},{4,52},{5,53},{6,54},{7,55},{8,56},{9,... | collective-permute-start | bytes 2949128 | tf_op jit(solution)/shard_map/ppermute | solution.py:51
  52.9 24.1 %collective-permute-start.5 = (bf16[640,768]{1,0:T(8,128)(2,1)}, bf16[640,768]{1,0:T(8,128)(2,1)}, u32[]{:S(2)}, u32[]{:S(2)}) collective-permute-start(bf16[640,768]{1,0:T(8,128)(2,1)} %collective-permute-done.2.refs_0_.refs_12_), channel_id=1, source_target_pairs={{0,16},{1,17},{2,18},{3,19},{4,20},{5,21},{6,22},{7,23},{8,24},{9,... | collective-permute-start | bytes 2949128 | tf_op jit(solution)/shard_map/ppermute | solution.py:51
  52.9 24.2 %collective-permute-start.10 = (bf16[640,768]{1,0:T(8,128)(2,1)S(1)}, bf16[640,768]{1,0:T(8,128)(2,1)}, u32[]{:S(2)}, u32[]{:S(2)}) collective-permute-start(bf16[640,768]{1,0:T(8,128)(2,1)S(1)} %constant_dynamic-update-slice_fusion.refs_2_.refs_10_), channel_id=1, source_target_pairs={{0,64},{1,65},{2,66},{3,67},{4,68},{5,69},{6,70},{7,71},{8,72},{9,... | collective-permute-start | bytes 2949128 | tf_op jit(solution)/shard_map/ppermute | solution.py:51
  61.0 64.9 %all-to-all-start = ((bf16[4,768,640]{2,1,0:T(8,128)(2,1)}), bf16[4,768,640]{2,1,0:T(8,128)(2,1)}, u32[]{:S(2)}, u32[]{:S(2)}) async-start(bf16[4,768,640]{2,1,0:T(8,128)(2,1)} %gradient.2), calls=%async_computation | async-start | bytes 7864320 | tf_op jit(solution)/shard_map/all_to_all | solution.py:386
  94.9 21.1 %collective-permute-start.20 = (bf16[320,640]{1,0:T(8,128)(2,1)}, bf16[320,640]{1,0:T(8,128)(2,1)S(1)}, u32[]{:S(2)}, u32[]{:S(2)}) collective-permute-start(bf16[320,640]{1,0:T(8,128)(2,1)} %get-tuple-element.108), channel_id=1, source_target_pairs={{0,8},{1,9},{2,10},{3,11},{4,12},{5,13},{6,14},{7,15},{8,0},{9,1},... | collective-permute-start | bytes 1228808 | tf_op jit(solution)/shard_map/ppermute | solution.py:51
  98.2 17.8 %collective-permute-start.21 = (bf16[320,640]{1,0:T(8,128)(2,1)}, bf16[320,640]{1,0:T(8,128)(2,1)S(1)}, u32[]{:S(2)}, u32[]{:S(2)}) collective-permute-start(bf16[320,640]{1,0:T(8,128)(2,1)} %get-tuple-element.109), channel_id=1, source_target_pairs={{0,12},{1,13},{2,14},{3,15},{4,0},{5,1},{6,2},{7,3},{8,4},{9,5},{1... | collective-permute-start | bytes 1228808 | tf_op jit(solution)/shard_map/ppermute | solution.py:51
  127.2 22.3 %all-to-all-start.1 = ((bf16[4,320,640]{2,1,0:T(8,128)(2,1)}), bf16[4,320,640]{2,1,0:T(8,128)(2,1)S(1)}, u32[]{:S(2)}, u32[]{:S(2)}) async-start(bf16[4,320,640]{2,1,0:T(8,128)(2,1)} %broadcast_in_dim.6), calls=%async_computation.1 | async-start | bytes 3276800 | tf_op jit(solution)/shard_map/all_to_all | solution.py:417
  130.8 16.9 %collective-permute-start.25 = (bf16[320,640]{1,0:T(8,128)(2,1)S(1)}, bf16[320,640]{1,0:T(8,128)(2,1)S(1)}, u32[]{:S(2)}, u32[]{:S(2)}) collective-permute-start(bf16[320,640]{1,0:T(8,128)(2,1)S(1)} %add_convert_fusion.1.refs_0_), channel_id=1, source_target_pairs={{0,64},{1,65},{2,66},{3,67},{4,68},{5,69},{6,70},{7,71},{8,72},{9,... | collective-permute-start | bytes 1228808 | tf_op jit(solution)/shard_map/ppermute | solution.py:51
  151.0 20.3 %all-to-all-start.2 = ((bf16[4,320,640]{2,1,0:T(8,128)(2,1)}), bf16[4,320,640]{2,1,0:T(8,128)(2,1)S(1)}, u32[]{:S(2)}, u32[]{:S(2)}) async-start(bf16[4,320,640]{2,1,0:T(8,128)(2,1)} %broadcast_in_dim.7), calls=%async_computation.2 | async-start | bytes 3276800 | tf_op jit(solution)/shard_map/all_to_all | solution.py:417
  158.2 17.9 %collective-permute-start.30 = (bf16[320,640]{1,0:T(8,128)(2,1)}, bf16[320,640]{1,0:T(8,128)(2,1)}, u32[]{:S(2)}, u32[]{:S(2)}) collective-permute-start(bf16[320,640]{1,0:T(8,128)(2,1)} %copy-done.23), channel_id=1, source_target_pairs={{0,2},{1,3},{2,0},{3,1},{4,6},{5,7},{6,4},{7,5},{8,10},{9,11},{10,... | collective-permute-start | bytes 1228808 | tf_op jit(solution)/shard_map/ppermute | solution.py:51
  159.0 17.1 %collective-permute-start.27 = (bf16[320,640]{1,0:T(8,128)(2,1)}, bf16[320,640]{1,0:T(8,128)(2,1)}, u32[]{:S(2)}, u32[]{:S(2)}) collective-permute-start(bf16[320,640]{1,0:T(8,128)(2,1)} %copy-done.11), channel_id=1, source_target_pairs={{0,12},{1,13},{2,14},{3,15},{4,0},{5,1},{6,2},{7,3},{8,4},{9,5},{1... | collective-permute-start | bytes 1228808 | tf_op jit(solution)/shard_map/ppermute | solution.py:51
  161.6 14.8 %collective-permute-start.26 = (bf16[320,640]{1,0:T(8,128)(2,1)}, bf16[320,640]{1,0:T(8,128)(2,1)}, u32[]{:S(2)}, u32[]{:S(2)}) collective-permute-start(bf16[320,640]{1,0:T(8,128)(2,1)} %copy-done.11), channel_id=1, source_target_pairs={{0,4},{1,5},{2,6},{3,7},{4,8},{5,9},{6,10},{7,11},{8,12},{9,13},{1... | collective-permute-start | bytes 1228808 | tf_op jit(solution)/shard_map/ppermute | solution.py:51
  171.3 54.4 %all-to-all-start.3 = ((bf16[4,768,640]{2,1,0:T(8,128)(2,1)}), bf16[4,768,640]{2,1,0:T(8,128)(2,1)}, u32[]{:S(2)}, u32[]{:S(2)}) async-start(bf16[4,768,640]{2,1,0:T(8,128)(2,1)} %gradient.3), calls=%async_computation.3 | async-start | bytes 7864320 | tf_op jit(solution)/shard_map/all_to_all | solution.py:431
  182.0 24.7 %collective-permute-start.37 = (bf16[768,640]{1,0:T(8,128)(2,1)}, bf16[768,640]{1,0:T(8,128)(2,1)}, u32[]{:S(2)}, u32[]{:S(2)}) collective-permute-start(bf16[768,640]{1,0:T(8,128)(2,1)} %fusion), channel_id=1, source_target_pairs={{0,64},{1,65},{2,66},{3,67},{4,68},{5,69},{6,70},{7,71},{8,72},{9,... | collective-permute-start | bytes 2949128 | tf_op jit(solution)/shard_map/ppermute | solution.py:51
  198.6 16.7 %collective-permute-start.35 = (bf16[320,640]{1,0:T(8,128)(2,1)}, bf16[320,640]{1,0:T(8,128)(2,1)S(1)}, u32[]{:S(2)}, u32[]{:S(2)}) collective-permute-start(bf16[320,640]{1,0:T(8,128)(2,1)} %square.1.refs_0_), channel_id=1, source_target_pairs={{0,2},{1,3},{2,0},{3,1},{4,6},{5,7},{6,4},{7,5},{8,10},{9,11},{10,... | collective-permute-start | bytes 1228808 | tf_op jit(solution)/shard_map/ppermute | solution.py:51
  199.2 22.3 %collective-permute-start.34 = (bf16[320,640]{1,0:T(8,128)(2,1)}, bf16[320,640]{1,0:T(8,128)(2,1)S(1)}, u32[]{:S(2)}, u32[]{:S(2)}) collective-permute-start(bf16[320,640]{1,0:T(8,128)(2,1)} %square.1.refs_0_), channel_id=1, source_target_pairs={{0,12},{1,13},{2,14},{3,15},{4,0},{5,1},{6,2},{7,3},{8,4},{9,5},{1... | collective-permute-start | bytes 1228808 | tf_op jit(solution)/shard_map/ppermute | solution.py:51
  203.7 17.8 %collective-permute-start.33 = (bf16[320,640]{1,0:T(8,128)(2,1)}, bf16[320,640]{1,0:T(8,128)(2,1)S(1)}, u32[]{:S(2)}, u32[]{:S(2)}) collective-permute-start(bf16[320,640]{1,0:T(8,128)(2,1)} %square.1.refs_0_), channel_id=1, source_target_pairs={{0,4},{1,5},{2,6},{3,7},{4,8},{5,9},{6,10},{7,11},{8,12},{9,13},{1... | collective-permute-start | bytes 1228808 | tf_op jit(solution)/shard_map/ppermute | solution.py:51
  (49 other events, 454.6 us)

commit v4 on v3

--- a/solution.py
+++ b/solution.py
@@ -175,27 +175,33 @@
 
 def gram_kernel(*refs):
     own, own_other = refs[8:10]
-    outs, (lhs, rhs, sems) = refs[10:14], refs[14:]
+    outs, (lhs, rhs, acc, sems) = refs[10:14], refs[14:]
     _, x, z, _, core = place()
-    copies = []
+    copies = ([], [])
+    for n, block in enumerate((own, own_other)):
+        source = block.at[rows_of(core, HALF), :]
+        copies[n].append(
+            pltpu.make_async_copy(source, lhs.at[:, n * COLS : (n + 1) * COLS], sems.at[8 + n])
+        )
     for n, block in enumerate(refs[:8]):
         slot = (x + n % 4 - z + 4) % 4
         side = slice(n // 4 * COLS, (n // 4 + 1) * COLS)
-        copies.append(pltpu.make_async_copy(block, rhs.at[rows_of(slot, ROWS), side], sems.at[n]))
-    for n, block in enumerate((own, own_other)):
-        copies.append(
-            pltpu.make_async_copy(
-                block.at[rows_of(core, HALF), :],
-                lhs.at[:, n * COLS : (n + 1) * COLS],
-                sems.at[8 + n],
-            )
+        copies[n // 4].append(
+            pltpu.make_async_copy(block, rhs.at[rows_of(slot, ROWS), side], sems.at[n])
         )
-    for copy in copies:
+    for copy in copies[0]:
         copy.start()
-    for copy in copies:
+    for copy in copies[0]:
         copy.wait()
-    for pair in range(2):
-        value = dot(lhs[...], rhs[pair * 2 * ROWS : (pair + 1) * 2 * ROWS, :], 1, 1)
+    for copy in copies[1]:
+        copy.start()
+    pairs = [slice(pair * 2 * ROWS, (pair + 1) * 2 * ROWS) for pair in range(2)]
+    for at in pairs:
+        acc[:, at] = dot(lhs[:, :COLS], rhs[at, :COLS], 1, 1)
+    for copy in copies[1]:
+        copy.wait()
+    for pair, at in enumerate(pairs):
+        value = acc[:, at] + dot(lhs[:, COLS:], rhs[at, COLS:], 1, 1)
         for n in range(2):
             out_ref = outs[pair * 2 + n]
             out_ref[...] = value[:, n * ROWS : (n + 1) * ROWS].astype(out_ref.dtype)
@@ -212,6 +218,7 @@
         scratch_shapes=[
             pltpu.VMEM((HALF, 2 * COLS), jnp.bfloat16),
             pltpu.VMEM((4 * ROWS, 2 * COLS), jnp.bfloat16),
+            pltpu.VMEM((HALF, 4 * ROWS), jnp.float32),
             pltpu.SemaphoreType.DMA((10,)),
         ],
         compiler_params=pltpu.CompilerParams(vmem_limit_bytes=VMEM),
@@ -253,13 +260,17 @@
                 rhs_sems.at[n],
             )
         )
-    for copy in copies:
+    chunks = [[copies[8 + n] for n in (2 * k, 2 * k + 1, 2 * k + 8, 2 * k + 9)] for k in range(4)]
+    for copy in copies[:8] + chunks[0]:
         copy.start()
     for copy in copies[:8]:
         copy.wait()
     for k in range(4):
-        for n in (2 * k, 2 * k + 1, 2 * k + 8, 2 * k + 9):
-            copies[8 + n].wait()
+        for copy in chunks[k]:
+            copy.wait()
+        if k < 3:
+            for copy in chunks[k + 1]:
+                copy.start()
         at = slice(k * 2 * ROWS, (k + 1) * 2 * ROWS)
         term = dot(lhs[:, at], rhs[at, :], 1, 0)
         if k:
@@ -307,13 +318,17 @@
                     rhs_sems.at[2 * n + side],
                 )
             )
-    for copy in copies:
+    chunks = [copies[8 + 4 * k : 12 + 4 * k] for k in range(4)]
+    for copy in copies[:8] + chunks[0]:
         copy.start()
     for copy in copies[:8]:
         copy.wait()
     for k in range(4):
-        for copy in copies[8 + 4 * k : 12 + 4 * k]:
+        for copy in chunks[k]:
             copy.wait()
+        if k < 3:
+            for copy in chunks[k + 1]:
+                copy.start()
         at = slice(k * 2 * ROWS, (k + 1) * 2 * ROWS)
         term = dot(lhs[:, at], rhs[at, :], 1, 0)
         if k:

time: 255 us -> 254 us (level)
  transfers between devices with their start and end apart: 46 -> 46, of which waited for: 27 -> 26; matrix products, arithmetic and copies ran while one was open for 3% -> 3% of each run, Pallas kernels for 24% -> 24%
where the time goes in v4:
time: 254 us; the launch traced here: 253 us
  waiting for transfers between devices  83.6 us (33%)
  starting transfers between devices  81.6 us (32%)
  Pallas kernels  71.7 us (28%)
  local copies, waits for them, and re-layouts  9.99 us (4%)
  other arithmetic  5.5 us (2%)
    ppermute x42, waiting for transfers between devices, move(): return lax.ppermute(array, ('y_hi', 'x', 'grid'), perm)  79.2 us
    ppermute x42, starting transfers between devices, move(): return lax.ppermute(array, ('y_hi', 'x', 'grid'), perm)  64.7 us
    pallas_call x2, Pallas kernels, gradient_partial(): pl.pallas_call(gradient_kernel, grid_spec=pltpu.PrefetchScalarGridSpec(nu...  17.4 us
    pallas_call x1, Pallas kernels, attention(): pl.pallas_call(body, grid_spec=pltpu.PrefetchScalarGridSpec(num_scalar_pr...  14.3 us
    pallas_call x2, Pallas kernels, gram_partial(): pl.pallas_call(gram_kernel, in_specs=[pl.BlockSpec(memory_space=pl.ANY)]...  13.6 us
    pallas_call x1, Pallas kernels, update_of(): pl.pallas_call(update_kernel, in_specs=[pl.BlockSpec(memory_space=pl.ANY)...  11.8 us
    pallas_call x1, Pallas kernels, square(): pl.pallas_call(square_kernel, in_specs=[pl.BlockSpec(memory_space=pl.ANY)...  8.57 us
    all_to_all x2, starting transfers between devices, along_x(): lax.all_to_all(jnp.broadcast_to(piece, (4, HALF, ROWS)), 'x', 0, 0, tiled...  7.14 us
  transfers between devices with their start and end apart: 46, of which 26 were waited for; matrix products, arithmetic and copies ran while one was open for 3% of the time, Pallas kernels for 24%

profile of v4, /device:TPU:1, one launch (start us, length us, event | category | flops | bytes accessed | tf_op | source)
XLA Modules:
  0.0 253.3 jit_solution(1271093821515046960)
XLA Ops:
  7.6 14.3 %attention.1.gq_ref = bf16[768,1024]{1,0:T(8,128)(2,1)} custom-call(s32[1]{0:T(128)} %bitcast.kv, bf16[1024,768]{1,0:T(8,128)(2,1)} %refs_0_.2, bf16[1024,1024]{1,0:T(8,128)(2,1)} %refs_1_.1, bf16[1024,1024]{1,0:T(8,128)(2,1)} %refs_2_.1, bf16[1024,768]{1,0:T(8,128)(2,1)} %refs_3_.1, bf16[1024,768]{1,0:T(8,128)(2,1)} %refs_4_.1), custom_call_target="tpu_custom_call" | custom-call | flops 24000000000 | bytes 8000000 | tf_op jit(solution)/shard_map/attention/pallas_call | solution.py:113
  21.9 5.4 %collective-permute-done.2.refs_0_.refs_12_ = bf16[640,768]{1,0:T(8,128)(2,1)} collective-permute-done((bf16[640,768]{1,0:T(8,128)(2,1)}, bf16[640,768]{1,0:T(8,128)(2,1)}, u32[]{:S(2)}, u32[]{:S(2)}) %collective-permute-start.2) | collective-permute-done | bytes 983072 | tf_op jit(solution)/shard_map/ppermute | solution.py:51
  37.5 8.7 %gradient.2 = bf16[4,768,640]{2,1,0:T(8,128)(2,1)} custom-call(s32[1]{0:T(128)} %bitcast.1.block_ref, bf16[768,1024]{1,0:T(8,128)(2,1)} %attention.1.gq_ref, bf16[1024,5120]{1,0:T(8,128)(2,1)} %in_ref.3), custom_call_target="tpu_custom_call" | custom-call | flops 8053063680 | bytes 12000000 | tf_op jit(solution)/shard_map/gradient/pallas_call | solution.py:133
  53.9 6.8 %gram.2 = (f32[320,640]{1,0:T(8,128)}, bf16[320,640]{1,0:T(8,128)(2,1)}, bf16[320,640]{1,0:T(8,128)(2,1)}, bf16[320,640]{1,0:T(8,128)(2,1)}) custom-call(bf16[640,768]{1,0:T(8,128)(2,1)} %refs_8_.5, bf16[640,768]{1,0:T(8,128)(2,1)} %copy-done.1, bf16[640,768]{1,0:T(8,128)(2,1)} %copy-done.3, bf16[640,768]{1,0:T(8,128)(2,1)} %copy-done.2, ...), custom_call_target="tpu_custom_call" | custom-call | flops 1 | bytes 1 | tf_op jit(solution)/shard_map/gram/pallas_call | solution.py:212
  60.7 5.0 %all-to-all-start = ((bf16[4,768,640]{2,1,0:T(8,128)(2,1)}), bf16[4,768,640]{2,1,0:T(8,128)(2,1)}, u32[]{:S(2)}, u32[]{:S(2)}) async-start(bf16[4,768,640]{2,1,0:T(8,128)(2,1)} %gradient.2), calls=%async_computation | async-start | bytes 7864320 | tf_op jit(solution)/shard_map/all_to_all | solution.py:401
  69.6 4.3 %collective-permute-done.6.refs_1_.refs_13_ = bf16[640,768]{1,0:T(8,128)(2,1)} collective-permute-done((bf16[640,768]{1,0:T(8,128)(2,1)}, bf16[640,768]{1,0:T(8,128)(2,1)}, u32[]{:S(2)}, u32[]{:S(2)}) %collective-permute-start.6) | collective-permute-done | bytes 983072 | tf_op jit(solution)/shard_map/ppermute | solution.py:51
  86.2 6.8 %gram.3 = (f32[320,640]{1,0:T(8,128)}, bf16[320,640]{1,0:T(8,128)(2,1)}, bf16[320,640]{1,0:T(8,128)(2,1)}, bf16[320,640]{1,0:T(8,128)(2,1)}) custom-call(bf16[640,768]{1,0:T(8,128)(2,1)} %collective-permute-done.2.refs_0_.refs_12_, bf16[640,768]{1,0:T(8,128)(2,1)} %collective-permute-done.6.refs_1_.refs_13_, ...), custom_call_target="tpu_custom_call" | custom-call | flops 1 | bytes 1 | tf_op jit(solution)/shard_map/gram/pallas_call | solution.py:212
  100.3 6.0 %collective-permute-done.19 = bf16[320,640]{1,0:T(8,128)(2,1)S(1)} collective-permute-done((bf16[320,640]{1,0:T(8,128)(2,1)}, bf16[320,640]{1,0:T(8,128)(2,1)S(1)}, u32[]{:S(2)}, u32[]{:S(2)}) %collective-permute-start.19) | collective-permute-done | bytes 409632 | tf_op jit(solution)/shard_map/ppermute | solution.py:51
  106.3 9.6 %collective-permute-done.20 = bf16[320,640]{1,0:T(8,128)(2,1)S(1)} collective-permute-done((bf16[320,640]{1,0:T(8,128)(2,1)}, bf16[320,640]{1,0:T(8,128)(2,1)S(1)}, u32[]{:S(2)}, u32[]{:S(2)}) %collective-permute-start.20) | collective-permute-done | bytes 409632 | tf_op jit(solution)/shard_map/ppermute | solution.py:51
  116.6 8.9 %collective-permute-done.22 = bf16[320,640]{1,0:T(8,128)(2,1)S(1)} collective-permute-done((bf16[320,640]{1,0:T(8,128)(2,1)S(1)}, bf16[320,640]{1,0:T(8,128)(2,1)S(1)}, u32[]{:S(2)}, u32[]{:S(2)}) %collective-permute-start.22) | collective-permute-done | bytes 409632 | tf_op jit(solution)/shard_map/ppermute | solution.py:51
  127.2 3.6 %all-to-all-start.1 = ((bf16[4,320,640]{2,1,0:T(8,128)(2,1)}), bf16[4,320,640]{2,1,0:T(8,128)(2,1)S(1)}, u32[]{:S(2)}, u32[]{:S(2)}) async-start(bf16[4,320,640]{2,1,0:T(8,128)(2,1)} %broadcast_in_dim.6), calls=%async_computation.1 | async-start | bytes 3276800 | tf_op jit(solution)/shard_map/all_to_all | solution.py:432
  135.2 8.7 %gradient.3 = bf16[4,768,640]{2,1,0:T(8,128)(2,1)} custom-call(s32[1]{0:T(128)} %bitcast.2.block_ref, bf16[768,1024]{1,0:T(8,128)(2,1)} %attention.1.gq_ref, bf16[1024,5120]{1,0:T(8,128)(2,1)} %in_ref.3), custom_call_target="tpu_custom_call" | custom-call | flops 8053063680 | bytes 12000000 | tf_op jit(solution)/shard_map/gradient/pallas_call | solution.py:133
  143.9 3.5 %fusion = bf16[768,640]{1,0:T(8,128)(2,1)} fusion(bf16[4,768,640]{2,1,0:T(8,128)(2,1)} %all-to-all-done), kind=kLoop, calls=%fused_computation.1 | loop fusion | flops 3932160 | bytes 4915200 | tf_op jit(solution)/shard_map/add | solution.py:438
  151.0 3.6 %all-to-all-start.2 = ((bf16[4,320,640]{2,1,0:T(8,128)(2,1)}), bf16[4,320,640]{2,1,0:T(8,128)(2,1)S(1)}, u32[]{:S(2)}, u32[]{:S(2)}) async-start(bf16[4,320,640]{2,1,0:T(8,128)(2,1)} %broadcast_in_dim.7), calls=%async_computation.2 | async-start | bytes 3276800 | tf_op jit(solution)/shard_map/all_to_all | solution.py:432
  163.9 4.0 %collective-permute-done.28.refs_7_ = bf16[320,640]{1,0:T(8,128)(2,1)} collective-permute-done((bf16[320,640]{1,0:T(8,128)(2,1)}, bf16[320,640]{1,0:T(8,128)(2,1)}, u32[]{:S(2)}, u32[]{:S(2)}) %collective-permute-start.28) | collective-permute-done | bytes 409632 | tf_op jit(solution)/shard_map/ppermute | solution.py:51
  167.9 3.7 %all-to-all-done.2.refs_9_ = bf16[4,320,640]{2,1,0:T(8,128)(2,1)S(1)} async-done(((bf16[4,320,640]{2,1,0:T(8,128)(2,1)}), bf16[4,320,640]{2,1,0:T(8,128)(2,1)S(1)}, u32[]{:S(2)}, u32[]{:S(2)}) %all-to-all-start.2) | async-done | bytes 1638432 | tf_op jit(solution)/shard_map/all_to_all | solution.py:432
  171.6 4.8 %all-to-all-start.3 = ((bf16[4,768,640]{2,1,0:T(8,128)(2,1)}), bf16[4,768,640]{2,1,0:T(8,128)(2,1)}, u32[]{:S(2)}, u32[]{:S(2)}) async-start(bf16[4,768,640]{2,1,0:T(8,128)(2,1)} %gradient.3), calls=%async_computation.3 | async-start | bytes 7864320 | tf_op jit(solution)/shard_map/all_to_all | solution.py:446
  176.6 5.3 %collective-permute-start.31 = (bf16[4,320,640]{2,1,0:T(8,128)(2,1)S(1)}, bf16[4,320,640]{2,1,0:T(8,128)(2,1)S(1)}, u32[]{:S(2)}, u32[]{:S(2)}) collective-permute-start(bf16[4,320,640]{2,1,0:T(8,128)(2,1)S(1)} %all-to-all-done.1.refs_8_), channel_id=1, source_target_pairs={{0,1},{1,0},{2,3},{3,2},{4,5},{5,4},{6,7},{7,6},{8,9},{9,8},{10,11... | collective-permute-start | bytes 4915208 | tf_op jit(solution)/shard_map/ppermute | solution.py:51
  187.6 8.6 %square.1.refs_0_ = bf16[320,640]{1,0:T(8,128)(2,1)} custom-call(bf16[320,640]{1,0:T(8,128)(2,1)} %copy-done.11, bf16[320,640]{1,0:T(8,128)(2,1)} %collective-permute-done.27.refs_1_, bf16[320,640]{1,0:T(8,128)(2,1)} %copy-done.23, bf16[320,640]{1,0:T(8,128)(2,1)} %collective-permute-done.26.refs_3_, bf16[320,640]{1,0:T(8,128)(2,1)} %copy-done.24, ...), custom_call_target="tpu_custom_call" | custom-call | flops 4194304000 | bytes 11000000 | tf_op jit(solution)/shard_map/square/pallas_call | solution.py:285
  198.6 4.4 %collective-permute-start.34 = (bf16[320,640]{1,0:T(8,128)(2,1)}, bf16[320,640]{1,0:T(8,128)(2,1)S(1)}, u32[]{:S(2)}, u32[]{:S(2)}) collective-permute-start(bf16[320,640]{1,0:T(8,128)(2,1)} %square.1.refs_0_), channel_id=1, source_target_pairs={{0,12},{1,13},{2,14},{3,15},{4,0},{5,1},{6,2},{7,3},{8,4},{9,5},{1... | collective-permute-start | bytes 1228808 | tf_op jit(solution)/shard_map/ppermute | solution.py:51
  208.7 6.3 %collective-permute-done.35.refs_4_ = bf16[320,640]{1,0:T(8,128)(2,1)S(1)} collective-permute-done((bf16[320,640]{1,0:T(8,128)(2,1)}, bf16[320,640]{1,0:T(8,128)(2,1)S(1)}, u32[]{:S(2)}, u32[]{:S(2)}) %collective-permute-start.35) | collective-permute-done | bytes 409632 | tf_op jit(solution)/shard_map/ppermute | solution.py:51
  215.0 6.0 %collective-permute-done.34.refs_1_ = bf16[320,640]{1,0:T(8,128)(2,1)S(1)} collective-permute-done((bf16[320,640]{1,0:T(8,128)(2,1)}, bf16[320,640]{1,0:T(8,128)(2,1)S(1)}, u32[]{:S(2)}, u32[]{:S(2)}) %collective-permute-start.34) | collective-permute-done | bytes 409632 | tf_op jit(solution)/shard_map/ppermute | solution.py:51
  225.0 6.0 %momentum.1 = f32[640,768]{1,0:T(8,128)} custom-call(f32[640,768]{1,0:T(8,128)} %m_ref.1, bf16[4,768,640]{2,1,0:T(8,128)(2,1)} %all-to-all-done.3.g_ref, bf16[768,640]{1,0:T(8,128)(2,1)} %collective-permute-done.37.h_ref), custom_call_target="tpu_custom_call" | custom-call | flops 4423680 | bytes 9000000 | tf_op jit(solution)/shard_map/momentum/pallas_call | solution.py:160
  237.0 11.8 %update.1 = (bf16[640,768]{1,0:T(8,128)(2,1)}, bf16[320,768]{1,0:T(8,128)(2,1)}) custom-call(bf16[320,640]{1,0:T(8,128)(2,1)} %square.1.refs_0_, bf16[320,640]{1,0:T(8,128)(2,1)} %copy-done.15, bf16[320,640]{1,0:T(8,128)(2,1)} %copy-done.13, bf16[320,640]{1,0:T(8,128)(2,1)} %copy-done.16, bf16[320,640]{1,0:T(8,128)(2,1)} %copy-done.14, ...), custom_call_target="tpu_custom_call" | custom-call | flops 1 | bytes 1 | tf_op jit(solution)/shard_map/update/pallas_call | solution.py:348
  (141 shorter events, 96.5 us)
Async XLA Ops:
  0.6 47.9 %collective-permute-start.7 = (bf16[640,768]{1,0:T(8,128)(2,1)}, bf16[640,768]{1,0:T(8,128)(2,1)S(1)}, u32[]{:S(2)}, u32[]{:S(2)}) collective-permute-start(bf16[640,768]{1,0:T(8,128)(2,1)} %refs_8_.5), channel_id=1, source_target_pairs={{0,1},{1,0},{2,3},{3,2},{4,5},{5,4},{6,7},{7,6},{8,9},{9,8},{10,11... | collective-permute-start | bytes 2949128 | tf_op jit(solution)/shard_map/ppermute | solution.py:51
  2.1 25.2 %collective-permute-start.2 = (bf16[640,768]{1,0:T(8,128)(2,1)}, bf16[640,768]{1,0:T(8,128)(2,1)}, u32[]{:S(2)}, u32[]{:S(2)}) collective-permute-start(bf16[640,768]{1,0:T(8,128)(2,1)} %refs_8_.5), channel_id=1, source_target_pairs={{0,64},{1,65},{2,66},{3,67},{4,68},{5,69},{6,70},{7,71},{8,72},{9,... | collective-permute-start | bytes 2949128 | tf_op jit(solution)/shard_map/ppermute | solution.py:51
  5.1 23.6 %collective-permute-start.1 = (bf16[640,768]{1,0:T(8,128)(2,1)}, bf16[640,768]{1,0:T(8,128)(2,1)S(1)}, u32[]{:S(2)}, u32[]{:S(2)}) collective-permute-start(bf16[640,768]{1,0:T(8,128)(2,1)} %refs_8_.5), channel_id=1, source_target_pairs={{0,48},{1,49},{2,50},{3,51},{4,52},{5,53},{6,54},{7,55},{8,56},{9,... | collective-permute-start | bytes 2949128 | tf_op jit(solution)/shard_map/ppermute | solution.py:51
  7.6 24.1 %collective-permute-start = (bf16[640,768]{1,0:T(8,128)(2,1)}, bf16[640,768]{1,0:T(8,128)(2,1)S(1)}, u32[]{:S(2)}, u32[]{:S(2)}) collective-permute-start(bf16[640,768]{1,0:T(8,128)(2,1)} %refs_8_.5), channel_id=1, source_target_pairs={{0,16},{1,17},{2,18},{3,19},{4,20},{5,21},{6,22},{7,23},{8,24},{9,... | collective-permute-start | bytes 2949128 | tf_op jit(solution)/shard_map/ppermute | solution.py:51
  31.7 16.8 %collective-permute-start.8 = (bf16[640,768]{1,0:T(8,128)(2,1)S(1)}, bf16[640,768]{1,0:T(8,128)(2,1)}, u32[]{:S(2)}, u32[]{:S(2)}) collective-permute-start(bf16[640,768]{1,0:T(8,128)(2,1)S(1)} %collective-permute-done.1.refs_1_.refs_9_), channel_id=1, source_target_pairs={{0,1},{1,0},{2,3},{3,2},{4,5},{5,4},{6,7},{7,6},{8,9},{9,8},{10,11... | collective-permute-start | bytes 2949128 | tf_op jit(solution)/shard_map/ppermute | solution.py:51
  50.1 17.3 %collective-permute-start.11 = (bf16[640,768]{1,0:T(8,128)(2,1)}, bf16[640,768]{1,0:T(8,128)(2,1)}, u32[]{:S(2)}, u32[]{:S(2)}) collective-permute-start(bf16[640,768]{1,0:T(8,128)(2,1)} %collective-permute-done.2.refs_0_.refs_12_), channel_id=1, source_target_pairs={{0,1},{1,0},{2,3},{3,2},{4,5},{5,4},{6,7},{7,6},{8,9},{9,8},{10,11... | collective-permute-start | bytes 2949128 | tf_op jit(solution)/shard_map/ppermute | solution.py:51
  50.2 23.7 %collective-permute-start.6 = (bf16[640,768]{1,0:T(8,128)(2,1)}, bf16[640,768]{1,0:T(8,128)(2,1)}, u32[]{:S(2)}, u32[]{:S(2)}) collective-permute-start(bf16[640,768]{1,0:T(8,128)(2,1)} %collective-permute-done.2.refs_0_.refs_12_), channel_id=1, source_target_pairs={{0,48},{1,49},{2,50},{3,51},{4,52},{5,53},{6,54},{7,55},{8,56},{9,... | collective-permute-start | bytes 2949128 | tf_op jit(solution)/shard_map/ppermute | solution.py:51
  52.9 24.1 %collective-permute-start.5 = (bf16[640,768]{1,0:T(8,128)(2,1)}, bf16[640,768]{1,0:T(8,128)(2,1)}, u32[]{:S(2)}, u32[]{:S(2)}) collective-permute-start(bf16[640,768]{1,0:T(8,128)(2,1)} %collective-permute-done.2.refs_0_.refs_12_), channel_id=1, source_target_pairs={{0,16},{1,17},{2,18},{3,19},{4,20},{5,21},{6,22},{7,23},{8,24},{9,... | collective-permute-start | bytes 2949128 | tf_op jit(solution)/shard_map/ppermute | solution.py:51
  52.9 24.2 %collective-permute-start.10 = (bf16[640,768]{1,0:T(8,128)(2,1)S(1)}, bf16[640,768]{1,0:T(8,128)(2,1)}, u32[]{:S(2)}, u32[]{:S(2)}) collective-permute-start(bf16[640,768]{1,0:T(8,128)(2,1)S(1)} %constant_dynamic-update-slice_fusion.refs_2_.refs_10_), channel_id=1, source_target_pairs={{0,64},{1,65},{2,66},{3,67},{4,68},{5,69},{6,70},{7,71},{8,72},{9,... | collective-permute-start | bytes 2949128 | tf_op jit(solution)/shard_map/ppermute | solution.py:51
  60.7 65.2 %all-to-all-start = ((bf16[4,768,640]{2,1,0:T(8,128)(2,1)}), bf16[4,768,640]{2,1,0:T(8,128)(2,1)}, u32[]{:S(2)}, u32[]{:S(2)}) async-start(bf16[4,768,640]{2,1,0:T(8,128)(2,1)} %gradient.2), calls=%async_computation | async-start | bytes 7864320 | tf_op jit(solution)/shard_map/all_to_all | solution.py:401
  94.9 21.0 %collective-permute-start.20 = (bf16[320,640]{1,0:T(8,128)(2,1)}, bf16[320,640]{1,0:T(8,128)(2,1)S(1)}, u32[]{:S(2)}, u32[]{:S(2)}) collective-permute-start(bf16[320,640]{1,0:T(8,128)(2,1)} %get-tuple-element.108), channel_id=1, source_target_pairs={{0,8},{1,9},{2,10},{3,11},{4,12},{5,13},{6,14},{7,15},{8,0},{9,1},... | collective-permute-start | bytes 1228808 | tf_op jit(solution)/shard_map/ppermute | solution.py:51
  98.2 17.7 %collective-permute-start.21 = (bf16[320,640]{1,0:T(8,128)(2,1)}, bf16[320,640]{1,0:T(8,128)(2,1)S(1)}, u32[]{:S(2)}, u32[]{:S(2)}) collective-permute-start(bf16[320,640]{1,0:T(8,128)(2,1)} %get-tuple-element.109), channel_id=1, source_target_pairs={{0,12},{1,13},{2,14},{3,15},{4,0},{5,1},{6,2},{7,3},{8,4},{9,5},{1... | collective-permute-start | bytes 1228808 | tf_op jit(solution)/shard_map/ppermute | solution.py:51
  127.2 22.4 %all-to-all-start.1 = ((bf16[4,320,640]{2,1,0:T(8,128)(2,1)}), bf16[4,320,640]{2,1,0:T(8,128)(2,1)S(1)}, u32[]{:S(2)}, u32[]{:S(2)}) async-start(bf16[4,320,640]{2,1,0:T(8,128)(2,1)} %broadcast_in_dim.6), calls=%async_computation.1 | async-start | bytes 3276800 | tf_op jit(solution)/shard_map/all_to_all | solution.py:432
  130.7 16.7 %collective-permute-start.25 = (bf16[320,640]{1,0:T(8,128)(2,1)S(1)}, bf16[320,640]{1,0:T(8,128)(2,1)S(1)}, u32[]{:S(2)}, u32[]{:S(2)}) collective-permute-start(bf16[320,640]{1,0:T(8,128)(2,1)S(1)} %add_convert_fusion.1.refs_0_), channel_id=1, source_target_pairs={{0,64},{1,65},{2,66},{3,67},{4,68},{5,69},{6,70},{7,71},{8,72},{9,... | collective-permute-start | bytes 1228808 | tf_op jit(solution)/shard_map/ppermute | solution.py:51
  151.0 20.5 %all-to-all-start.2 = ((bf16[4,320,640]{2,1,0:T(8,128)(2,1)}), bf16[4,320,640]{2,1,0:T(8,128)(2,1)S(1)}, u32[]{:S(2)}, u32[]{:S(2)}) async-start(bf16[4,320,640]{2,1,0:T(8,128)(2,1)} %broadcast_in_dim.7), calls=%async_computation.2 | async-start | bytes 3276800 | tf_op jit(solution)/shard_map/all_to_all | solution.py:432
  157.9 18.5 %collective-permute-start.30 = (bf16[320,640]{1,0:T(8,128)(2,1)}, bf16[320,640]{1,0:T(8,128)(2,1)}, u32[]{:S(2)}, u32[]{:S(2)}) collective-permute-start(bf16[320,640]{1,0:T(8,128)(2,1)} %copy-done.23), channel_id=1, source_target_pairs={{0,2},{1,3},{2,0},{3,1},{4,6},{5,7},{6,4},{7,5},{8,10},{9,11},{10,... | collective-permute-start | bytes 1228808 | tf_op jit(solution)/shard_map/ppermute | solution.py:51
  158.6 17.8 %collective-permute-start.27 = (bf16[320,640]{1,0:T(8,128)(2,1)}, bf16[320,640]{1,0:T(8,128)(2,1)}, u32[]{:S(2)}, u32[]{:S(2)}) collective-permute-start(bf16[320,640]{1,0:T(8,128)(2,1)} %copy-done.11), channel_id=1, source_target_pairs={{0,12},{1,13},{2,14},{3,15},{4,0},{5,1},{6,2},{7,3},{8,4},{9,5},{1... | collective-permute-start | bytes 1228808 | tf_op jit(solution)/shard_map/ppermute | solution.py:51
  161.2 15.4 %collective-permute-start.26 = (bf16[320,640]{1,0:T(8,128)(2,1)}, bf16[320,640]{1,0:T(8,128)(2,1)}, u32[]{:S(2)}, u32[]{:S(2)}) collective-permute-start(bf16[320,640]{1,0:T(8,128)(2,1)} %copy-done.11), channel_id=1, source_target_pairs={{0,4},{1,5},{2,6},{3,7},{4,8},{5,9},{6,10},{7,11},{8,12},{9,13},{1... | collective-permute-start | bytes 1228808 | tf_op jit(solution)/shard_map/ppermute | solution.py:51
  161.2 15.4 %collective-permute-start.29 = (bf16[320,640]{1,0:T(8,128)(2,1)}, bf16[320,640]{1,0:T(8,128)(2,1)}, u32[]{:S(2)}, u32[]{:S(2)}) collective-permute-start(bf16[320,640]{1,0:T(8,128)(2,1)} %copy-done.24), channel_id=1, source_target_pairs={{0,12},{1,13},{2,14},{3,15},{4,0},{5,1},{6,2},{7,3},{8,4},{9,5},{1... | collective-permute-start | bytes 1228808 | tf_op jit(solution)/shard_map/ppermute | solution.py:51
  171.6 53.4 %all-to-all-start.3 = ((bf16[4,768,640]{2,1,0:T(8,128)(2,1)}), bf16[4,768,640]{2,1,0:T(8,128)(2,1)}, u32[]{:S(2)}, u32[]{:S(2)}) async-start(bf16[4,768,640]{2,1,0:T(8,128)(2,1)} %gradient.3), calls=%async_computation.3 | async-start | bytes 7864320 | tf_op jit(solution)/shard_map/all_to_all | solution.py:446
  182.0 24.7 %collective-permute-start.37 = (bf16[768,640]{1,0:T(8,128)(2,1)}, bf16[768,640]{1,0:T(8,128)(2,1)}, u32[]{:S(2)}, u32[]{:S(2)}) collective-permute-start(bf16[768,640]{1,0:T(8,128)(2,1)} %fusion), channel_id=1, source_target_pairs={{0,64},{1,65},{2,66},{3,67},{4,68},{5,69},{6,70},{7,71},{8,72},{9,... | collective-permute-start | bytes 2949128 | tf_op jit(solution)/shard_map/ppermute | solution.py:51
  197.9 17.1 %collective-permute-start.35 = (bf16[320,640]{1,0:T(8,128)(2,1)}, bf16[320,640]{1,0:T(8,128)(2,1)S(1)}, u32[]{:S(2)}, u32[]{:S(2)}) collective-permute-start(bf16[320,640]{1,0:T(8,128)(2,1)} %square.1.refs_0_), channel_id=1, source_target_pairs={{0,2},{1,3},{2,0},{3,1},{4,6},{5,7},{6,4},{7,5},{8,10},{9,11},{10,... | collective-permute-start | bytes 1228808 | tf_op jit(solution)/shard_map/ppermute | solution.py:51
  198.6 22.4 %collective-permute-start.34 = (bf16[320,640]{1,0:T(8,128)(2,1)}, bf16[320,640]{1,0:T(8,128)(2,1)S(1)}, u32[]{:S(2)}, u32[]{:S(2)}) collective-permute-start(bf16[320,640]{1,0:T(8,128)(2,1)} %square.1.refs_0_), channel_id=1, source_target_pairs={{0,12},{1,13},{2,14},{3,15},{4,0},{5,1},{6,2},{7,3},{8,4},{9,5},{1... | collective-permute-start | bytes 1228808 | tf_op jit(solution)/shard_map/ppermute | solution.py:51
  203.0 18.0 %collective-permute-start.33 = (bf16[320,640]{1,0:T(8,128)(2,1)}, bf16[320,640]{1,0:T(8,128)(2,1)S(1)}, u32[]{:S(2)}, u32[]{:S(2)}) collective-permute-start(bf16[320,640]{1,0:T(8,128)(2,1)} %square.1.refs_0_), channel_id=1, source_target_pairs={{0,4},{1,5},{2,6},{3,7},{4,8},{5,9},{6,10},{7,11},{8,12},{9,13},{1... | collective-permute-start | bytes 1228808 | tf_op jit(solution)/shard_map/ppermute | solution.py:51
  (49 other events, 454.9 us)

commit v5 on v4

--- a/solution.py
+++ b/solution.py
@@ -369,12 +369,12 @@
     f32, bf16 = jnp.float32, jnp.bfloat16
 
     own = iterate
+    across = move(own, Y_HI)
+    above = move(own, X_DOWN)
     below = move(own, X_UP)
-    above = move(own, X_DOWN)
-    across = move(own, Y_HI)
     kv_index = (lax.axis_index("grid") // 2).astype(jnp.int32).reshape(1)
     grad_query_t = attention(queries, key_rows, values, attn_out, grad_out, kv_index)
-    below, above, across, grad_query_t = together((below, above, across, grad_query_t))
+    across, above, below, grad_query_t = together((across, above, below, grad_query_t))
 
     far_top, far_bottom = move(below[:HALF], X_UP), move(above[HALF:], X_DOWN)
     own_other, above_other, below_other = move(own, CORE), move(above, CORE), move(below, CORE)
@@ -452,10 +452,10 @@
         (here, there, move(here, CORE), move(there, CORE)),
     )
 
-    z_below, z_above = move(combined, Z_UP), move(combined, Z_DOWN)
-    lo, z_far = move(combined, Y_LO), move(combined, Z_FAR)
+    z_far, lo = move(combined, Z_FAR), move(combined, Y_LO)
+    z_above, z_below = move(combined, Z_DOWN), move(combined, Z_UP)
     far_term = move(far_term, Y_HI)
-    z_below, z_above, lo, z_far, far_term = together((z_below, z_above, lo, z_far, far_term))
+    z_far, lo, z_above, z_below, far_term = together((z_far, lo, z_above, z_below, far_term))
     lo_below, lo_above, lo_far = move(lo, Z_UP), move(lo, Z_DOWN), move(z_far, Y_LO)
     momentum_next = momentum_of(momentum, terms, far_term)
     lo_below, lo_above, lo_far, momentum_next = together(

time: 254 us -> 253 us (level)
  transfers between devices with their start and end apart: 46 -> 46, of which waited for: 26 -> 27; matrix products, arithmetic and copies ran while one was open for 3% -> 3% of each run, Pallas kernels for 24% -> 24%
where the time goes in v5:
time: 253 us; the launch traced here: 252 us
  waiting for transfers between devices  83.6 us (33%)
  starting transfers between devices  80 us (32%)
  Pallas kernels  71.7 us (28%)
  local copies, waits for them, and re-layouts  9.96 us (4%)
  other arithmetic  5.5 us (2%)
    ppermute x42, waiting for transfers between devices, move(): return lax.ppermute(array, ('y_hi', 'x', 'grid'), perm)  78.3 us
    ppermute x42, starting transfers between devices, move(): return lax.ppermute(array, ('y_hi', 'x', 'grid'), perm)  62.8 us
    pallas_call x2, Pallas kernels, gradient_partial(): pl.pallas_call(gradient_kernel, grid_spec=pltpu.PrefetchScalarGridSpec(nu...  17.4 us
    pallas_call x1, Pallas kernels, attention(): pl.pallas_call(body, grid_spec=pltpu.PrefetchScalarGridSpec(num_scalar_pr...  14.3 us
    pallas_call x2, Pallas kernels, gram_partial(): pl.pallas_call(gram_kernel, in_specs=[pl.BlockSpec(memory_space=pl.ANY)]...  13.6 us
    pallas_call x1, Pallas kernels, update_of(): pl.pallas_call(update_kernel, in_specs=[pl.BlockSpec(memory_space=pl.ANY)...  11.8 us
    pallas_call x1, Pallas kernels, square(): pl.pallas_call(square_kernel, in_specs=[pl.BlockSpec(memory_space=pl.ANY)...  8.57 us
    all_to_all x2, starting transfers between devices, along_x(): lax.all_to_all(jnp.broadcast_to(piece, (4, HALF, ROWS)), 'x', 0, 0, tiled...  7.46 us
  transfers between devices with their start and end apart: 46, of which 27 were waited for; matrix products, arithmetic and copies ran while one was open for 3% of the time, Pallas kernels for 24%

profile of v5, /device:TPU:1, one launch (start us, length us, event | category | flops | bytes accessed | tf_op | source)
XLA Modules:
  0.0 251.7 jit_solution(16552402866981675322)
XLA Ops:
  7.8 14.3 %attention.1.gq_ref = bf16[768,1024]{1,0:T(8,128)(2,1)} custom-call(s32[1]{0:T(128)} %bitcast.kv, bf16[1024,768]{1,0:T(8,128)(2,1)} %refs_0_.2, bf16[1024,1024]{1,0:T(8,128)(2,1)} %refs_1_.1, bf16[1024,1024]{1,0:T(8,128)(2,1)} %refs_2_.1, bf16[1024,768]{1,0:T(8,128)(2,1)} %refs_3_.1, bf16[1024,768]{1,0:T(8,128)(2,1)} %refs_4_.1), custom_call_target="tpu_custom_call" | custom-call | flops 24000000000 | bytes 8000000 | tf_op jit(solution)/shard_map/attention/pallas_call | solution.py:113
  22.1 4.9 %collective-permute-done.2.refs_3_.refs_11_ = bf16[640,768]{1,0:T(8,128)(2,1)S(1)} collective-permute-done((bf16[640,768]{1,0:T(8,128)(2,1)}, bf16[640,768]{1,0:T(8,128)(2,1)S(1)}, u32[]{:S(2)}, u32[]{:S(2)}) %collective-permute-start.2) | collective-permute-done | bytes 983072 | tf_op jit(solution)/shard_map/ppermute | solution.py:51
  35.2 8.7 %gradient.2 = bf16[4,768,640]{2,1,0:T(8,128)(2,1)} custom-call(s32[1]{0:T(128)} %bitcast.1.block_ref, bf16[768,1024]{1,0:T(8,128)(2,1)} %attention.1.gq_ref, bf16[1024,5120]{1,0:T(8,128)(2,1)} %in_ref.3), custom_call_target="tpu_custom_call" | custom-call | flops 8053063680 | bytes 12000000 | tf_op jit(solution)/shard_map/gradient/pallas_call | solution.py:133
  54.4 6.8 %gram.2 = (f32[320,640]{1,0:T(8,128)}, bf16[320,640]{1,0:T(8,128)(2,1)}, bf16[320,640]{1,0:T(8,128)(2,1)}, bf16[320,640]{1,0:T(8,128)(2,1)}) custom-call(bf16[640,768]{1,0:T(8,128)(2,1)} %refs_8_.5, bf16[640,768]{1,0:T(8,128)(2,1)} %copy-done.2, bf16[640,768]{1,0:T(8,128)(2,1)} %copy-done.3, bf16[640,768]{1,0:T(8,128)(2,1)} %copy-done.1, ...), custom_call_target="tpu_custom_call" | custom-call | flops 1 | bytes 1 | tf_op jit(solution)/shard_map/gram/pallas_call | solution.py:212
  61.2 5.0 %all-to-all-start = ((bf16[4,768,640]{2,1,0:T(8,128)(2,1)}), bf16[4,768,640]{2,1,0:T(8,128)(2,1)}, u32[]{:S(2)}, u32[]{:S(2)}) async-start(bf16[4,768,640]{2,1,0:T(8,128)(2,1)} %gradient.2), calls=%async_computation | async-start | bytes 7864320 | tf_op jit(solution)/shard_map/all_to_all | solution.py:401
  74.7 4.3 %collective-permute-done.13 = bf16[320,640]{1,0:T(8,128)(2,1)S(1)} collective-permute-done((bf16[320,640]{1,0:T(8,128)(2,1)S(1)}, bf16[320,640]{1,0:T(8,128)(2,1)S(1)}, u32[]{:S(2)}, u32[]{:S(2)}) %collective-permute-start.13) | collective-permute-done | bytes 409632 | tf_op jit(solution)/shard_map/ppermute | solution.py:51
  86.7 6.8 %gram.3 = (f32[320,640]{1,0:T(8,128)}, bf16[320,640]{1,0:T(8,128)(2,1)}, bf16[320,640]{1,0:T(8,128)(2,1)}, bf16[320,640]{1,0:T(8,128)(2,1)}) custom-call(bf16[640,768]{1,0:T(8,128)(2,1)} %collective-permute-done.refs_0_.refs_12_, bf16[640,768]{1,0:T(8,128)(2,1)} %collective-permute-done.6.refs_1_.refs_13_, ...), custom_call_target="tpu_custom_call" | custom-call | flops 1 | bytes 1 | tf_op jit(solution)/shard_map/gram/pallas_call | solution.py:212
  100.0 5.6 %collective-permute-done.19 = bf16[320,640]{1,0:T(8,128)(2,1)S(1)} collective-permute-done((bf16[320,640]{1,0:T(8,128)(2,1)}, bf16[320,640]{1,0:T(8,128)(2,1)S(1)}, u32[]{:S(2)}, u32[]{:S(2)}) %collective-permute-start.19) | collective-permute-done | bytes 409632 | tf_op jit(solution)/shard_map/ppermute | solution.py:51
  105.6 9.9 %collective-permute-done.20 = bf16[320,640]{1,0:T(8,128)(2,1)S(1)} collective-permute-done((bf16[320,640]{1,0:T(8,128)(2,1)}, bf16[320,640]{1,0:T(8,128)(2,1)S(1)}, u32[]{:S(2)}, u32[]{:S(2)}) %collective-permute-start.20) | collective-permute-done | bytes 409632 | tf_op jit(solution)/shard_map/ppermute | solution.py:51
  116.3 8.9 %collective-permute-done.22 = bf16[320,640]{1,0:T(8,128)(2,1)S(1)} collective-permute-done((bf16[320,640]{1,0:T(8,128)(2,1)S(1)}, bf16[320,640]{1,0:T(8,128)(2,1)S(1)}, u32[]{:S(2)}, u32[]{:S(2)}) %collective-permute-start.22) | collective-permute-done | bytes 409632 | tf_op jit(solution)/shard_map/ppermute | solution.py:51
  126.9 3.9 %all-to-all-start.1 = ((bf16[4,320,640]{2,1,0:T(8,128)(2,1)}), bf16[4,320,640]{2,1,0:T(8,128)(2,1)S(1)}, u32[]{:S(2)}, u32[]{:S(2)}) async-start(bf16[4,320,640]{2,1,0:T(8,128)(2,1)} %broadcast_in_dim.6), calls=%async_computation.1 | async-start | bytes 3276800 | tf_op jit(solution)/shard_map/all_to_all | solution.py:432
  133.8 8.7 %gradient.3 = bf16[4,768,640]{2,1,0:T(8,128)(2,1)} custom-call(s32[1]{0:T(128)} %bitcast.2.block_ref, bf16[768,1024]{1,0:T(8,128)(2,1)} %attention.1.gq_ref, bf16[1024,5120]{1,0:T(8,128)(2,1)} %in_ref.3), custom_call_target="tpu_custom_call" | custom-call | flops 8053063680 | bytes 12000000 | tf_op jit(solution)/shard_map/gradient/pallas_call | solution.py:133
  142.5 3.5 %fusion = bf16[768,640]{1,0:T(8,128)(2,1)} fusion(bf16[4,768,640]{2,1,0:T(8,128)(2,1)} %all-to-all-done), kind=kLoop, calls=%fused_computation.1 | loop fusion | flops 3932160 | bytes 4915200 | tf_op jit(solution)/shard_map/add | solution.py:438
  150.7 3.6 %all-to-all-start.2 = ((bf16[4,320,640]{2,1,0:T(8,128)(2,1)}), bf16[4,320,640]{2,1,0:T(8,128)(2,1)S(1)}, u32[]{:S(2)}, u32[]{:S(2)}) async-start(bf16[4,320,640]{2,1,0:T(8,128)(2,1)} %broadcast_in_dim.7), calls=%async_computation.2 | async-start | bytes 3276800 | tf_op jit(solution)/shard_map/all_to_all | solution.py:432
  163.4 4.5 %collective-permute-done.28.refs_7_ = bf16[320,640]{1,0:T(8,128)(2,1)} collective-permute-done((bf16[320,640]{1,0:T(8,128)(2,1)}, bf16[320,640]{1,0:T(8,128)(2,1)}, u32[]{:S(2)}, u32[]{:S(2)}) %collective-permute-start.28) | collective-permute-done | bytes 409632 | tf_op jit(solution)/shard_map/ppermute | solution.py:51
  167.9 3.7 %all-to-all-done.2.refs_9_ = bf16[4,320,640]{2,1,0:T(8,128)(2,1)S(1)} async-done(((bf16[4,320,640]{2,1,0:T(8,128)(2,1)}), bf16[4,320,640]{2,1,0:T(8,128)(2,1)S(1)}, u32[]{:S(2)}, u32[]{:S(2)}) %all-to-all-start.2) | async-done | bytes 1638432 | tf_op jit(solution)/shard_map/all_to_all | solution.py:432
  171.6 4.8 %all-to-all-start.3 = ((bf16[4,768,640]{2,1,0:T(8,128)(2,1)}), bf16[4,768,640]{2,1,0:T(8,128)(2,1)}, u32[]{:S(2)}, u32[]{:S(2)}) async-start(bf16[4,768,640]{2,1,0:T(8,128)(2,1)} %gradient.3), calls=%async_computation.3 | async-start | bytes 7864320 | tf_op jit(solution)/shard_map/all_to_all | solution.py:446
  176.7 4.9 %collective-permute-start.31 = (bf16[4,320,640]{2,1,0:T(8,128)(2,1)S(1)}, bf16[4,320,640]{2,1,0:T(8,128)(2,1)S(1)}, u32[]{:S(2)}, u32[]{:S(2)}) collective-permute-start(bf16[4,320,640]{2,1,0:T(8,128)(2,1)S(1)} %all-to-all-done.1.refs_8_), channel_id=1, source_target_pairs={{0,1},{1,0},{2,3},{3,2},{4,5},{5,4},{6,7},{7,6},{8,9},{9,8},{10,11... | collective-permute-start | bytes 4915208 | tf_op jit(solution)/shard_map/ppermute | solution.py:51
  187.3 8.6 %square.1.refs_0_ = bf16[320,640]{1,0:T(8,128)(2,1)} custom-call(bf16[320,640]{1,0:T(8,128)(2,1)} %copy-done.11, bf16[320,640]{1,0:T(8,128)(2,1)} %collective-permute-done.27.refs_1_, bf16[320,640]{1,0:T(8,128)(2,1)} %copy-done.23, bf16[320,640]{1,0:T(8,128)(2,1)} %collective-permute-done.26.refs_3_, bf16[320,640]{1,0:T(8,128)(2,1)} %copy-done.24, ...), custom_call_target="tpu_custom_call" | custom-call | flops 4194304000 | bytes 11000000 | tf_op jit(solution)/shard_map/square/pallas_call | solution.py:285
  195.9 3.4 %collective-permute-start.36 = (bf16[320,640]{1,0:T(8,128)(2,1)}, bf16[320,640]{1,0:T(8,128)(2,1)S(1)}, u32[]{:S(2)}, u32[]{:S(2)}) collective-permute-start(bf16[320,640]{1,0:T(8,128)(2,1)} %square.1.refs_0_), channel_id=1, source_target_pairs={{0,4},{1,5},{2,6},{3,7},{4,8},{5,9},{6,10},{7,11},{8,12},{9,13},{1... | collective-permute-start | bytes 1228808 | tf_op jit(solution)/shard_map/ppermute | solution.py:51
  206.5 5.2 %collective-permute-done.36.refs_3_ = bf16[320,640]{1,0:T(8,128)(2,1)S(1)} collective-permute-done((bf16[320,640]{1,0:T(8,128)(2,1)}, bf16[320,640]{1,0:T(8,128)(2,1)S(1)}, u32[]{:S(2)}, u32[]{:S(2)}) %collective-permute-start.36) | collective-permute-done | bytes 409632 | tf_op jit(solution)/shard_map/ppermute | solution.py:51
  211.7 7.7 %collective-permute-done.35.refs_1_ = bf16[320,640]{1,0:T(8,128)(2,1)S(1)} collective-permute-done((bf16[320,640]{1,0:T(8,128)(2,1)}, bf16[320,640]{1,0:T(8,128)(2,1)S(1)}, u32[]{:S(2)}, u32[]{:S(2)}) %collective-permute-start.35) | collective-permute-done | bytes 409632 | tf_op jit(solution)/shard_map/ppermute | solution.py:51
  223.4 6.0 %momentum.1 = f32[640,768]{1,0:T(8,128)} custom-call(f32[640,768]{1,0:T(8,128)} %m_ref.1, bf16[4,768,640]{2,1,0:T(8,128)(2,1)} %all-to-all-done.3.g_ref, bf16[768,640]{1,0:T(8,128)(2,1)} %collective-permute-done.37.h_ref), custom_call_target="tpu_custom_call" | custom-call | flops 4423680 | bytes 9000000 | tf_op jit(solution)/shard_map/momentum/pallas_call | solution.py:160
  234.7 11.8 %update.1 = (bf16[640,768]{1,0:T(8,128)(2,1)}, bf16[320,768]{1,0:T(8,128)(2,1)}) custom-call(bf16[320,640]{1,0:T(8,128)(2,1)} %square.1.refs_0_, bf16[320,640]{1,0:T(8,128)(2,1)} %copy-done.14, bf16[320,640]{1,0:T(8,128)(2,1)} %copy-done.16, bf16[320,640]{1,0:T(8,128)(2,1)} %copy-done.13, bf16[320,640]{1,0:T(8,128)(2,1)} %copy-done.15, ...), custom_call_target="tpu_custom_call" | custom-call | flops 1 | bytes 1 | tf_op jit(solution)/shard_map/update/pallas_call | solution.py:348
  (141 shorter events, 95.3 us)
Async XLA Ops:
  0.6 45.6 %collective-permute-start.7 = (bf16[640,768]{1,0:T(8,128)(2,1)}, bf16[640,768]{1,0:T(8,128)(2,1)S(1)}, u32[]{:S(2)}, u32[]{:S(2)}) collective-permute-start(bf16[640,768]{1,0:T(8,128)(2,1)} %refs_8_.5), channel_id=1, source_target_pairs={{0,1},{1,0},{2,3},{3,2},{4,5},{5,4},{6,7},{7,6},{8,9},{9,8},{10,11... | collective-permute-start | bytes 2949128 | tf_op jit(solution)/shard_map/ppermute | solution.py:51
  2.1 24.8 %collective-permute-start.2 = (bf16[640,768]{1,0:T(8,128)(2,1)}, bf16[640,768]{1,0:T(8,128)(2,1)S(1)}, u32[]{:S(2)}, u32[]{:S(2)}) collective-permute-start(bf16[640,768]{1,0:T(8,128)(2,1)} %refs_8_.5), channel_id=1, source_target_pairs={{0,16},{1,17},{2,18},{3,19},{4,20},{5,21},{6,22},{7,23},{8,24},{9,... | collective-permute-start | bytes 2949128 | tf_op jit(solution)/shard_map/ppermute | solution.py:51
  3.4 23.5 %collective-permute-start.1 = (bf16[640,768]{1,0:T(8,128)(2,1)}, bf16[640,768]{1,0:T(8,128)(2,1)S(1)}, u32[]{:S(2)}, u32[]{:S(2)}) collective-permute-start(bf16[640,768]{1,0:T(8,128)(2,1)} %refs_8_.5), channel_id=1, source_target_pairs={{0,48},{1,49},{2,50},{3,51},{4,52},{5,53},{6,54},{7,55},{8,56},{9,... | collective-permute-start | bytes 2949128 | tf_op jit(solution)/shard_map/ppermute | solution.py:51
  4.8 24.6 %collective-permute-start = (bf16[640,768]{1,0:T(8,128)(2,1)}, bf16[640,768]{1,0:T(8,128)(2,1)}, u32[]{:S(2)}, u32[]{:S(2)}) collective-permute-start(bf16[640,768]{1,0:T(8,128)(2,1)} %refs_8_.5), channel_id=1, source_target_pairs={{0,64},{1,65},{2,66},{3,67},{4,68},{5,69},{6,70},{7,71},{8,72},{9,... | collective-permute-start | bytes 2949128 | tf_op jit(solution)/shard_map/ppermute | solution.py:51
  29.5 16.8 %collective-permute-start.8 = (bf16[640,768]{1,0:T(8,128)(2,1)S(1)}, bf16[640,768]{1,0:T(8,128)(2,1)}, u32[]{:S(2)}, u32[]{:S(2)}) collective-permute-start(bf16[640,768]{1,0:T(8,128)(2,1)S(1)} %collective-permute-done.1.refs_1_.refs_9_), channel_id=1, source_target_pairs={{0,1},{1,0},{2,3},{3,2},{4,5},{5,4},{6,7},{7,6},{8,9},{9,8},{10,11... | collective-permute-start | bytes 2949128 | tf_op jit(solution)/shard_map/ppermute | solution.py:51
  47.8 20.2 %collective-permute-start.11 = (bf16[640,768]{1,0:T(8,128)(2,1)}, bf16[640,768]{1,0:T(8,128)(2,1)}, u32[]{:S(2)}, u32[]{:S(2)}) collective-permute-start(bf16[640,768]{1,0:T(8,128)(2,1)} %collective-permute-done.refs_0_.refs_12_), channel_id=1, source_target_pairs={{0,1},{1,0},{2,3},{3,2},{4,5},{5,4},{6,7},{7,6},{8,9},{9,8},{10,11... | collective-permute-start | bytes 2949128 | tf_op jit(solution)/shard_map/ppermute | solution.py:51
  47.9 23.7 %collective-permute-start.6 = (bf16[640,768]{1,0:T(8,128)(2,1)}, bf16[640,768]{1,0:T(8,128)(2,1)}, u32[]{:S(2)}, u32[]{:S(2)}) collective-permute-start(bf16[640,768]{1,0:T(8,128)(2,1)} %collective-permute-done.refs_0_.refs_12_), channel_id=1, source_target_pairs={{0,48},{1,49},{2,50},{3,51},{4,52},{5,53},{6,54},{7,55},{8,56},{9,... | collective-permute-start | bytes 2949128 | tf_op jit(solution)/shard_map/ppermute | solution.py:51
  50.5 24.1 %collective-permute-start.5 = (bf16[640,768]{1,0:T(8,128)(2,1)}, bf16[640,768]{1,0:T(8,128)(2,1)}, u32[]{:S(2)}, u32[]{:S(2)}) collective-permute-start(bf16[640,768]{1,0:T(8,128)(2,1)} %collective-permute-done.refs_0_.refs_12_), channel_id=1, source_target_pairs={{0,16},{1,17},{2,18},{3,19},{4,20},{5,21},{6,22},{7,23},{8,24},{9,... | collective-permute-start | bytes 2949128 | tf_op jit(solution)/shard_map/ppermute | solution.py:51
  50.5 24.2 %collective-permute-start.10 = (bf16[640,768]{1,0:T(8,128)(2,1)S(1)}, bf16[640,768]{1,0:T(8,128)(2,1)}, u32[]{:S(2)}, u32[]{:S(2)}) collective-permute-start(bf16[640,768]{1,0:T(8,128)(2,1)S(1)} %constant_dynamic-update-slice_fusion.refs_2_.refs_10_), channel_id=1, source_target_pairs={{0,64},{1,65},{2,66},{3,67},{4,68},{5,69},{6,70},{7,71},{8,72},{9,... | collective-permute-start | bytes 2949128 | tf_op jit(solution)/shard_map/ppermute | solution.py:51
  61.2 64.3 %all-to-all-start = ((bf16[4,768,640]{2,1,0:T(8,128)(2,1)}), bf16[4,768,640]{2,1,0:T(8,128)(2,1)}, u32[]{:S(2)}, u32[]{:S(2)}) async-start(bf16[4,768,640]{2,1,0:T(8,128)(2,1)} %gradient.2), calls=%async_computation | async-start | bytes 7864320 | tf_op jit(solution)/shard_map/all_to_all | solution.py:401
  94.8 20.7 %collective-permute-start.20 = (bf16[320,640]{1,0:T(8,128)(2,1)}, bf16[320,640]{1,0:T(8,128)(2,1)S(1)}, u32[]{:S(2)}, u32[]{:S(2)}) collective-permute-start(bf16[320,640]{1,0:T(8,128)(2,1)} %get-tuple-element.108), channel_id=1, source_target_pairs={{0,8},{1,9},{2,10},{3,11},{4,12},{5,13},{6,14},{7,15},{8,0},{9,1},... | collective-permute-start | bytes 1228808 | tf_op jit(solution)/shard_map/ppermute | solution.py:51
  97.8 17.8 %collective-permute-start.21 = (bf16[320,640]{1,0:T(8,128)(2,1)}, bf16[320,640]{1,0:T(8,128)(2,1)S(1)}, u32[]{:S(2)}, u32[]{:S(2)}) collective-permute-start(bf16[320,640]{1,0:T(8,128)(2,1)} %get-tuple-element.109), channel_id=1, source_target_pairs={{0,12},{1,13},{2,14},{3,15},{4,0},{5,1},{6,2},{7,3},{8,4},{9,5},{1... | collective-permute-start | bytes 1228808 | tf_op jit(solution)/shard_map/ppermute | solution.py:51
  126.9 22.4 %all-to-all-start.1 = ((bf16[4,320,640]{2,1,0:T(8,128)(2,1)}), bf16[4,320,640]{2,1,0:T(8,128)(2,1)S(1)}, u32[]{:S(2)}, u32[]{:S(2)}) async-start(bf16[4,320,640]{2,1,0:T(8,128)(2,1)} %broadcast_in_dim.6), calls=%async_computation.1 | async-start | bytes 3276800 | tf_op jit(solution)/shard_map/all_to_all | solution.py:432
  150.7 20.8 %all-to-all-start.2 = ((bf16[4,320,640]{2,1,0:T(8,128)(2,1)}), bf16[4,320,640]{2,1,0:T(8,128)(2,1)S(1)}, u32[]{:S(2)}, u32[]{:S(2)}) async-start(bf16[4,320,640]{2,1,0:T(8,128)(2,1)} %broadcast_in_dim.7), calls=%async_computation.2 | async-start | bytes 3276800 | tf_op jit(solution)/shard_map/all_to_all | solution.py:432
  157.6 18.7 %collective-permute-start.30 = (bf16[320,640]{1,0:T(8,128)(2,1)}, bf16[320,640]{1,0:T(8,128)(2,1)}, u32[]{:S(2)}, u32[]{:S(2)}) collective-permute-start(bf16[320,640]{1,0:T(8,128)(2,1)} %copy-done.23), channel_id=1, source_target_pairs={{0,2},{1,3},{2,0},{3,1},{4,6},{5,7},{6,4},{7,5},{8,10},{9,11},{10,... | collective-permute-start | bytes 1228808 | tf_op jit(solution)/shard_map/ppermute | solution.py:51
  158.0 18.4 %collective-permute-start.27 = (bf16[320,640]{1,0:T(8,128)(2,1)}, bf16[320,640]{1,0:T(8,128)(2,1)}, u32[]{:S(2)}, u32[]{:S(2)}) collective-permute-start(bf16[320,640]{1,0:T(8,128)(2,1)} %copy-done.11), channel_id=1, source_target_pairs={{0,12},{1,13},{2,14},{3,15},{4,0},{5,1},{6,2},{7,3},{8,4},{9,5},{1... | collective-permute-start | bytes 1228808 | tf_op jit(solution)/shard_map/ppermute | solution.py:51
  160.7 15.9 %collective-permute-start.26 = (bf16[320,640]{1,0:T(8,128)(2,1)}, bf16[320,640]{1,0:T(8,128)(2,1)}, u32[]{:S(2)}, u32[]{:S(2)}) collective-permute-start(bf16[320,640]{1,0:T(8,128)(2,1)} %copy-done.11), channel_id=1, source_target_pairs={{0,4},{1,5},{2,6},{3,7},{4,8},{5,9},{6,10},{7,11},{8,12},{9,13},{1... | collective-permute-start | bytes 1228808 | tf_op jit(solution)/shard_map/ppermute | solution.py:51
  160.7 15.9 %collective-permute-start.29 = (bf16[320,640]{1,0:T(8,128)(2,1)}, bf16[320,640]{1,0:T(8,128)(2,1)}, u32[]{:S(2)}, u32[]{:S(2)}) collective-permute-start(bf16[320,640]{1,0:T(8,128)(2,1)} %copy-done.24), channel_id=1, source_target_pairs={{0,12},{1,13},{2,14},{3,15},{4,0},{5,1},{6,2},{7,3},{8,4},{9,5},{1... | collective-permute-start | bytes 1228808 | tf_op jit(solution)/shard_map/ppermute | solution.py:51
  171.6 51.8 %all-to-all-start.3 = ((bf16[4,768,640]{2,1,0:T(8,128)(2,1)}), bf16[4,768,640]{2,1,0:T(8,128)(2,1)}, u32[]{:S(2)}, u32[]{:S(2)}) async-start(bf16[4,768,640]{2,1,0:T(8,128)(2,1)} %gradient.3), calls=%async_computation.3 | async-start | bytes 7864320 | tf_op jit(solution)/shard_map/all_to_all | solution.py:446
  181.7 24.7 %collective-permute-start.37 = (bf16[768,640]{1,0:T(8,128)(2,1)}, bf16[768,640]{1,0:T(8,128)(2,1)}, u32[]{:S(2)}, u32[]{:S(2)}) collective-permute-start(bf16[768,640]{1,0:T(8,128)(2,1)} %fusion), channel_id=1, source_target_pairs={{0,64},{1,65},{2,66},{3,67},{4,68},{5,69},{6,70},{7,71},{8,72},{9,... | collective-permute-start | bytes 2949128 | tf_op jit(solution)/shard_map/ppermute | solution.py:51
  195.9 15.8 %collective-permute-start.36 = (bf16[320,640]{1,0:T(8,128)(2,1)}, bf16[320,640]{1,0:T(8,128)(2,1)S(1)}, u32[]{:S(2)}, u32[]{:S(2)}) collective-permute-start(bf16[320,640]{1,0:T(8,128)(2,1)} %square.1.refs_0_), channel_id=1, source_target_pairs={{0,4},{1,5},{2,6},{3,7},{4,8},{5,9},{6,10},{7,11},{8,12},{9,13},{1... | collective-permute-start | bytes 1228808 | tf_op jit(solution)/shard_map/ppermute | solution.py:51
  199.2 20.1 %collective-permute-start.35 = (bf16[320,640]{1,0:T(8,128)(2,1)}, bf16[320,640]{1,0:T(8,128)(2,1)S(1)}, u32[]{:S(2)}, u32[]{:S(2)}) collective-permute-start(bf16[320,640]{1,0:T(8,128)(2,1)} %square.1.refs_0_), channel_id=1, source_target_pairs={{0,12},{1,13},{2,14},{3,15},{4,0},{5,1},{6,2},{7,3},{8,4},{9,5},{1... | collective-permute-start | bytes 1228808 | tf_op jit(solution)/shard_map/ppermute | solution.py:51
  201.9 17.4 %collective-permute-start.34 = (bf16[320,640]{1,0:T(8,128)(2,1)}, bf16[320,640]{1,0:T(8,128)(2,1)S(1)}, u32[]{:S(2)}, u32[]{:S(2)}) collective-permute-start(bf16[320,640]{1,0:T(8,128)(2,1)} %square.1.refs_0_), channel_id=1, source_target_pairs={{0,2},{1,3},{2,0},{3,1},{4,6},{5,7},{6,4},{7,5},{8,10},{9,11},{10,... | collective-permute-start | bytes 1228808 | tf_op jit(solution)/shard_map/ppermute | solution.py:51
  202.3 19.0 %collective-permute-start.33 = (bf16[320,640]{1,0:T(8,128)(2,1)}, bf16[320,640]{1,0:T(8,128)(2,1)S(1)}, u32[]{:S(2)}, u32[]{:S(2)}) collective-permute-start(bf16[320,640]{1,0:T(8,128)(2,1)} %square.1.refs_0_), channel_id=1, source_target_pairs={{0,8},{1,9},{2,10},{3,11},{4,12},{5,13},{6,14},{7,15},{8,0},{9,1},... | collective-permute-start | bytes 1228808 | tf_op jit(solution)/shard_map/ppermute | solution.py:51
  (49 other events, 447.9 us)

commit v6 on v5

--- a/solution.py
+++ b/solution.py
@@ -420,7 +420,7 @@
     other, other1, other2, other3, near2 = together((other, other1, other2, other3, near2))
     other1, other2, other3 = move(other1, Z_UP), move(other2, Z_FAR), move(other3, Z_DOWN)
     near = near + near1.astype(f32) + near3.astype(f32) + near2.astype(f32)
-    other1, other2, other3, near = together((other1, other2, other3, near))
+    other2, other3, other1, near = together((other2, other3, other1, near))
     other = other + other1.astype(f32) + other3.astype(f32) + other2.astype(f32)
     same = yh == yl
     kept = jnp.where(same, near, other)

time: 253 us -> 252 us (level)
  starting transfers between devices: 80 us -> 76.5 us
  waiting for transfers between devices: 83.6 us -> 86.4 us
    ppermute x42, starting transfers between devices: 62.8 us -> 59.3 us  [move(): return lax.ppermute(array, ('y_hi', 'x', 'grid'), perm)]
    all_to_all x2, waiting for transfers between devices: 5.35 us -> 8.8 us  [along_x(): lax.all_to_all(jnp.broadcast_to(piece, (4, HALF, ROWS)), 'x', 0, 0, tiled...]
where the time goes in v6:
time: 252 us; the launch traced here: 251 us
  waiting for transfers between devices  86.4 us (34%)
  starting transfers between devices  76.5 us (30%)
  Pallas kernels  71.7 us (28%)
  local copies, waits for them, and re-layouts  9.96 us (4%)
  other arithmetic  5.5 us (2%)
    ppermute x42, waiting for transfers between devices, move(): return lax.ppermute(array, ('y_hi', 'x', 'grid'), perm)  77.6 us
    ppermute x42, starting transfers between devices, move(): return lax.ppermute(array, ('y_hi', 'x', 'grid'), perm)  59.3 us
    pallas_call x2, Pallas kernels, gradient_partial(): pl.pallas_call(gradient_kernel, grid_spec=pltpu.PrefetchScalarGridSpec(nu...  17.4 us
    pallas_call x1, Pallas kernels, attention(): pl.pallas_call(body, grid_spec=pltpu.PrefetchScalarGridSpec(num_scalar_pr...  14.3 us
    pallas_call x2, Pallas kernels, gram_partial(): pl.pallas_call(gram_kernel, in_specs=[pl.BlockSpec(memory_space=pl.ANY)]...  13.6 us
    pallas_call x1, Pallas kernels, update_of(): pl.pallas_call(update_kernel, in_specs=[pl.BlockSpec(memory_space=pl.ANY)...  11.8 us
    all_to_all x2, waiting for transfers between devices, along_x(): lax.all_to_all(jnp.broadcast_to(piece, (4, HALF, ROWS)), 'x', 0, 0, tiled...  8.8 us
    pallas_call x1, Pallas kernels, square(): pl.pallas_call(square_kernel, in_specs=[pl.BlockSpec(memory_space=pl.ANY)...  8.57 us
  transfers between devices with their start and end apart: 46, of which 27 were waited for; matrix products, arithmetic and copies ran while one was open for 3% of the time, Pallas kernels for 24%

profile of v6, /device:TPU:1, one launch (start us, length us, event | category | flops | bytes accessed | tf_op | source)
XLA Modules:
  0.0 251.0 jit_solution(12657842009518525137)
XLA Ops:
  7.8 14.3 %attention.1.gq_ref = bf16[768,1024]{1,0:T(8,128)(2,1)} custom-call(s32[1]{0:T(128)} %bitcast.kv, bf16[1024,768]{1,0:T(8,128)(2,1)} %refs_0_.2, bf16[1024,1024]{1,0:T(8,128)(2,1)} %refs_1_.1, bf16[1024,1024]{1,0:T(8,128)(2,1)} %refs_2_.1, bf16[1024,768]{1,0:T(8,128)(2,1)} %refs_3_.1, bf16[1024,768]{1,0:T(8,128)(2,1)} %refs_4_.1), custom_call_target="tpu_custom_call" | custom-call | flops 24000000000 | bytes 8000000 | tf_op jit(solution)/shard_map/attention/pallas_call | solution.py:113
  22.1 4.9 %collective-permute-done.2.refs_3_.refs_11_ = bf16[640,768]{1,0:T(8,128)(2,1)S(1)} collective-permute-done((bf16[640,768]{1,0:T(8,128)(2,1)}, bf16[640,768]{1,0:T(8,128)(2,1)S(1)}, u32[]{:S(2)}, u32[]{:S(2)}) %collective-permute-start.2) | collective-permute-done | bytes 983072 | tf_op jit(solution)/shard_map/ppermute | solution.py:51
  35.2 8.7 %gradient.2 = bf16[4,768,640]{2,1,0:T(8,128)(2,1)} custom-call(s32[1]{0:T(128)} %bitcast.1.block_ref, bf16[768,1024]{1,0:T(8,128)(2,1)} %attention.1.gq_ref, bf16[1024,5120]{1,0:T(8,128)(2,1)} %in_ref.3), custom_call_target="tpu_custom_call" | custom-call | flops 8053063680 | bytes 12000000 | tf_op jit(solution)/shard_map/gradient/pallas_call | solution.py:133
  54.4 6.8 %gram.2 = (f32[320,640]{1,0:T(8,128)}, bf16[320,640]{1,0:T(8,128)(2,1)}, bf16[320,640]{1,0:T(8,128)(2,1)}, bf16[320,640]{1,0:T(8,128)(2,1)}) custom-call(bf16[640,768]{1,0:T(8,128)(2,1)} %refs_8_.5, bf16[640,768]{1,0:T(8,128)(2,1)} %copy-done.2, bf16[640,768]{1,0:T(8,128)(2,1)} %copy-done.3, bf16[640,768]{1,0:T(8,128)(2,1)} %copy-done.1, ...), custom_call_target="tpu_custom_call" | custom-call | flops 1 | bytes 1 | tf_op jit(solution)/shard_map/gram/pallas_call | solution.py:212
  61.2 5.0 %all-to-all-start = ((bf16[4,768,640]{2,1,0:T(8,128)(2,1)}), bf16[4,768,640]{2,1,0:T(8,128)(2,1)}, u32[]{:S(2)}, u32[]{:S(2)}) async-start(bf16[4,768,640]{2,1,0:T(8,128)(2,1)} %gradient.2), calls=%async_computation | async-start | bytes 7864320 | tf_op jit(solution)/shard_map/all_to_all | solution.py:401
  74.7 4.3 %collective-permute-done.13 = bf16[320,640]{1,0:T(8,128)(2,1)S(1)} collective-permute-done((bf16[320,640]{1,0:T(8,128)(2,1)S(1)}, bf16[320,640]{1,0:T(8,128)(2,1)S(1)}, u32[]{:S(2)}, u32[]{:S(2)}) %collective-permute-start.13) | collective-permute-done | bytes 409632 | tf_op jit(solution)/shard_map/ppermute | solution.py:51
  86.7 6.8 %gram.3 = (f32[320,640]{1,0:T(8,128)}, bf16[320,640]{1,0:T(8,128)(2,1)}, bf16[320,640]{1,0:T(8,128)(2,1)}, bf16[320,640]{1,0:T(8,128)(2,1)}) custom-call(bf16[640,768]{1,0:T(8,128)(2,1)} %collective-permute-done.refs_0_.refs_12_, bf16[640,768]{1,0:T(8,128)(2,1)} %collective-permute-done.6.refs_1_.refs_13_, ...), custom_call_target="tpu_custom_call" | custom-call | flops 1 | bytes 1 | tf_op jit(solution)/shard_map/gram/pallas_call | solution.py:212
  99.4 6.5 %collective-permute-done.19 = bf16[320,640]{1,0:T(8,128)(2,1)S(1)} collective-permute-done((bf16[320,640]{1,0:T(8,128)(2,1)}, bf16[320,640]{1,0:T(8,128)(2,1)S(1)}, u32[]{:S(2)}, u32[]{:S(2)}) %collective-permute-start.19) | collective-permute-done | bytes 409632 | tf_op jit(solution)/shard_map/ppermute | solution.py:51
  105.9 9.3 %collective-permute-done.20 = bf16[320,640]{1,0:T(8,128)(2,1)S(1)} collective-permute-done((bf16[320,640]{1,0:T(8,128)(2,1)}, bf16[320,640]{1,0:T(8,128)(2,1)S(1)}, u32[]{:S(2)}, u32[]{:S(2)}) %collective-permute-start.20) | collective-permute-done | bytes 409632 | tf_op jit(solution)/shard_map/ppermute | solution.py:51
  116.7 9.9 %collective-permute-done.22 = bf16[320,640]{1,0:T(8,128)(2,1)S(1)} collective-permute-done((bf16[320,640]{1,0:T(8,128)(2,1)S(1)}, bf16[320,640]{1,0:T(8,128)(2,1)S(1)}, u32[]{:S(2)}, u32[]{:S(2)}) %collective-permute-start.22) | collective-permute-done | bytes 409632 | tf_op jit(solution)/shard_map/ppermute | solution.py:51
  128.1 3.9 %all-to-all-start.1 = ((bf16[4,320,640]{2,1,0:T(8,128)(2,1)}), bf16[4,320,640]{2,1,0:T(8,128)(2,1)S(1)}, u32[]{:S(2)}, u32[]{:S(2)}) async-start(bf16[4,320,640]{2,1,0:T(8,128)(2,1)} %broadcast_in_dim.6), calls=%async_computation.1 | async-start | bytes 3276800 | tf_op jit(solution)/shard_map/all_to_all | solution.py:432
  136.6 8.7 %gradient.3 = bf16[4,768,640]{2,1,0:T(8,128)(2,1)} custom-call(s32[1]{0:T(128)} %bitcast.2.block_ref, bf16[768,1024]{1,0:T(8,128)(2,1)} %attention.1.gq_ref, bf16[1024,5120]{1,0:T(8,128)(2,1)} %in_ref.3), custom_call_target="tpu_custom_call" | custom-call | flops 8053063680 | bytes 12000000 | tf_op jit(solution)/shard_map/gradient/pallas_call | solution.py:133
  145.3 3.5 %fusion = bf16[768,640]{1,0:T(8,128)(2,1)} fusion(bf16[4,768,640]{2,1,0:T(8,128)(2,1)} %all-to-all-done), kind=kLoop, calls=%fused_computation.1 | loop fusion | flops 3932160 | bytes 4915200 | tf_op jit(solution)/shard_map/add | solution.py:438
  152.9 3.6 %all-to-all-start.2 = ((bf16[4,320,640]{2,1,0:T(8,128)(2,1)}), bf16[4,320,640]{2,1,0:T(8,128)(2,1)S(1)}, u32[]{:S(2)}, u32[]{:S(2)}) async-start(bf16[4,320,640]{2,1,0:T(8,128)(2,1)} %broadcast_in_dim.7), calls=%async_computation.2 | async-start | bytes 3276800 | tf_op jit(solution)/shard_map/all_to_all | solution.py:432
  163.4 4.5 %collective-permute-done.28.refs_7_ = bf16[320,640]{1,0:T(8,128)(2,1)} collective-permute-done((bf16[320,640]{1,0:T(8,128)(2,1)}, bf16[320,640]{1,0:T(8,128)(2,1)}, u32[]{:S(2)}, u32[]{:S(2)}) %collective-permute-start.28) | collective-permute-done | bytes 409632 | tf_op jit(solution)/shard_map/ppermute | solution.py:51
  167.9 7.1 %all-to-all-done.2.refs_9_ = bf16[4,320,640]{2,1,0:T(8,128)(2,1)S(1)} async-done(((bf16[4,320,640]{2,1,0:T(8,128)(2,1)}), bf16[4,320,640]{2,1,0:T(8,128)(2,1)S(1)}, u32[]{:S(2)}, u32[]{:S(2)}) %all-to-all-start.2) | async-done | bytes 1638432 | tf_op jit(solution)/shard_map/all_to_all | solution.py:432
  175.0 4.8 %all-to-all-start.3 = ((bf16[4,768,640]{2,1,0:T(8,128)(2,1)}), bf16[4,768,640]{2,1,0:T(8,128)(2,1)}, u32[]{:S(2)}, u32[]{:S(2)}) async-start(bf16[4,768,640]{2,1,0:T(8,128)(2,1)} %gradient.3), calls=%async_computation.3 | async-start | bytes 7864320 | tf_op jit(solution)/shard_map/all_to_all | solution.py:446
  179.9 3.9 %collective-permute-start.31 = (bf16[4,320,640]{2,1,0:T(8,128)(2,1)S(1)}, bf16[4,320,640]{2,1,0:T(8,128)(2,1)S(1)}, u32[]{:S(2)}, u32[]{:S(2)}) collective-permute-start(bf16[4,320,640]{2,1,0:T(8,128)(2,1)S(1)} %all-to-all-done.1.refs_8_), channel_id=1, source_target_pairs={{0,1},{1,0},{2,3},{3,2},{4,5},{5,4},{6,7},{7,6},{8,9},{9,8},{10,11... | collective-permute-start | bytes 4915208 | tf_op jit(solution)/shard_map/ppermute | solution.py:51
  189.5 8.6 %square.1.refs_0_ = bf16[320,640]{1,0:T(8,128)(2,1)} custom-call(bf16[320,640]{1,0:T(8,128)(2,1)} %copy-done.11, bf16[320,640]{1,0:T(8,128)(2,1)} %collective-permute-done.27.refs_1_, bf16[320,640]{1,0:T(8,128)(2,1)} %copy-done.23, bf16[320,640]{1,0:T(8,128)(2,1)} %collective-permute-done.26.refs_3_, bf16[320,640]{1,0:T(8,128)(2,1)} %copy-done.24, ...), custom_call_target="tpu_custom_call" | custom-call | flops 4194304000 | bytes 11000000 | tf_op jit(solution)/shard_map/square/pallas_call | solution.py:285
  203.7 4.9 %collective-permute-done.37.h_ref = bf16[768,640]{1,0:T(8,128)(2,1)} collective-permute-done((bf16[768,640]{1,0:T(8,128)(2,1)}, bf16[768,640]{1,0:T(8,128)(2,1)}, u32[]{:S(2)}, u32[]{:S(2)}) %collective-permute-start.37) | collective-permute-done | bytes 983072 | tf_op jit(solution)/shard_map/ppermute | solution.py:51
  211.7 4.2 %collective-permute-done.34.refs_4_ = bf16[320,640]{1,0:T(8,128)(2,1)S(1)} collective-permute-done((bf16[320,640]{1,0:T(8,128)(2,1)}, bf16[320,640]{1,0:T(8,128)(2,1)S(1)}, u32[]{:S(2)}, u32[]{:S(2)}) %collective-permute-start.34) | collective-permute-done | bytes 409632 | tf_op jit(solution)/shard_map/ppermute | solution.py:51
  215.9 5.4 %collective-permute-done.33.refs_2_ = bf16[320,640]{1,0:T(8,128)(2,1)S(1)} collective-permute-done((bf16[320,640]{1,0:T(8,128)(2,1)}, bf16[320,640]{1,0:T(8,128)(2,1)S(1)}, u32[]{:S(2)}, u32[]{:S(2)}) %collective-permute-start.33) | collective-permute-done | bytes 409632 | tf_op jit(solution)/shard_map/ppermute | solution.py:51
  223.2 6.0 %momentum.1 = f32[640,768]{1,0:T(8,128)} custom-call(f32[640,768]{1,0:T(8,128)} %m_ref.1, bf16[4,768,640]{2,1,0:T(8,128)(2,1)} %all-to-all-done.3.g_ref, bf16[768,640]{1,0:T(8,128)(2,1)} %collective-permute-done.37.h_ref), custom_call_target="tpu_custom_call" | custom-call | flops 4423680 | bytes 9000000 | tf_op jit(solution)/shard_map/momentum/pallas_call | solution.py:160
  233.3 11.8 %update.1 = (bf16[640,768]{1,0:T(8,128)(2,1)}, bf16[320,768]{1,0:T(8,128)(2,1)}) custom-call(bf16[320,640]{1,0:T(8,128)(2,1)} %square.1.refs_0_, bf16[320,640]{1,0:T(8,128)(2,1)} %copy-done.14, bf16[320,640]{1,0:T(8,128)(2,1)} %copy-done.16, bf16[320,640]{1,0:T(8,128)(2,1)} %copy-done.13, bf16[320,640]{1,0:T(8,128)(2,1)} %copy-done.15, ...), custom_call_target="tpu_custom_call" | custom-call | flops 1 | bytes 1 | tf_op jit(solution)/shard_map/update/pallas_call | solution.py:348
  (141 shorter events, 92.8 us)
Async XLA Ops:
  0.6 45.6 %collective-permute-start.7 = (bf16[640,768]{1,0:T(8,128)(2,1)}, bf16[640,768]{1,0:T(8,128)(2,1)S(1)}, u32[]{:S(2)}, u32[]{:S(2)}) collective-permute-start(bf16[640,768]{1,0:T(8,128)(2,1)} %refs_8_.5), channel_id=1, source_target_pairs={{0,1},{1,0},{2,3},{3,2},{4,5},{5,4},{6,7},{7,6},{8,9},{9,8},{10,11... | collective-permute-start | bytes 2949128 | tf_op jit(solution)/shard_map/ppermute | solution.py:51
  2.1 24.8 %collective-permute-start.2 = (bf16[640,768]{1,0:T(8,128)(2,1)}, bf16[640,768]{1,0:T(8,128)(2,1)S(1)}, u32[]{:S(2)}, u32[]{:S(2)}) collective-permute-start(bf16[640,768]{1,0:T(8,128)(2,1)} %refs_8_.5), channel_id=1, source_target_pairs={{0,16},{1,17},{2,18},{3,19},{4,20},{5,21},{6,22},{7,23},{8,24},{9,... | collective-permute-start | bytes 2949128 | tf_op jit(solution)/shard_map/ppermute | solution.py:51
  3.4 23.5 %collective-permute-start.1 = (bf16[640,768]{1,0:T(8,128)(2,1)}, bf16[640,768]{1,0:T(8,128)(2,1)S(1)}, u32[]{:S(2)}, u32[]{:S(2)}) collective-permute-start(bf16[640,768]{1,0:T(8,128)(2,1)} %refs_8_.5), channel_id=1, source_target_pairs={{0,48},{1,49},{2,50},{3,51},{4,52},{5,53},{6,54},{7,55},{8,56},{9,... | collective-permute-start | bytes 2949128 | tf_op jit(solution)/shard_map/ppermute | solution.py:51
  4.8 24.6 %collective-permute-start = (bf16[640,768]{1,0:T(8,128)(2,1)}, bf16[640,768]{1,0:T(8,128)(2,1)}, u32[]{:S(2)}, u32[]{:S(2)}) collective-permute-start(bf16[640,768]{1,0:T(8,128)(2,1)} %refs_8_.5), channel_id=1, source_target_pairs={{0,64},{1,65},{2,66},{3,67},{4,68},{5,69},{6,70},{7,71},{8,72},{9,... | collective-permute-start | bytes 2949128 | tf_op jit(solution)/shard_map/ppermute | solution.py:51
  29.5 16.8 %collective-permute-start.8 = (bf16[640,768]{1,0:T(8,128)(2,1)S(1)}, bf16[640,768]{1,0:T(8,128)(2,1)}, u32[]{:S(2)}, u32[]{:S(2)}) collective-permute-start(bf16[640,768]{1,0:T(8,128)(2,1)S(1)} %collective-permute-done.1.refs_1_.refs_9_), channel_id=1, source_target_pairs={{0,1},{1,0},{2,3},{3,2},{4,5},{5,4},{6,7},{7,6},{8,9},{9,8},{10,11... | collective-permute-start | bytes 2949128 | tf_op jit(solution)/shard_map/ppermute | solution.py:51
  30.9 15.3 %collective-permute-start.9 = (bf16[640,768]{1,0:T(8,128)(2,1)S(1)}, bf16[640,768]{1,0:T(8,128)(2,1)}, u32[]{:S(2)}, u32[]{:S(2)}) collective-permute-start(bf16[640,768]{1,0:T(8,128)(2,1)S(1)} %collective-permute-done.2.refs_3_.refs_11_), channel_id=1, source_target_pairs={{0,1},{1,0},{2,3},{3,2},{4,5},{5,4},{6,7},{7,6},{8,9},{9,8},{10,11... | collective-permute-start | bytes 2949128 | tf_op jit(solution)/shard_map/ppermute | solution.py:51
  47.8 20.2 %collective-permute-start.11 = (bf16[640,768]{1,0:T(8,128)(2,1)}, bf16[640,768]{1,0:T(8,128)(2,1)}, u32[]{:S(2)}, u32[]{:S(2)}) collective-permute-start(bf16[640,768]{1,0:T(8,128)(2,1)} %collective-permute-done.refs_0_.refs_12_), channel_id=1, source_target_pairs={{0,1},{1,0},{2,3},{3,2},{4,5},{5,4},{6,7},{7,6},{8,9},{9,8},{10,11... | collective-permute-start | bytes 2949128 | tf_op jit(solution)/shard_map/ppermute | solution.py:51
  47.9 23.7 %collective-permute-start.6 = (bf16[640,768]{1,0:T(8,128)(2,1)}, bf16[640,768]{1,0:T(8,128)(2,1)}, u32[]{:S(2)}, u32[]{:S(2)}) collective-permute-start(bf16[640,768]{1,0:T(8,128)(2,1)} %collective-permute-done.refs_0_.refs_12_), channel_id=1, source_target_pairs={{0,48},{1,49},{2,50},{3,51},{4,52},{5,53},{6,54},{7,55},{8,56},{9,... | collective-permute-start | bytes 2949128 | tf_op jit(solution)/shard_map/ppermute | solution.py:51
  50.5 24.1 %collective-permute-start.5 = (bf16[640,768]{1,0:T(8,128)(2,1)}, bf16[640,768]{1,0:T(8,128)(2,1)}, u32[]{:S(2)}, u32[]{:S(2)}) collective-permute-start(bf16[640,768]{1,0:T(8,128)(2,1)} %collective-permute-done.refs_0_.refs_12_), channel_id=1, source_target_pairs={{0,16},{1,17},{2,18},{3,19},{4,20},{5,21},{6,22},{7,23},{8,24},{9,... | collective-permute-start | bytes 2949128 | tf_op jit(solution)/shard_map/ppermute | solution.py:51
  50.5 24.2 %collective-permute-start.10 = (bf16[640,768]{1,0:T(8,128)(2,1)S(1)}, bf16[640,768]{1,0:T(8,128)(2,1)}, u32[]{:S(2)}, u32[]{:S(2)}) collective-permute-start(bf16[640,768]{1,0:T(8,128)(2,1)S(1)} %constant_dynamic-update-slice_fusion.refs_2_.refs_10_), channel_id=1, source_target_pairs={{0,64},{1,65},{2,66},{3,67},{4,68},{5,69},{6,70},{7,71},{8,72},{9,... | collective-permute-start | bytes 2949128 | tf_op jit(solution)/shard_map/ppermute | solution.py:51
  61.2 65.6 %all-to-all-start = ((bf16[4,768,640]{2,1,0:T(8,128)(2,1)}), bf16[4,768,640]{2,1,0:T(8,128)(2,1)}, u32[]{:S(2)}, u32[]{:S(2)}) async-start(bf16[4,768,640]{2,1,0:T(8,128)(2,1)} %gradient.2), calls=%async_computation | async-start | bytes 7864320 | tf_op jit(solution)/shard_map/all_to_all | solution.py:401
  96.5 18.7 %collective-permute-start.20 = (bf16[320,640]{1,0:T(8,128)(2,1)}, bf16[320,640]{1,0:T(8,128)(2,1)S(1)}, u32[]{:S(2)}, u32[]{:S(2)}) collective-permute-start(bf16[320,640]{1,0:T(8,128)(2,1)} %get-tuple-element.108), channel_id=1, source_target_pairs={{0,12},{1,13},{2,14},{3,15},{4,0},{5,1},{6,2},{7,3},{8,4},{9,5},{1... | collective-permute-start | bytes 1228808 | tf_op jit(solution)/shard_map/ppermute | solution.py:51
  97.2 18.7 %collective-permute-start.21 = (bf16[320,640]{1,0:T(8,128)(2,1)}, bf16[320,640]{1,0:T(8,128)(2,1)S(1)}, u32[]{:S(2)}, u32[]{:S(2)}) collective-permute-start(bf16[320,640]{1,0:T(8,128)(2,1)} %get-tuple-element.109), channel_id=1, source_target_pairs={{0,4},{1,5},{2,6},{3,7},{4,8},{5,9},{6,10},{7,11},{8,12},{9,13},{1... | collective-permute-start | bytes 1228808 | tf_op jit(solution)/shard_map/ppermute | solution.py:51
  128.1 23.3 %all-to-all-start.1 = ((bf16[4,320,640]{2,1,0:T(8,128)(2,1)}), bf16[4,320,640]{2,1,0:T(8,128)(2,1)S(1)}, u32[]{:S(2)}, u32[]{:S(2)}) async-start(bf16[4,320,640]{2,1,0:T(8,128)(2,1)} %broadcast_in_dim.6), calls=%async_computation.1 | async-start | bytes 3276800 | tf_op jit(solution)/shard_map/all_to_all | solution.py:432
  132.0 16.8 %collective-permute-start.25 = (bf16[320,640]{1,0:T(8,128)(2,1)S(1)}, bf16[320,640]{1,0:T(8,128)(2,1)S(1)}, u32[]{:S(2)}, u32[]{:S(2)}) collective-permute-start(bf16[320,640]{1,0:T(8,128)(2,1)S(1)} %add_convert_fusion.1.refs_0_), channel_id=1, source_target_pairs={{0,64},{1,65},{2,66},{3,67},{4,68},{5,69},{6,70},{7,71},{8,72},{9,... | collective-permute-start | bytes 1228808 | tf_op jit(solution)/shard_map/ppermute | solution.py:51
  132.9 15.9 %collective-permute-start.24 = (bf16[320,640]{1,0:T(8,128)(2,1)S(1)}, bf16[320,640]{1,0:T(8,128)(2,1)S(1)}, u32[]{:S(2)}, u32[]{:S(2)}) collective-permute-start(bf16[320,640]{1,0:T(8,128)(2,1)S(1)} %add_convert_fusion.1.refs_0_), channel_id=1, source_target_pairs={{0,8},{1,9},{2,10},{3,11},{4,12},{5,13},{6,14},{7,15},{8,0},{9,1},... | collective-permute-start | bytes 1228808 | tf_op jit(solution)/shard_map/ppermute | solution.py:51
  152.9 22.0 %all-to-all-start.2 = ((bf16[4,320,640]{2,1,0:T(8,128)(2,1)}), bf16[4,320,640]{2,1,0:T(8,128)(2,1)S(1)}, u32[]{:S(2)}, u32[]{:S(2)}) async-start(bf16[4,320,640]{2,1,0:T(8,128)(2,1)} %broadcast_in_dim.7), calls=%async_computation.2 | async-start | bytes 3276800 | tf_op jit(solution)/shard_map/all_to_all | solution.py:432
  158.2 21.6 %collective-permute-start.30 = (bf16[320,640]{1,0:T(8,128)(2,1)}, bf16[320,640]{1,0:T(8,128)(2,1)}, u32[]{:S(2)}, u32[]{:S(2)}) collective-permute-start(bf16[320,640]{1,0:T(8,128)(2,1)} %copy-done.23), channel_id=1, source_target_pairs={{0,2},{1,3},{2,0},{3,1},{4,6},{5,7},{6,4},{7,5},{8,10},{9,11},{10,... | collective-permute-start | bytes 1228808 | tf_op jit(solution)/shard_map/ppermute | solution.py:51
  158.6 21.3 %collective-permute-start.27 = (bf16[320,640]{1,0:T(8,128)(2,1)}, bf16[320,640]{1,0:T(8,128)(2,1)}, u32[]{:S(2)}, u32[]{:S(2)}) collective-permute-start(bf16[320,640]{1,0:T(8,128)(2,1)} %copy-done.11), channel_id=1, source_target_pairs={{0,12},{1,13},{2,14},{3,15},{4,0},{5,1},{6,2},{7,3},{8,4},{9,5},{1... | collective-permute-start | bytes 1228808 | tf_op jit(solution)/shard_map/ppermute | solution.py:51
  160.7 19.1 %collective-permute-start.26 = (bf16[320,640]{1,0:T(8,128)(2,1)}, bf16[320,640]{1,0:T(8,128)(2,1)}, u32[]{:S(2)}, u32[]{:S(2)}) collective-permute-start(bf16[320,640]{1,0:T(8,128)(2,1)} %copy-done.11), channel_id=1, source_target_pairs={{0,4},{1,5},{2,6},{3,7},{4,8},{5,9},{6,10},{7,11},{8,12},{9,13},{1... | collective-permute-start | bytes 1228808 | tf_op jit(solution)/shard_map/ppermute | solution.py:51
  160.7 19.1 %collective-permute-start.29 = (bf16[320,640]{1,0:T(8,128)(2,1)}, bf16[320,640]{1,0:T(8,128)(2,1)}, u32[]{:S(2)}, u32[]{:S(2)}) collective-permute-start(bf16[320,640]{1,0:T(8,128)(2,1)} %copy-done.24), channel_id=1, source_target_pairs={{0,12},{1,13},{2,14},{3,15},{4,0},{5,1},{6,2},{7,3},{8,4},{9,5},{1... | collective-permute-start | bytes 1228808 | tf_op jit(solution)/shard_map/ppermute | solution.py:51
  175.0 48.2 %all-to-all-start.3 = ((bf16[4,768,640]{2,1,0:T(8,128)(2,1)}), bf16[4,768,640]{2,1,0:T(8,128)(2,1)}, u32[]{:S(2)}, u32[]{:S(2)}) async-start(bf16[4,768,640]{2,1,0:T(8,128)(2,1)} %gradient.3), calls=%async_computation.3 | async-start | bytes 7864320 | tf_op jit(solution)/shard_map/all_to_all | solution.py:446
  183.9 24.7 %collective-permute-start.37 = (bf16[768,640]{1,0:T(8,128)(2,1)}, bf16[768,640]{1,0:T(8,128)(2,1)}, u32[]{:S(2)}, u32[]{:S(2)}) collective-permute-start(bf16[768,640]{1,0:T(8,128)(2,1)} %fusion), channel_id=1, source_target_pairs={{0,64},{1,65},{2,66},{3,67},{4,68},{5,69},{6,70},{7,71},{8,72},{9,... | collective-permute-start | bytes 2949128 | tf_op jit(solution)/shard_map/ppermute | solution.py:51
  202.3 19.0 %collective-permute-start.33 = (bf16[320,640]{1,0:T(8,128)(2,1)}, bf16[320,640]{1,0:T(8,128)(2,1)S(1)}, u32[]{:S(2)}, u32[]{:S(2)}) collective-permute-start(bf16[320,640]{1,0:T(8,128)(2,1)} %square.1.refs_0_), channel_id=1, source_target_pairs={{0,8},{1,9},{2,10},{3,11},{4,12},{5,13},{6,14},{7,15},{8,0},{9,1},... | collective-permute-start | bytes 1228808 | tf_op jit(solution)/shard_map/ppermute | solution.py:51
  (49 other events, 448.5 us)
